TPU v7x, 32 devices: a whole 2x2x4 slice. The times are simulated.
32 devices in a mesh: groups: 2 (over y), req: 4 (over x, core), tp: 4 (over z).
Axes of the slice: x: 2, y: 2, z: 4, core: 2. Of those that a mesh axis runs over, the one named last changes fastest.
Arguments:
- tokens: bfloat16 [4096, 8192], P(('groups', 'req'), 'tp'), parts along dimension 0, may hold values from -6 to 6
- norm_gain: bfloat16 [8192], replicated, may hold values from 0.25 to 1.75
- w_query: bfloat16 [8192, 4096], P(None, 'tp'), may hold values from -0.0625 to 0.0625
- key_weight: bfloat16 [8192, 1024], P(None, 'tp'), may hold values from -0.0625 to 0.0625
- value_weight: bfloat16 [8192, 1024], P(None, 'tp'), may hold values from -0.0625 to 0.0625
- lengths: int32 [8], P('groups'), parts along dimension 0, may hold values from 1 to 512, 1024 in all
- plan: int32 [32], P('groups'), parts along dimension 0, may hold values from 0 to 15, as said below
Outputs:
- attended: bfloat16 [4096, 4096], P(('groups', 'req'), 'tp'), parts along dimension 0
- cache: bfloat16 [2, 4096, 1024], P(None, ('groups', 'req'), 'tp'), parts along dimension 1
There are 2 independent parts, one for each index of `groups`. A program takes and returns all parts, laid end to end along the dimension named above; an argument that names none is the same for every part. Nothing has to cross between parts.
Inputs may be any that keep to these rules, and one draw needn't show every extreme that they name: lengths: the longest request is exactly 512. plan is a permutation of the spans 0 to 15; span g is request g // 4 at positions (g % 4) * 128 onward; slot k belongs to worker k // 4; the 4 spans of one request go to 4 different workers.
All inputs are finite; a program needn't handle non-finite values.
Results may differ from a plain program's by a relative error of at most 0.008.
Values may be sent and summed in bfloat16 or wider, within the bound.
No kernel may reach another device: no remote copies, remote signals or barrier semaphores. Data moves between devices by JAX's collectives and lax.ppermute only.
A program may use at most 128 MiB of HBM per device.

v0:
```python
import functools
import math

import jax
import jax.numpy as jnp
import numpy as np
from jax import lax
from jax.experimental import pallas as pl
from jax.experimental.pallas import tpu as pltpu
from jax.sharding import PartitionSpec as P

HEAD_SIZE = 128
SPAN = 128
ALIGN = 16
SHARES = (4, 6, 6)
GROUPS = ((0, 1), (2,))
DEPTH = 1024
MEBI = 1024 * 1024
F32, BF16 = jnp.float32, jnp.bfloat16


def run_of(lengths_ref, request, count):
    start = jnp.int32(0)
    length = jnp.int32(0)
    for other in range(count):
        amount = lengths_ref[other]
        start = start + jnp.where(other < request, amount, 0)
        length = jnp.where(other == request, amount, length)
    return start, length


def iota(shape, dimension):
    return lax.broadcasted_iota(jnp.int32, shape, dimension)


def deal_kernel(chips, bases, sizes, twins, lengths_ref, *refs):
    me = lax.axis_index("req")
    chip, core = lax.div(me, 2), lax.rem(me, 2)
    sources, refs = refs[: len(twins)], refs[len(twins) :]
    count = 2 * len(sizes)
    priors, out_refs = refs[:-count], refs[-count:]
    requests = [me + 1 - 2 * core if twin else me for twin in twins]
    runs = [run_of(lengths_ref, request, 2 * chips) for request in requests]
    slots = sources[0].shape[0]
    for chunk, (base, rows) in enumerate(zip(bases, sizes)):
        home_ref, away_ref = out_refs[2 * chunk : 2 * chunk + 2]
        for hop in range(chips):
            target = lax.rem(chip + hop, chips) * 2 + core
            number = base + target * rows + iota((rows, slots), 0)
            slot = iota((rows, slots), 1)
            total = None
            for (start, length), source in zip(runs, sources):
                hot = ((number - start == slot) & (slot < length)).astype(BF16)
                part = jnp.dot(hot, source[...], preferred_element_type=F32)
                total = part if total is None else total + part
            total = total.astype(BF16)
            if hop == 0:
                home_ref[...] = total + priors[2 * chunk][...] if priors else total
            elif priors:
                away_ref[hop - 1] = total + priors[2 * chunk + 1][hop - 1]
            else:
                away_ref[hop - 1] = total


def deal(chips, bases, sizes, lengths, sources, twins, priors=()):
    slots, width = sources[0].shape
    block = min(1024, width)
    out_specs, out_shape = [], []
    for rows in sizes:
        out_specs += [
            pl.BlockSpec((rows, block), lambda i: (0, i)),
            pl.BlockSpec((chips - 1, rows, block), lambda i: (0, 0, i)),
        ]
        out_shape += [
            jax.ShapeDtypeStruct((rows, width), BF16),
            jax.ShapeDtypeStruct((chips - 1, rows, width), BF16),
        ]
    return pl.pallas_call(
        functools.partial(deal_kernel, chips, bases, sizes, twins),
        grid=(width // block,),
        in_specs=[pl.BlockSpec(memory_space=pltpu.SMEM)]
        + [pl.BlockSpec((slots, block), lambda i: (0, i)) for _ in sources]
        + (out_specs if priors else []),
        out_specs=out_specs,
        out_shape=out_shape,
        compiler_params=pltpu.CompilerParams(vmem_limit_bytes=24 * MEBI),
        cost_estimate=pl.CostEstimate(
            flops=2 * len(sources) * chips * sum(sizes) * slots * width,
            bytes_accessed=2 * len(sources) * slots * width + 2 * chips * sum(sizes) * width,
            transcendentals=0,
        ),
        name="deal",
    )(lengths, *sources, *priors)


def merge_kernel(count, home_ref, *refs):
    total = home_ref[...]
    for ref in refs[:count]:
        total = total + ref[...]
    passed = (len(refs) - count - 1) // 2
    refs[count + passed][...] = total


def merge(home, arrived, later):
    count = len(arrived)
    vmem, anywhere = pl.BlockSpec(memory_space=pltpu.VMEM), pl.BlockSpec(memory_space=pl.ANY)
    block, *later = pl.pallas_call(
        functools.partial(merge_kernel, count),
        in_specs=[vmem] * (count + 1) + [anywhere] * len(later),
        out_specs=[vmem] + [anywhere] * len(later),
        out_shape=[jax.ShapeDtypeStruct(leaf.shape, leaf.dtype) for leaf in (home, *later)],
        input_output_aliases={count + 1 + at: 1 + at for at in range(len(later))},
        compiler_params=pltpu.CompilerParams(vmem_limit_bytes=8 * MEBI),
        cost_estimate=pl.CostEstimate(
            flops=home.size, bytes_accessed=2 * home.size * (count + 2), transcendentals=0
        ),
        name="merge",
    )(home, *arrived, *later)
    return block, later


def after(array, anchors):
    def kernel(*refs):
        pass

    anywhere = pl.BlockSpec(memory_space=pl.ANY)
    return pl.pallas_call(
        kernel,
        in_specs=[anywhere] * (1 + len(anchors)),
        out_specs=anywhere,
        out_shape=jax.ShapeDtypeStruct(array.shape, array.dtype),
        input_output_aliases={0: 0},
        compiler_params=pltpu.CompilerParams(vmem_limit_bytes=MEBI),
        name="after",
    )(array, *anchors)


def routes_of(shards):
    if shards == 4:
        routes = [
            (-1, [(1, 2), (2, 1)]),
            (-1, [(0, 1), (1, 0), (2, 3), (3, 2)]),
            (-1, [(0, 2), (1, 3), (2, 0), (3, 1)]),
            (2, [(2, 3), (1, 0)]),
        ]
    else:
        routes = []
        for step in range(1, shards):
            source = len(routes) - 2 if step > 1 else -1
            routes.append((source, [(at, at + 1) for at in range(step - 1, shards - 1)]))
            source = len(routes) - 2 if step > 1 else -1
            routes.append((source, [(at, at - 1) for at in range(1, shards - step + 1)]))
    held, depth = [list(range(shards))], [0]
    for source, pairs in routes:
        now = [-1] * shards
        for start, end in pairs:
            now[end] = held[source + 1][start]
        held.append(now)
        depth.append(depth[source + 1] + 1)
    return routes, held, depth


def visits_of(held, shards):
    visits = [
        [(piece, now[at]) for piece, now in enumerate(held) if now[at] >= 0]
        for at in range(shards)
    ]
    count = max(len(line) for line in visits)
    table = []
    for line in visits:
        pad = (-1, line[-1][1] if line else 0)
        line = line + [pad] * (count - len(line))
        table.append([piece for piece, _ in line] + [shard for _, shard in line])
    return np.array(table, np.int32), count


def project_kernel(
    count, carries, final, shards, steps, bases, sizes, members, place_ref, lengths_ref, *refs
):
    pieces, refs = refs[: count * len(sizes)], refs[count * len(sizes) :]
    gain_ref, query_ref, key_ref, value_ref = refs[:4]
    refs = refs[4:]
    if carries:
        sums_in, squares_in = refs[:2]
        refs = refs[2:]
    frequency_ref, refs = refs[0], refs[1:]
    if final:
        out_ref, refs = refs[0], refs[1:]
    sums, squares, chosen = refs
    visit, step = pl.program_id(0), pl.program_id(1)
    visits = pl.num_programs(0)
    rows, depth = chosen.shape
    piece = place_ref[visit]

    @pl.when((visit == 0) & (step == 0))
    def _():
        sums[...] = sums_in[...] if carries else jnp.zeros_like(sums)
        squares[...] = squares_in[...] if carries else jnp.zeros_like(squares)

    for index in range(count):

        @pl.when(piece == index)
        def _():
            columns = pl.ds(pl.multiple_of(step * depth, depth), depth)
            at = 0
            for chunk, size in enumerate(sizes):
                chosen[at : at + size, :] = pieces[chunk * count + index][:, columns]
                at += size

    @pl.when(piece >= 0)
    def _():
        wide = chosen[...].astype(F32)
        square = wide * wide
        part = square[:, :128]
        for at in range(128, depth, 128):
            part = part + square[:, at : at + 128]
        squares[...] += part
        scaled = (wide * gain_ref[...]).astype(BF16)
        at = 0
        for weight in (query_ref, key_ref, value_ref):
            columns = slice(at, at + weight.shape[1])
            sums[:, columns] += jnp.dot(scaled, weight[...], preferred_element_type=F32)
            at += weight.shape[1]

    if final:

        @pl.when((visit == visits - 1) & (step == steps - 1))
        def _():
            me = lax.axis_index("req")
            number = jnp.concatenate(
                [
                    base + me * size + iota((size, HEAD_SIZE), 0)
                    for base, size in zip(bases, sizes)
                ],
                axis=0,
            )
            start = jnp.zeros((rows, HEAD_SIZE), jnp.int32)
            before = jnp.int32(0)
            for other in range(members):
                before = before + lengths_ref[other]
                start = jnp.where(number >= before, before, start)
            angle = (number - start).astype(F32) * frequency_ref[...]
            cosine, sine = jnp.cos(angle), jnp.sin(angle)
            sine = jnp.where(iota((rows, HEAD_SIZE), 1) < HEAD_SIZE // 2, -sine, sine)
            mean = jnp.sum(squares[...], axis=1, keepdims=True) / (shards * steps * depth)
            scale = lax.rsqrt(mean + 1e-05)
            turned = query_ref.shape[1] + key_ref.shape[1]
            for at in range(0, sums.shape[1], HEAD_SIZE):
                columns = slice(at, at + HEAD_SIZE)
                head = sums[:, columns] * scale
                if at < turned:
                    head = head * cosine + pltpu.roll(head, HEAD_SIZE // 2, 1) * sine
                out_ref[:, columns] = head.astype(BF16)


def project(
    final, shards, bases, sizes, place, visits, lengths, lines, gain, weights, carried, frequency
):
    pieces = [piece for line in lines for piece in line]
    rows, width = sum(sizes), pieces[0].shape[1]
    depth = min(DEPTH, width)
    steps = width // depth
    columns = sum(weight.shape[1] for weight in weights)

    def block_of(visit, step, place_ref):
        step = jnp.where(place_ref[visit] < 0, steps - 1, step)
        return place_ref[visits + visit] * steps + step

    def whole(shape):
        return pl.BlockSpec(shape, lambda visit, step, place_ref, lengths_ref: (0, 0))

    def deep(block, dimension):
        def where(visit, step, place_ref, lengths_ref):
            at = block_of(visit, step, place_ref)
            return (at, 0) if dimension == 0 else (0, at)

        return pl.BlockSpec(block, where)

    operands = [*pieces, gain, *weights, *carried, frequency]
    in_specs = [whole(piece.shape) for piece in pieces]
    in_specs += [deep((1, depth), 1)]
    in_specs += [deep((depth, weight.shape[1]), 0) for weight in weights]
    in_specs += [whole(leaf.shape) for leaf in carried]
    in_specs += [whole((1, HEAD_SIZE))]
    scratch = [pltpu.VMEM((rows, depth), BF16)]
    if final:
        out_shape = [jax.ShapeDtypeStruct((rows, columns), BF16)]
        scratch = [pltpu.VMEM((rows, columns), F32), pltpu.VMEM((rows, 128), F32), *scratch]
    else:
        out_shape = [
            jax.ShapeDtypeStruct((rows, columns), F32),
            jax.ShapeDtypeStruct((rows, 128), F32),
        ]
    return pl.pallas_call(
        functools.partial(
            project_kernel,
            len(lines[0]),
            bool(carried),
            final,
            shards,
            steps,
            bases,
            sizes,
            lengths.shape[0],
        ),
        grid_spec=pltpu.PrefetchScalarGridSpec(
            num_scalar_prefetch=2,
            grid=(visits, steps),
            in_specs=in_specs,
            out_specs=[whole(leaf.shape) for leaf in out_shape],
            scratch_shapes=scratch,
        ),
        out_shape=out_shape,
        compiler_params=pltpu.CompilerParams(vmem_limit_bytes=32 * MEBI),
        cost_estimate=pl.CostEstimate(
            flops=2 * rows * width * columns * visits,
            bytes_accessed=2 * width * columns * visits + 8 * rows * columns,
            transcendentals=0,
        ),
        name="project",
    )(place, lengths, *operands)


def attend_kernel(
    chips, groups, known, prior, query_width, key_width, lengths_ref, plan_ref, *refs
):
    blocks, refs = refs[: -12 if prior else -10], refs[-10:]
    attended_out, cache_out, attended_ref, cache_ref, rows_ref, queries_ref = refs[:6]
    scores_ref, top_ref, sems, out_sems = refs[6:]
    workers = 2 * chips
    me = lax.axis_index("req")
    chip, core = lax.div(me, 2), lax.rem(me, 2)
    slots = cache_ref.shape[1]
    spans = slots // SPAN
    total = workers * sum(sum(sizes) for _, sizes in groups)
    copies = []
    for group, (bases, sizes) in enumerate(groups):
        for hop in range(chips):
            source = lax.rem(chip - hop + chips, chips) * 2
            for twin in range(2):
                owner = source + (core if twin == 0 else 1 - core)
                block = blocks[(group * chips + hop) * 2 + twin]
                first = 0
                for base, rows in zip(bases, sizes):
                    at = pl.multiple_of(base + owner * rows, ALIGN)
                    copies.append(
                        pltpu.make_async_copy(
                            block.at[pl.ds(first, rows), :],
                            rows_ref.at[pl.ds(at, rows), :],
                            sems.at[len(copies)],
                        )
                    )
                    first += rows
    for copy in copies:
        copy.start()
    rows_ref[total:, :] = jnp.zeros((rows_ref.shape[0] - total, rows_ref.shape[1]), BF16)
    for copy in copies:
        copy.wait()

    def window(row, columns):
        first = pl.multiple_of(lax.div(row, ALIGN) * ALIGN, ALIGN)
        shape = (SPAN, 2 * SPAN)
        hot = (iota(shape, 1) == iota(shape, 0) + (row - first)).astype(BF16)
        return jnp.dot(
            hot, rows_ref[pl.ds(first, 2 * SPAN), columns], preferred_element_type=F32
        )

    own_start, own_length = run_of(lengths_ref, me, workers)
    mine = (own_start + own_length <= known) & (own_start + own_length > prior)
    cache_copy = pltpu.make_async_copy(cache_ref, cache_out, out_sems.at[spans])

    @pl.when(mine)
    def _():
        def step(part, carry):
            at = pl.multiple_of(part * SPAN, SPAN)

            @pl.when(at < own_length)
            def _():
                picked = window(own_start + at, slice(query_width, query_width + 2 * key_width))
                live = at + iota(picked.shape, 0) < own_length
                picked = jnp.where(live, picked, 0.0).astype(BF16)
                cache_ref[0, pl.ds(at, SPAN), :] = picked[:, :key_width]
                cache_ref[1, pl.ds(at, SPAN), :] = picked[:, key_width:]

            @pl.when(at >= own_length)
            def _():
                empty = jnp.zeros((SPAN, key_width), BF16)
                cache_ref[0, pl.ds(at, SPAN), :] = empty
                cache_ref[1, pl.ds(at, SPAN), :] = empty

            return carry

        lax.fori_loop(0, spans, step, 0)
        cache_copy.start()

    heads, key_heads = query_width // HEAD_SIZE, key_width // HEAD_SIZE
    group = heads // key_heads
    factor = math.log2(math.e) / math.sqrt(HEAD_SIZE)
    tall = group * SPAN

    def span_of(slot):
        span = plan_ref[me * spans + slot]
        start, length = run_of(lengths_ref, lax.div(span, spans), workers)
        offset = lax.rem(span, spans) * SPAN
        dead = offset >= length
        needed = start + jnp.minimum(offset + SPAN, length)
        due = jnp.logical_not(dead) & (needed <= known) & (needed > prior)
        return start, length, offset, dead, due

    def result(slot):
        rows = pl.ds(pl.multiple_of(slot * SPAN, SPAN), SPAN)
        return pltpu.make_async_copy(
            attended_ref.at[rows, :], attended_out.at[rows, :], out_sems.at[slot]
        )

    def attend_slot(slot, carry):
        start, length, offset, dead, due = span_of(slot)
        out_rows = pl.ds(pl.multiple_of(slot * SPAN, SPAN), SPAN)

        if not prior:

            @pl.when(dead)
            def _():
                attended_ref[out_rows, :] = jnp.zeros((SPAN, query_width), BF16)
                result(slot).start()

        @pl.when(due)
        def _():
            queries = window(start + offset, slice(0, query_width)).astype(BF16)
            for head in range(heads):
                at = head % group * SPAN
                queries_ref[head // group, at : at + SPAN, :] = queries[
                    :, head * HEAD_SIZE : (head + 1) * HEAD_SIZE
                ]
            first = pl.multiple_of(lax.div(start, ALIGN) * ALIGN, ALIGN)
            shift = start - first
            reach = shift + jnp.minimum(offset + SPAN, length)
            tiles = lax.div(reach + SPAN - 1, SPAN)

            def attend_head(head, carry):
                def columns(at):
                    return pl.ds(pl.multiple_of(at + head * HEAD_SIZE, HEAD_SIZE), HEAD_SIZE)

                def tile_rows(tile):
                    return pl.ds(pl.multiple_of(first + tile * SPAN, ALIGN), SPAN)

                top_ref[...] = jnp.full((tall, SPAN), -1e30, F32)

                def score(tile, carry):
                    keys = rows_ref[tile_rows(tile), columns(query_width)]
                    scores = lax.dot_general(
                        queries_ref[head],
                        keys,
                        (((1,), (1,)), ((), ())),
                        preferred_element_type=F32,
                    )
                    key_pos = tile * SPAN + iota((SPAN, SPAN), 1) - shift
                    query_pos = offset + iota((SPAN, SPAN), 0)
                    allowed = (key_pos >= 0) & (key_pos <= query_pos) & (key_pos < length)
                    bias = jnp.where(allowed, 0.0, -1e30)
                    scores = scores + jnp.concatenate([bias] * group, axis=0)
                    scores_ref[tile] = scores
                    top_ref[...] = jnp.maximum(top_ref[...], scores)
                    return carry

                lax.fori_loop(0, tiles, score, 0)
                top = jnp.max(top_ref[...], axis=1, keepdims=True)

                def mix(tile, carry):
                    weights = jnp.exp2((scores_ref[tile] - top) * factor).astype(BF16)
                    values = rows_ref[tile_rows(tile), columns(query_width + key_width)]
                    values = jnp.concatenate([values, jnp.ones((SPAN, HEAD_SIZE), BF16)], axis=1)
                    return carry + jnp.dot(weights, values, preferred_element_type=F32)

                mixed = lax.fori_loop(0, tiles, mix, jnp.zeros((tall, 2 * HEAD_SIZE), F32))
                mixed = mixed[:, :HEAD_SIZE] / mixed[:, HEAD_SIZE:]
                live = offset + iota((SPAN, HEAD_SIZE), 0) < length
                for at in range(group):
                    left = pl.multiple_of((head * group + at) * HEAD_SIZE, HEAD_SIZE)
                    attended_ref[out_rows, pl.ds(left, HEAD_SIZE)] = jnp.where(
                        live, mixed[at * SPAN : (at + 1) * SPAN], 0.0
                    ).astype(BF16)
                return carry

            lax.fori_loop(0, key_heads, attend_head, 0)
            result(slot).start()

        return carry

    lax.fori_loop(0, spans, attend_slot, 0)

    def finish(slot, carry):
        _, _, _, dead, due = span_of(slot)

        @pl.when(due if prior else due | dead)
        def _():
            result(slot).wait()

        return carry

    lax.fori_loop(0, spans, finish, 0)

    @pl.when(mine)
    def _():
        cache_copy.wait()


def attend(chips, groups, known, prior, widths, slots, lengths, plan, blocks, outputs):
    query_width, key_width = widths
    width = query_width + 2 * key_width
    total = 2 * chips * sum(sum(sizes) for _, sizes in groups)
    copies = 2 * chips * sum(len(sizes) for _, sizes in groups)
    key_heads, tall = key_width // HEAD_SIZE, query_width // key_width * SPAN
    at = 2 + len(blocks)
    return pl.pallas_call(
        functools.partial(attend_kernel, chips, groups, known, prior, query_width, key_width),
        in_specs=[pl.BlockSpec(memory_space=pltpu.SMEM)] * 2
        + [pl.BlockSpec(memory_space=pl.ANY)] * (len(blocks) + len(outputs)),
        out_specs=[pl.BlockSpec(memory_space=pl.ANY)] * 2,
        out_shape=[
            jax.ShapeDtypeStruct((slots, query_width), BF16),
            jax.ShapeDtypeStruct((2, slots, key_width), BF16),
        ],
        input_output_aliases={at + index: index for index in range(len(outputs))},
        scratch_shapes=[
            pltpu.VMEM((slots, query_width), BF16),
            pltpu.VMEM((2, slots, key_width), BF16),
            pltpu.VMEM((total + 2 * SPAN, width), BF16),
            pltpu.VMEM((key_heads, tall, HEAD_SIZE), BF16),
            pltpu.VMEM((slots // SPAN + 1, tall, SPAN), F32),
            pltpu.VMEM((tall, SPAN), F32),
            pltpu.SemaphoreType.DMA((copies,)),
            pltpu.SemaphoreType.DMA((slots // SPAN + 1,)),
        ],
        compiler_params=pltpu.CompilerParams(vmem_limit_bytes=32 * MEBI),
        name="attend",
    )(lengths, plan, *blocks, *outputs)


def shift_chips(value, hop, chips):
    pairs = [(2 * x + c, 2 * ((x + hop) % chips) + c) for x in range(chips) for c in range(2)]
    return lax.ppermute(value, "req", pairs)


def swap_cores(value, chips):
    return lax.ppermute(value, "req", [(d, d ^ 1) for d in range(2 * chips)])


def local(
    chips, shards, tokens, norm_gain, w_query, key_weight, value_weight, lengths, plan
):
    workers = 2 * chips
    slots = tokens.shape[0]
    live = slots // 2
    sizes = [live * share // sum(SHARES) // ALIGN * ALIGN for share in SHARES]
    sizes[-1] = live - sum(sizes[:-1])
    bases = [workers * sum(sizes[:chunk]) for chunk in range(len(sizes))]
    weights = [
        pltpu.with_memory_space_constraint(weight, pltpu.HBM)
        for weight in (w_query, key_weight, value_weight)
    ]
    gain = norm_gain.astype(F32).reshape(1, -1)
    halfway = HEAD_SIZE // 2
    frequency = np.exp(-np.arange(halfway) * 2.0 / HEAD_SIZE * math.log(500000.0))
    frequency = jnp.asarray(np.tile(frequency, 2)[None, :], F32)

    twin = swap_cores(tokens, chips)
    first = deal(chips, bases[:1], sizes[:1], lengths, [tokens], [False])
    dealt = [
        *deal(chips, bases[:1], sizes[:1], lengths, [twin], [True], first),
        *deal(chips, bases[1:], sizes[1:], lengths, [tokens, twin], [False, True]),
    ]
    homes, aways = dealt[::2], dealt[1::2]
    routes, owned, depth = routes_of(shards)
    early = [piece for piece in range(len(owned)) if depth[piece] < max(depth)]
    late = [piece for piece in range(len(owned)) if depth[piece] == max(depth)]
    direct = [piece for piece in range(len(owned)) if depth[piece] == 1]

    def relay(line):
        for index, (source, pairs) in enumerate(routes):
            if index + 1 not in direct:
                line[index + 1] = lax.ppermute(line[source + 1], "tp", pairs)

    lines = []
    for chunk in range(len(sizes)):
        arrived = [shift_chips(aways[chunk][hop - 1], hop, chips) for hop in range(1, chips)]
        places = [(chunk - 1, piece) for piece in direct if chunk]
        places += [(chunk - 2, piece) for piece in late if chunk > 1]
        later = aways[chunk + 1 : chunk + 2] + [lines[at][piece] for at, piece in places]
        block, later = merge(homes[chunk], arrived, later)
        if chunk + 1 < len(sizes):
            aways[chunk + 1] = later.pop(0)
        for (at, piece), leaf in zip(places, later):
            lines[at][piece] = leaf
        line = {0: block}
        for index, (source, pairs) in enumerate(routes):
            if index + 1 in direct:
                line[index + 1] = lax.ppermute(block, "tp", pairs)
        lines.append(line)
        for line in lines[-2:-1]:
            relay(line)

    tables, counts = zip(
        *(visits_of([owned[piece] for piece in group], shards) for group in (early, late))
    )
    table = jnp.asarray(np.concatenate(tables, axis=1))
    table = lax.dynamic_index_in_dim(table, lax.axis_index("tp"), 0, keepdims=False)
    places = table[: 2 * counts[0]], table[2 * counts[0] :]

    blocks, groups, outputs, known = [], [], (), 0
    widths = w_query.shape[1], key_weight.shape[1]
    for chunks in GROUPS:
        if len(sizes) - 1 in chunks:
            for source in {source + 1 for source, _ in routes} - {0}:
                if depth[source] == 1:
                    lines[-1][source] = after(lines[-1][source], blocks[:1])
            relay(lines[-1])
        span = [bases[chunk] for chunk in chunks], [sizes[chunk] for chunk in chunks]
        groups.append(span)
        carried = ()
        for place, count, chosen in zip(places, counts, (early, late)):
            carried = project(
                chosen is late,
                shards,
                *span,
                place,
                count,
                lengths,
                [[lines[chunk][piece] for piece in chosen] for chunk in chunks],
                gain,
                weights,
                carried,
                frequency,
            )
        block = carried[0]
        here = [block] + [shift_chips(block, hop, chips) for hop in range(1, chips)]
        for piece in here:
            blocks += [piece, swap_cores(piece, chips)]
        prior, known = known, known + workers * sum(span[1])
        outputs = attend(
            chips, tuple(groups), known, prior, widths, slots, lengths, plan, blocks, outputs
        )
    return tuple(outputs)


def solution(mesh):
    placed = (
        P(("groups", "req"), "tp"),
        P(),
        P(None, "tp"),
        P(None, "tp"),
        P(None, "tp"),
        P("groups"),
        P("groups"),
    )
    return jax.shard_map(
        functools.partial(local, mesh.shape["req"] // 2, mesh.shape["tp"]),
        mesh=mesh,
        in_specs=placed,
        out_specs=(P(("groups", "req"), "tp"), P(None, ("groups", "req"), "tp")),
        check_vma=False,
    )
```

profile of v0, /device:TPU:0, one launch (start us, length us, event | category | flops | bytes accessed | tf_op | source)
XLA Modules:
  0.0 137.3 jit_solution(7487273045368550249)
XLA Ops:
  0.6 0.5 collective-permute-start
  1.1 1.6 %copy-done = bf16[512,2048]{1,0:T(8,128)(2,1)S(1)} copy-done((bf16[512,2048]{1,0:T(8,128)(2,1)S(1)}, bf16[512,2048]{1,0:T(8,128)(2,1)}, u32[]{:S(2)}) %copy-start) | copy-done | bytes 2097176
  2.7 0.7 copy-done.4
  3.4 1.6 %deal.4 = (bf16[64,2048]{1,0:T(8,128)(2,1)S(1)}, bf16[1,64,2048]{2,1,0:T(8,128)(2,1)S(1)}) custom-call(s32[4]{0:T(128)S(1)} %copy-done.4, bf16[512,2048]{1,0:T(8,128)(2,1)S(1)} %copy-done), custom_call_target="tpu_custom_call" | custom-call | flops 268435456 | bytes 2621440 | tf_op jit(solution)/shard_map/deal/pallas_call | solution.py:78
  5.0 0.1 collective-permute-done.refs_1_.refs_0_
  5.1 1.7 %deal.5 = (bf16[64,2048]{1,0:T(8,128)(2,1)S(1)}, bf16[1,64,2048]{2,1,0:T(8,128)(2,1)S(1)}) custom-call(s32[4]{0:T(128)S(1)} %copy-done.4, bf16[512,2048]{1,0:T(8,128)(2,1)S(1)} %collective-permute-done.refs_1_.refs_0_, bf16[64,2048]{1,0:T(8,128)(2,1)S(1)} %get-tuple-element.30.refs_1_, bf16[1,64,2048]{2,1,0:T(8,128)(2,1)S(1)} %get-tuple-element.31.refs_2_), custom_call_target="tpu_custom_call" | custom-call | flops 268435456 | bytes 2621440 | tf_op jit(solution)/shard_map/deal/pallas_call | solution.py:78
  6.8 0.0 copy-start.5
  6.8 0.0 copy-start.6
  6.8 2.9 %collective-permute-start.1 = (bf16[64,2048]{1,0:T(8,128)(2,1)S(1)}, bf16[64,2048]{1,0:T(8,128)(2,1)S(1)}, u32[]{:S(2)}, u32[]{:S(2)}) collective-permute-start(bf16[64,2048]{1,0:T(8,128)(2,1)S(1)} %bitcast.14), channel_id=1, source_target_pairs={{0,8},{4,12},{8,0},{12,4},{1,9},{5,13},{9,1},{13,5},{2,10},{6,14},... | collective-permute-start | bytes 786440 | tf_op jit(solution)/shard_map/ppermute | solution.py:542
  9.8 3.7 %deal.3 = (bf16[96,2048]{1,0:T(8,128)(2,1)S(1)}, bf16[1,96,2048]{2,1,0:T(8,128)(2,1)S(1)}, bf16[96,2048]{1,0:T(8,128)(2,1)S(1)}, bf16[1,96,2048]{2,1,0:T(8,128)(2,1)S(1)}) custom-call(s32[4]{0:T(128)S(1)} %copy-done.4, bf16[512,2048]{1,0:T(8,128)(2,1)S(1)} %copy-done.1, bf16[512,2048]{1,0:T(8,128)(2,1)S(1)} %collective-permute-done.refs_1_.refs_0_), custom_call_target="tpu_custom_call" | custom-call | flops 1610612736 | bytes 5767168 | tf_op jit(solution)/shard_map/deal/pallas_call | solution.py:78
  13.5 2.9 %collective-permute-done.1.refs_0_ = bf16[64,2048]{1,0:T(8,128)(2,1)S(1)} collective-permute-done((bf16[64,2048]{1,0:T(8,128)(2,1)S(1)}, bf16[64,2048]{1,0:T(8,128)(2,1)S(1)}, u32[]{:S(2)}, u32[]{:S(2)}) %collective-permute-start.1) | collective-permute-done | bytes 262176 | tf_op jit(solution)/shard_map/ppermute | solution.py:542
  16.4 0.0 copy-start.2
  16.4 1.8 %collective-permute-start.2 = (bf16[96,2048]{1,0:T(8,128)(2,1)S(1)}, bf16[96,2048]{1,0:T(8,128)(2,1)S(1)}, u32[]{:S(2)}, u32[]{:S(2)}) collective-permute-start(bf16[96,2048]{1,0:T(8,128)(2,1)S(1)} %bitcast.12), channel_id=1, source_target_pairs={{0,8},{4,12},{8,0},{12,4},{1,9},{5,13},{9,1},{13,5},{2,10},{6,14},... | collective-permute-start | bytes 1179656 | tf_op jit(solution)/shard_map/ppermute | solution.py:542
  18.2 2.6 %collective-permute-start.5 = (bf16[64,2048]{1,0:T(8,128)(2,1)S(1)}, bf16[64,2048]{1,0:T(8,128)(2,1)S(1)}, u32[]{:S(2)}, u32[]{:S(2)}) collective-permute-start(bf16[64,2048]{1,0:T(8,128)(2,1)S(1)} %get-tuple-element.37.refs_0_), channel_id=1, source_target_pairs={{0,2},{1,3},{2,0},{3,1},{4,6},{5,7},{6,4},{7,5},{8,10},{9,11},{10,... | collective-permute-start | bytes 786440 | tf_op jit(solution)/shard_map/ppermute | solution.py:598
  20.8 1.6 %collective-permute-start.4 = (bf16[64,2048]{1,0:T(8,128)(2,1)S(1)}, bf16[64,2048]{1,0:T(8,128)(2,1)S(1)}, u32[]{:S(2)}, u32[]{:S(2)}) collective-permute-start(bf16[64,2048]{1,0:T(8,128)(2,1)S(1)} %get-tuple-element.37.refs_0_), channel_id=1, source_target_pairs={{0,1},{1,0},{2,3},{3,2},{4,5},{5,4},{6,7},{7,6},{8,9},{9,8},{10,11... | collective-permute-start | bytes 786440 | tf_op jit(solution)/shard_map/ppermute | solution.py:598
  22.4 0.7 collective-permute-start.3
  23.1 10.1 %collective-permute-done.5.refs_4_ = bf16[64,2048]{1,0:T(8,128)(2,1)S(1)} collective-permute-done((bf16[64,2048]{1,0:T(8,128)(2,1)S(1)}, bf16[64,2048]{1,0:T(8,128)(2,1)S(1)}, u32[]{:S(2)}, u32[]{:S(2)}) %collective-permute-start.5) | collective-permute-done | bytes 262176 | tf_op jit(solution)/shard_map/ppermute | solution.py:598
  33.2 0.0 collective-permute-done.4.refs_3_
  33.2 0.0 collective-permute-done.3.refs_2_
  33.2 0.0 collective-permute-done.2.refs_0_
  33.3 0.6 collective-permute-start.6
  33.9 7.0 %collective-permute-start.9 = (bf16[96,2048]{1,0:T(8,128)(2,1)S(1)}, bf16[96,2048]{1,0:T(8,128)(2,1)S(1)}, u32[]{:S(2)}, u32[]{:S(2)}) collective-permute-start(bf16[96,2048]{1,0:T(8,128)(2,1)S(1)} %get-tuple-element.39.refs_4_), channel_id=1, source_target_pairs={{0,2},{1,3},{2,0},{3,1},{4,6},{5,7},{6,4},{7,5},{8,10},{9,11},{10,... | collective-permute-start | bytes 1179656 | tf_op jit(solution)/shard_map/ppermute | solution.py:598
  40.8 0.0 copy-done.2
  40.9 0.0 collective-permute-start.8
  40.9 0.7 collective-permute-start.7
  41.5 1.3 collective-permute-start.10
  42.8 0.7 constant_dynamic-slice_fusion
  43.5 21.6 %collective-permute-done.10.refs_4_ = bf16[64,2048]{1,0:T(8,128)(2,1)S(1)} collective-permute-done((bf16[64,2048]{1,0:T(8,128)(2,1)S(1)}, bf16[64,2048]{1,0:T(8,128)(2,1)S(1)}, u32[]{:S(2)}, u32[]{:S(2)}) %collective-permute-start.10) | collective-permute-done | bytes 262176 | tf_op jit(solution)/shard_map/ppermute | solution.py:582
  65.1 0.0 collective-permute-done.6.refs_0_
  65.1 0.0 collective-permute-done.9.refs_3_
  65.1 0.0 collective-permute-done.8.refs_2_
  65.1 0.0 collective-permute-done.7.refs_1_
  65.2 1.3 collective-permute-start.11
  66.5 0.1 slice_bitcast_fusion.1.place_ref
  66.6 0.7 reshape.13
  67.3 2.7 %collective-permute-start.18 = (bf16[96,2048]{1,0:T(8,128)(2,1)S(1)}, bf16[96,2048]{1,0:T(8,128)(2,1)S(1)}, u32[]{:S(2)}, u32[]{:S(2)}) collective-permute-start(bf16[96,2048]{1,0:T(8,128)(2,1)S(1)} %get-tuple-element.49.refs_0_), channel_id=1, source_target_pairs={{0,1},{1,0},{2,3},{3,2},{4,5},{5,4},{6,7},{7,6},{8,9},{9,8},{10,11... | collective-permute-start | bytes 1179656 | tf_op jit(solution)/shard_map/ppermute | solution.py:598
  69.9 0.7 collective-permute-start.17
  70.6 2.8 %collective-permute-start.15 = (bf16[96,2048]{1,0:T(8,128)(2,1)S(1)}, bf16[96,2048]{1,0:T(8,128)(2,1)S(1)}, u32[]{:S(2)}, u32[]{:S(2)}) collective-permute-start(bf16[96,2048]{1,0:T(8,128)(2,1)S(1)} %get-tuple-element.49.refs_0_), channel_id=1, source_target_pairs={{0,2},{1,3},{2,0},{3,1},{4,6},{5,7},{6,4},{7,5},{8,10},{9,11},{10,... | collective-permute-start | bytes 1179656 | tf_op jit(solution)/shard_map/ppermute | solution.py:598
  73.4 0.9 copy-done.3
  74.3 10.0 %project.4 = (f32[160,1536]{1,0:T(8,128)S(1)}, f32[160,128]{1,0:T(8,128)S(1)}) custom-call(s32[8]{0:T(128)S(1)} %slice_bitcast_fusion.place_ref, s32[4]{0:T(128)S(1)} %copy-done.5, bf16[64,2048]{1,0:T(8,128)(2,1)S(1)} %copy-done.3, bf16[64,2048]{1,0:T(8,128)(2,1)S(1)} %get-tuple-element.43.refs_1_, bf16[64,2048]{1,0:T(8,128)(2,1)S(1)} %get-tuple-element.44.refs_2_, ...), custom_call_target="tpu_custom_call" | custom-call | flops 4026531840 | bytes 27131904 | tf_op jit(solution)/shard_map/project/pallas_call | solution.py:294
  84.3 0.0 collective-permute-done.11.refs_1_
  84.4 4.7 %project.5.refs_1_.refs_0_ = bf16[160,1536]{1,0:T(8,128)(2,1)S(1)} custom-call(s32[2]{0:T(128)S(1)} %slice_bitcast_fusion.1.place_ref, s32[4]{0:T(128)S(1)} %copy-done.5, bf16[64,2048]{1,0:T(8,128)(2,1)S(1)} %get-tuple-element.41.refs_0_, bf16[96,2048]{1,0:T(8,128)(2,1)S(1)} %collective-permute-done.11.refs_1_, f32[1,8192]{1,0:T(1,128)S(1)} %bitcast.9, ...), custom_call_target="tpu_custom_call" | custom-call | flops 1006632960 | bytes 8257536 | tf_op jit(solution)/shard_map/project/pallas_call | solution.py:294
  89.1 9.5 %collective-permute-done.15.refs_0_ = bf16[96,2048]{1,0:T(8,128)(2,1)S(1)} collective-permute-done((bf16[96,2048]{1,0:T(8,128)(2,1)S(1)}, bf16[96,2048]{1,0:T(8,128)(2,1)S(1)}, u32[]{:S(2)}, u32[]{:S(2)}) %collective-permute-start.15) | collective-permute-done | bytes 393248 | tf_op jit(solution)/shard_map/ppermute | solution.py:598
  98.5 1.3 collective-permute-start.16
  99.8 1.5 %collective-permute-start.13 = (bf16[160,1536]{1,0:T(8,128)(2,1)S(1)}, bf16[160,1536]{1,0:T(8,128)(2,1)S(1)}, u32[]{:S(2)}, u32[]{:S(2)}) collective-permute-start(bf16[160,1536]{1,0:T(8,128)(2,1)S(1)} %project.5.refs_1_.refs_0_), channel_id=1, source_target_pairs={{0,8},{4,12},{8,0},{12,4},{1,9},{5,13},{9,1},{13,5},{2,10},{6,14},... | collective-permute-start | bytes 1474568 | tf_op jit(solution)/shard_map/ppermute | solution.py:542
  101.4 0.0 collective-permute-done.18.refs_2_
  101.4 0.0 collective-permute-done.17.refs_1_
  101.4 9.8 %project.6 = (f32[96,1536]{1,0:T(8,128)S(1)}, f32[96,128]{1,0:T(8,128)S(1)}) custom-call(s32[8]{0:T(128)S(1)} %slice_bitcast_fusion.place_ref, s32[4]{0:T(128)S(1)} %copy-done.5, bf16[96,2048]{1,0:T(8,128)(2,1)S(1)} %get-tuple-element.49.refs_0_, bf16[96,2048]{1,0:T(8,128)(2,1)S(1)} %collective-permute-done.17.refs_1_, ...), custom_call_target="tpu_custom_call" | custom-call | flops 2415919104 | bytes 26345472 | tf_op jit(solution)/shard_map/project/pallas_call | solution.py:294
  111.2 0.0 collective-permute-done.16.refs_0_
  111.2 0.0 copy-start.7
  111.2 4.4 %project.7.refs_4_ = bf16[96,1536]{1,0:T(8,128)(2,1)S(1)} custom-call(s32[2]{0:T(128)S(1)} %slice_bitcast_fusion.1.place_ref, s32[4]{0:T(128)S(1)} %copy-done.5, bf16[96,2048]{1,0:T(8,128)(2,1)S(1)} %collective-permute-done.16.refs_0_, f32[1,8192]{1,0:T(1,128)S(1)} %bitcast.11, bf16[8192,1024]{1,0:T(8,128)(2,1)} %refs_2_.1, bf16[8192,256]{1,0:T(8,128)(2,1)} %refs_3_.3, ...), custom_call_target="tpu_custom_call" | custom-call | flops 603979776 | bytes 7471104 | tf_op jit(solution)/shard_map/project/pallas_call | solution.py:294
  115.7 0.6 collective-permute-start.20
  116.3 0.0 collective-permute-start.12
  116.3 0.0 collective-permute-done.13.refs_2_
  116.3 0.5 collective-permute-start.14
  116.8 0.0 collective-permute-start.19
  116.8 6.0 %collective-permute-done.20.refs_6_ = bf16[96,1536]{1,0:T(8,128)(2,1)S(1)} collective-permute-done((bf16[96,1536]{1,0:T(8,128)(2,1)S(1)}, bf16[96,1536]{1,0:T(8,128)(2,1)S(1)}, u32[]{:S(2)}, u32[]{:S(2)}) %collective-permute-start.20) | collective-permute-done | bytes 294944 | tf_op jit(solution)/shard_map/ppermute | solution.py:542
  122.8 0.0 collective-permute-start.21
  122.8 0.0 collective-permute-done.12.refs_1_
  122.8 0.0 collective-permute-done.14.refs_3_
  122.8 8.6 %attend.2 = (bf16[512,1024]{1,0:T(8,128)(2,1)}, bf16[2,512,256]{2,1,0:T(8,128)(2,1)}) custom-call(s32[4]{0:T(128)S(1)} %copy-done.5, s32[16]{0:T(128)S(1)} %copy-done.7, bf16[160,1536]{1,0:T(8,128)(2,1)S(1)} %project.5.refs_1_.refs_0_, bf16[160,1536]{1,0:T(8,128)(2,1)S(1)} %collective-permute-done.12.refs_1_, ...), custom_call_target="tpu_custom_call" | custom-call | tf_op jit(solution)/shard_map/attend/pallas_call | solution.py:515
  131.4 0.0 collective-permute-done.19.refs_5_
  131.4 0.0 collective-permute-done.21.refs_7_
  131.5 5.8 %attend.3 = (bf16[512,1024]{1,0:T(8,128)(2,1)}, bf16[2,512,256]{2,1,0:T(8,128)(2,1)}) custom-call(s32[4]{0:T(128)S(1)} %copy-done.5, s32[16]{0:T(128)S(1)} %copy-done.7, bf16[160,1536]{1,0:T(8,128)(2,1)S(1)} %project.5.refs_1_.refs_0_, bf16[160,1536]{1,0:T(8,128)(2,1)S(1)} %collective-permute-done.12.refs_1_, ...), custom_call_target="tpu_custom_call", output_to_operand_aliasing={{0}: (10, {}), {1}: (11, {})} | custom-call | tf_op jit(solution)/shard_map/attend/pallas_call | solution.py:515
  (13 shorter events, 0.1 us)
Async XLA Ops:
  0.6 4.5 %collective-permute-start = (bf16[512,2048]{1,0:T(8,128)(2,1)}, bf16[512,2048]{1,0:T(8,128)(2,1)S(1)}, u32[]{:S(2)}, u32[]{:S(2)}) collective-permute-start(bf16[512,2048]{1,0:T(8,128)(2,1)} %refs_0_.3), channel_id=1, source_target_pairs={{0,4},{4,0},{8,12},{12,8},{1,5},{5,1},{9,13},{13,9},{2,6},{6,2},{1... | collective-permute-start | bytes 6291464 | tf_op jit(solution)/shard_map/ppermute | solution.py:546
  1.1 1.6 %copy-start = (bf16[512,2048]{1,0:T(8,128)(2,1)S(1)}, bf16[512,2048]{1,0:T(8,128)(2,1)}, u32[]{:S(2)}) copy-start(bf16[512,2048]{1,0:T(8,128)(2,1)} %refs_0_.3) | copy-start | bytes 6291460
  2.7 0.7 copy-start.4
  3.4 6.4 %copy-start.1 = (bf16[512,2048]{1,0:T(8,128)(2,1)S(1)}, bf16[512,2048]{1,0:T(8,128)(2,1)}, u32[]{:S(2)}) copy-start(bf16[512,2048]{1,0:T(8,128)(2,1)} %refs_0_.3) | copy-start | bytes 6291460
  6.8 66.6 %copy-start.5 = (s32[4]{0:T(128)S(1)}, s32[4]{0:T(128)}, u32[]{:S(2)}) copy-start(s32[4]{0:T(128)} %lengths_ref.17) | copy-start | bytes 52
  6.8 66.5 %copy-start.6 = (f32[1,128]{1,0:T(1,128)S(1)}, f32[1,128]{1,0:T(1,128)}, u32[]{:S(2)}) copy-start(f32[1,128]{1,0:T(1,128)} %constant.14.clone.refs_12_.refs_8_.refs_7_) | copy-start | bytes 1540
  6.8 9.5 %collective-permute-start.1 = (bf16[64,2048]{1,0:T(8,128)(2,1)S(1)}, bf16[64,2048]{1,0:T(8,128)(2,1)S(1)}, u32[]{:S(2)}, u32[]{:S(2)}) collective-permute-start(bf16[64,2048]{1,0:T(8,128)(2,1)S(1)} %bitcast.14), channel_id=1, source_target_pairs={{0,8},{4,12},{8,0},{12,4},{1,9},{5,13},{9,1},{13,5},{2,10},{6,14},... | collective-permute-start | bytes 786440 | tf_op jit(solution)/shard_map/ppermute | solution.py:542
  16.4 24.4 %copy-start.2 = (bf16[64,2048]{1,0:T(8,128)(2,1)}, bf16[64,2048]{1,0:T(8,128)(2,1)S(1)}, u32[]{:S(2)}) copy-start(bf16[64,2048]{1,0:T(8,128)(2,1)S(1)} %get-tuple-element.37.refs_0_) | copy-start | bytes 786436
  16.4 16.8 %collective-permute-start.2 = (bf16[96,2048]{1,0:T(8,128)(2,1)S(1)}, bf16[96,2048]{1,0:T(8,128)(2,1)S(1)}, u32[]{:S(2)}, u32[]{:S(2)}) collective-permute-start(bf16[96,2048]{1,0:T(8,128)(2,1)S(1)} %bitcast.12), channel_id=1, source_target_pairs={{0,8},{4,12},{8,0},{12,4},{1,9},{5,13},{9,1},{13,5},{2,10},{6,14},... | collective-permute-start | bytes 1179656 | tf_op jit(solution)/shard_map/ppermute | solution.py:542
  18.2 15.0 %collective-permute-start.5 = (bf16[64,2048]{1,0:T(8,128)(2,1)S(1)}, bf16[64,2048]{1,0:T(8,128)(2,1)S(1)}, u32[]{:S(2)}, u32[]{:S(2)}) collective-permute-start(bf16[64,2048]{1,0:T(8,128)(2,1)S(1)} %get-tuple-element.37.refs_0_), channel_id=1, source_target_pairs={{0,2},{1,3},{2,0},{3,1},{4,6},{5,7},{6,4},{7,5},{8,10},{9,11},{10,... | collective-permute-start | bytes 786440 | tf_op jit(solution)/shard_map/ppermute | solution.py:598
  20.8 12.4 %collective-permute-start.4 = (bf16[64,2048]{1,0:T(8,128)(2,1)S(1)}, bf16[64,2048]{1,0:T(8,128)(2,1)S(1)}, u32[]{:S(2)}, u32[]{:S(2)}) collective-permute-start(bf16[64,2048]{1,0:T(8,128)(2,1)S(1)} %get-tuple-element.37.refs_0_), channel_id=1, source_target_pairs={{0,1},{1,0},{2,3},{3,2},{4,5},{5,4},{6,7},{7,6},{8,9},{9,8},{10,11... | collective-permute-start | bytes 786440 | tf_op jit(solution)/shard_map/ppermute | solution.py:598
  22.4 10.8 %collective-permute-start.3 = (bf16[64,2048]{1,0:T(8,128)(2,1)S(1)}, bf16[64,2048]{1,0:T(8,128)(2,1)S(1)}, u32[]{:S(2)}, u32[]{:S(2)}) collective-permute-start(bf16[64,2048]{1,0:T(8,128)(2,1)S(1)} %get-tuple-element.37.refs_0_), channel_id=1, source_target_pairs={{1,2},{2,1},{5,6},{6,5},{9,10},{10,9},{13,14},{14,13},{17,18},{18,... | collective-permute-start | bytes 786440 | tf_op jit(solution)/shard_map/ppermute | solution.py:598
  33.3 31.8 %collective-permute-start.6 = (bf16[96,2048]{1,0:T(8,128)(2,1)S(1)}, bf16[96,2048]{1,0:T(8,128)(2,1)S(1)}, u32[]{:S(2)}, u32[]{:S(2)}) collective-permute-start(bf16[96,2048]{1,0:T(8,128)(2,1)S(1)} %bitcast.13), channel_id=1, source_target_pairs={{0,8},{4,12},{8,0},{12,4},{1,9},{5,13},{9,1},{13,5},{2,10},{6,14},... | collective-permute-start | bytes 1179656 | tf_op jit(solution)/shard_map/ppermute | solution.py:542
  33.9 31.2 %collective-permute-start.9 = (bf16[96,2048]{1,0:T(8,128)(2,1)S(1)}, bf16[96,2048]{1,0:T(8,128)(2,1)S(1)}, u32[]{:S(2)}, u32[]{:S(2)}) collective-permute-start(bf16[96,2048]{1,0:T(8,128)(2,1)S(1)} %get-tuple-element.39.refs_4_), channel_id=1, source_target_pairs={{0,2},{1,3},{2,0},{3,1},{4,6},{5,7},{6,4},{7,5},{8,10},{9,11},{10,... | collective-permute-start | bytes 1179656 | tf_op jit(solution)/shard_map/ppermute | solution.py:598
  40.9 24.3 %collective-permute-start.8 = (bf16[96,2048]{1,0:T(8,128)(2,1)S(1)}, bf16[96,2048]{1,0:T(8,128)(2,1)S(1)}, u32[]{:S(2)}, u32[]{:S(2)}) collective-permute-start(bf16[96,2048]{1,0:T(8,128)(2,1)S(1)} %get-tuple-element.39.refs_4_), channel_id=1, source_target_pairs={{0,1},{1,0},{2,3},{3,2},{4,5},{5,4},{6,7},{7,6},{8,9},{9,8},{10,11... | collective-permute-start | bytes 1179656 | tf_op jit(solution)/shard_map/ppermute | solution.py:598
  40.9 24.3 %collective-permute-start.7 = (bf16[96,2048]{1,0:T(8,128)(2,1)S(1)}, bf16[96,2048]{1,0:T(8,128)(2,1)S(1)}, u32[]{:S(2)}, u32[]{:S(2)}) collective-permute-start(bf16[96,2048]{1,0:T(8,128)(2,1)S(1)} %get-tuple-element.39.refs_4_), channel_id=1, source_target_pairs={{1,2},{2,1},{5,6},{6,5},{9,10},{10,9},{13,14},{14,13},{17,18},{18,... | collective-permute-start | bytes 1179656 | tf_op jit(solution)/shard_map/ppermute | solution.py:598
  41.5 23.6 %collective-permute-start.10 = (bf16[64,2048]{1,0:T(8,128)(2,1)S(1)}, bf16[64,2048]{1,0:T(8,128)(2,1)S(1)}, u32[]{:S(2)}, u32[]{:S(2)}) collective-permute-start(bf16[64,2048]{1,0:T(8,128)(2,1)S(1)} %get-tuple-element.40.refs_3_), channel_id=1, source_target_pairs={{2,3},{1,0},{6,7},{5,4},{10,11},{9,8},{14,15},{13,12},{18,19},{17,... | collective-permute-start | bytes 786440 | tf_op jit(solution)/shard_map/ppermute | solution.py:582
  65.2 19.2 %collective-permute-start.11 = (bf16[96,2048]{1,0:T(8,128)(2,1)S(1)}, bf16[96,2048]{1,0:T(8,128)(2,1)S(1)}, u32[]{:S(2)}, u32[]{:S(2)}) collective-permute-start(bf16[96,2048]{1,0:T(8,128)(2,1)S(1)} %get-tuple-element.42.refs_7_), channel_id=1, source_target_pairs={{2,3},{1,0},{6,7},{5,4},{10,11},{9,8},{14,15},{13,12},{18,19},{17,... | collective-permute-start | bytes 1179656 | tf_op jit(solution)/shard_map/ppermute | solution.py:582
  67.3 34.1 %collective-permute-start.18 = (bf16[96,2048]{1,0:T(8,128)(2,1)S(1)}, bf16[96,2048]{1,0:T(8,128)(2,1)S(1)}, u32[]{:S(2)}, u32[]{:S(2)}) collective-permute-start(bf16[96,2048]{1,0:T(8,128)(2,1)S(1)} %get-tuple-element.49.refs_0_), channel_id=1, source_target_pairs={{0,1},{1,0},{2,3},{3,2},{4,5},{5,4},{6,7},{7,6},{8,9},{9,8},{10,11... | collective-permute-start | bytes 1179656 | tf_op jit(solution)/shard_map/ppermute | solution.py:598
  69.9 31.4 %collective-permute-start.17 = (bf16[96,2048]{1,0:T(8,128)(2,1)S(1)}, bf16[96,2048]{1,0:T(8,128)(2,1)S(1)}, u32[]{:S(2)}, u32[]{:S(2)}) collective-permute-start(bf16[96,2048]{1,0:T(8,128)(2,1)S(1)} %get-tuple-element.49.refs_0_), channel_id=1, source_target_pairs={{1,2},{2,1},{5,6},{6,5},{9,10},{10,9},{13,14},{14,13},{17,18},{18,... | collective-permute-start | bytes 1179656 | tf_op jit(solution)/shard_map/ppermute | solution.py:598
  70.6 27.9 %collective-permute-start.15 = (bf16[96,2048]{1,0:T(8,128)(2,1)S(1)}, bf16[96,2048]{1,0:T(8,128)(2,1)S(1)}, u32[]{:S(2)}, u32[]{:S(2)}) collective-permute-start(bf16[96,2048]{1,0:T(8,128)(2,1)S(1)} %get-tuple-element.49.refs_0_), channel_id=1, source_target_pairs={{0,2},{1,3},{2,0},{3,1},{4,6},{5,7},{6,4},{7,5},{8,10},{9,11},{10,... | collective-permute-start | bytes 1179656 | tf_op jit(solution)/shard_map/ppermute | solution.py:598
  73.4 1.0 copy-start.3
  98.5 12.7 %collective-permute-start.16 = (bf16[96,2048]{1,0:T(8,128)(2,1)S(1)}, bf16[96,2048]{1,0:T(8,128)(2,1)S(1)}, u32[]{:S(2)}, u32[]{:S(2)}) collective-permute-start(bf16[96,2048]{1,0:T(8,128)(2,1)S(1)} %after.1.refs_3_), channel_id=1, source_target_pairs={{2,3},{1,0},{6,7},{5,4},{10,11},{9,8},{14,15},{13,12},{18,19},{17,... | collective-permute-start | bytes 1179656 | tf_op jit(solution)/shard_map/ppermute | solution.py:582
  99.8 16.4 %collective-permute-start.13 = (bf16[160,1536]{1,0:T(8,128)(2,1)S(1)}, bf16[160,1536]{1,0:T(8,128)(2,1)S(1)}, u32[]{:S(2)}, u32[]{:S(2)}) collective-permute-start(bf16[160,1536]{1,0:T(8,128)(2,1)S(1)} %project.5.refs_1_.refs_0_), channel_id=1, source_target_pairs={{0,8},{4,12},{8,0},{12,4},{1,9},{5,13},{9,1},{13,5},{2,10},{6,14},... | collective-permute-start | bytes 1474568 | tf_op jit(solution)/shard_map/ppermute | solution.py:542
  111.2 11.6 %copy-start.7 = (s32[16]{0:T(128)S(1)}, s32[16]{0:T(128)}, u32[]{:S(2)}) copy-start(s32[16]{0:T(128)} %plan_ref.3) | copy-start | bytes 196
  115.7 7.2 %collective-permute-start.20 = (bf16[96,1536]{1,0:T(8,128)(2,1)S(1)}, bf16[96,1536]{1,0:T(8,128)(2,1)S(1)}, u32[]{:S(2)}, u32[]{:S(2)}) collective-permute-start(bf16[96,1536]{1,0:T(8,128)(2,1)S(1)} %project.7.refs_4_), channel_id=1, source_target_pairs={{0,8},{4,12},{8,0},{12,4},{1,9},{5,13},{9,1},{13,5},{2,10},{6,14},... | collective-permute-start | bytes 884744 | tf_op jit(solution)/shard_map/ppermute | solution.py:542
  116.3 6.6 %collective-permute-start.12 = (bf16[160,1536]{1,0:T(8,128)(2,1)S(1)}, bf16[160,1536]{1,0:T(8,128)(2,1)S(1)}, u32[]{:S(2)}, u32[]{:S(2)}) collective-permute-start(bf16[160,1536]{1,0:T(8,128)(2,1)S(1)} %project.5.refs_1_.refs_0_), channel_id=1, source_target_pairs={{0,4},{4,0},{8,12},{12,8},{1,5},{5,1},{9,13},{13,9},{2,6},{6,2},{1... | collective-permute-start | bytes 1474568 | tf_op jit(solution)/shard_map/ppermute | solution.py:546
  116.3 6.6 %collective-permute-start.14 = (bf16[160,1536]{1,0:T(8,128)(2,1)S(1)}, bf16[160,1536]{1,0:T(8,128)(2,1)S(1)}, u32[]{:S(2)}, u32[]{:S(2)}) collective-permute-start(bf16[160,1536]{1,0:T(8,128)(2,1)S(1)} %collective-permute-done.13.refs_2_), channel_id=1, source_target_pairs={{0,4},{4,0},{8,12},{12,8},{1,5},{5,1},{9,13},{13,9},{2,6},{6,2},{1... | collective-permute-start | bytes 1474568 | tf_op jit(solution)/shard_map/ppermute | solution.py:546
  116.8 14.7 %collective-permute-start.19 = (bf16[96,1536]{1,0:T(8,128)(2,1)S(1)}, bf16[96,1536]{1,0:T(8,128)(2,1)S(1)}, u32[]{:S(2)}, u32[]{:S(2)}) collective-permute-start(bf16[96,1536]{1,0:T(8,128)(2,1)S(1)} %project.7.refs_4_), channel_id=1, source_target_pairs={{0,4},{4,0},{8,12},{12,8},{1,5},{5,1},{9,13},{13,9},{2,6},{6,2},{1... | collective-permute-start | bytes 884744 | tf_op jit(solution)/shard_map/ppermute | solution.py:546
  122.8 8.6 %collective-permute-start.21 = (bf16[96,1536]{1,0:T(8,128)(2,1)S(1)}, bf16[96,1536]{1,0:T(8,128)(2,1)S(1)}, u32[]{:S(2)}, u32[]{:S(2)}) collective-permute-start(bf16[96,1536]{1,0:T(8,128)(2,1)S(1)} %collective-permute-done.20.refs_6_), channel_id=1, source_target_pairs={{0,4},{4,0},{8,12},{12,8},{1,5},{5,1},{9,13},{13,9},{2,6},{6,2},{1... | collective-permute-start | bytes 884744 | tf_op jit(solution)/shard_map/ppermute | solution.py:546
where the time goes:
time: 140 us; the launch traced here: 137 us
  Pallas kernels  50.5 us (36%)
  waiting for transfers between devices  50.2 us (36%)
  starting transfers between devices  31 us (22%)
  local copies, waits for them, and re-layouts  4 us (3%)
    pallas_call x4, Pallas kernels, project(): pl.pallas_call(functools.partial(project_kernel, len(lines[0]), bool(carr...  29 us
    ppermute x3, waiting for transfers between devices, relay(): line[index + 1] = lax.ppermute(line[source + 1], 'tp', pairs)  21.6 us
    ppermute x9, waiting for transfers between devices, local(): line[index + 1] = lax.ppermute(block, 'tp', pairs)  19.6 us
    ppermute x9, starting transfers between devices, local(): line[index + 1] = lax.ppermute(block, 'tp', pairs)  18.6 us
    pallas_call x2, Pallas kernels, attend(): pl.pallas_call(functools.partial(attend_kernel, chips, groups, known, pri...  14.4 us
    ppermute x5, waiting for transfers between devices, shift_chips(): return lax.ppermute(value, 'req', pairs)  8.91 us
    ppermute x5, starting transfers between devices, shift_chips(): return lax.ppermute(value, 'req', pairs)  7.49 us
    pallas_call x3, Pallas kernels, deal(): pl.pallas_call(functools.partial(deal_kernel, chips, bases, sizes, twins)...  7.04 us
  transfers between devices with their start and end apart: 22, of which 6 were waited for; matrix products, arithmetic and copies ran while one was open for 1% of the time, Pallas kernels for 31%

commit v1 on v0

--- a/solution.py
+++ b/solution.py
@@ -12,6 +12,7 @@
 HEAD_SIZE = 128
 SPAN = 128
 ALIGN = 16
+TILE = 2 * SPAN
 SHARES = (4, 6, 6)
 GROUPS = ((0, 1), (2,))
 DEPTH = 1024
@@ -117,22 +118,6 @@
         name="merge",
     )(home, *arrived, *later)
     return block, later
-
-
-def after(array, anchors):
-    def kernel(*refs):
-        pass
-
-    anywhere = pl.BlockSpec(memory_space=pl.ANY)
-    return pl.pallas_call(
-        kernel,
-        in_specs=[anywhere] * (1 + len(anchors)),
-        out_specs=anywhere,
-        out_shape=jax.ShapeDtypeStruct(array.shape, array.dtype),
-        input_output_aliases={0: 0},
-        compiler_params=pltpu.CompilerParams(vmem_limit_bytes=MEBI),
-        name="after",
-    )(array, *anchors)
 
 
 def routes_of(shards):
@@ -435,54 +420,59 @@
             first = pl.multiple_of(lax.div(start, ALIGN) * ALIGN, ALIGN)
             shift = start - first
             reach = shift + jnp.minimum(offset + SPAN, length)
-            tiles = lax.div(reach + SPAN - 1, SPAN)
-
-            def attend_head(head, carry):
-                def columns(at):
-                    return pl.ds(pl.multiple_of(at + head * HEAD_SIZE, HEAD_SIZE), HEAD_SIZE)
-
-                def tile_rows(tile):
-                    return pl.ds(pl.multiple_of(first + tile * SPAN, ALIGN), SPAN)
-
-                top_ref[...] = jnp.full((tall, SPAN), -1e30, F32)
-
-                def score(tile, carry):
-                    keys = rows_ref[tile_rows(tile), columns(query_width)]
+            tiles = lax.div(reach + TILE - 1, TILE)
+
+            def columns(at, head):
+                return slice(at + head * HEAD_SIZE, at + (head + 1) * HEAD_SIZE)
+
+            def tile_rows(tile):
+                return pl.ds(pl.multiple_of(first + tile * TILE, ALIGN), TILE)
+
+            top_ref[...] = jnp.full(top_ref.shape, -1e30, F32)
+
+            def score(tile, carry):
+                key_pos = tile * TILE + iota((SPAN, TILE), 1) - shift
+                query_pos = offset + iota((SPAN, TILE), 0)
+                allowed = (key_pos >= 0) & (key_pos <= query_pos) & (key_pos < length)
+                bias = jnp.where(allowed, 0.0, -1e30)
+                bias = jnp.concatenate([bias] * group, axis=0)
+                for head in range(key_heads):
                     scores = lax.dot_general(
                         queries_ref[head],
-                        keys,
+                        rows_ref[tile_rows(tile), columns(query_width, head)],
                         (((1,), (1,)), ((), ())),
                         preferred_element_type=F32,
                     )
-                    key_pos = tile * SPAN + iota((SPAN, SPAN), 1) - shift
-                    query_pos = offset + iota((SPAN, SPAN), 0)
-                    allowed = (key_pos >= 0) & (key_pos <= query_pos) & (key_pos < length)
-                    bias = jnp.where(allowed, 0.0, -1e30)
-                    scores = scores + jnp.concatenate([bias] * group, axis=0)
-                    scores_ref[tile] = scores
-                    top_ref[...] = jnp.maximum(top_ref[...], scores)
-                    return carry
-
-                lax.fori_loop(0, tiles, score, 0)
-                top = jnp.max(top_ref[...], axis=1, keepdims=True)
-
-                def mix(tile, carry):
-                    weights = jnp.exp2((scores_ref[tile] - top) * factor).astype(BF16)
-                    values = rows_ref[tile_rows(tile), columns(query_width + key_width)]
-                    values = jnp.concatenate([values, jnp.ones((SPAN, HEAD_SIZE), BF16)], axis=1)
-                    return carry + jnp.dot(weights, values, preferred_element_type=F32)
-
-                mixed = lax.fori_loop(0, tiles, mix, jnp.zeros((tall, 2 * HEAD_SIZE), F32))
-                mixed = mixed[:, :HEAD_SIZE] / mixed[:, HEAD_SIZE:]
-                live = offset + iota((SPAN, HEAD_SIZE), 0) < length
-                for at in range(group):
-                    left = pl.multiple_of((head * group + at) * HEAD_SIZE, HEAD_SIZE)
-                    attended_ref[out_rows, pl.ds(left, HEAD_SIZE)] = jnp.where(
-                        live, mixed[at * SPAN : (at + 1) * SPAN], 0.0
-                    ).astype(BF16)
+                    scores = scores + bias
+                    scores_ref[head, tile] = scores
+                    top_ref[head] = jnp.maximum(top_ref[head], scores)
                 return carry
 
-            lax.fori_loop(0, key_heads, attend_head, 0)
+            lax.fori_loop(0, tiles, score, 0)
+            tops = [jnp.max(top_ref[head], axis=1, keepdims=True) for head in range(key_heads)]
+
+            def mix(tile, carry):
+                ones = jnp.ones((TILE, HEAD_SIZE), BF16)
+                totals = []
+                for head in range(key_heads):
+                    weights = jnp.exp2((scores_ref[head, tile] - tops[head]) * factor)
+                    values = rows_ref[tile_rows(tile), columns(query_width + key_width, head)]
+                    values = jnp.concatenate([values, ones], axis=1)
+                    totals.append(
+                        carry[head]
+                        + jnp.dot(weights.astype(BF16), values, preferred_element_type=F32)
+                    )
+                return tuple(totals)
+
+            empty = jnp.zeros((tall, 2 * HEAD_SIZE), F32)
+            mixed = lax.fori_loop(0, tiles, mix, (empty,) * key_heads)
+            live = offset + iota((SPAN, HEAD_SIZE), 0) < length
+            for head in range(heads):
+                at = head % group * SPAN
+                part = mixed[head // group][at : at + SPAN]
+                part = part[:, :HEAD_SIZE] / part[:, HEAD_SIZE:]
+                attended_ref[out_rows, columns(0, head)] = jnp.where(live, part, 0.0).astype(BF16)
+
             result(slot).start()
 
         return carry
@@ -525,10 +515,10 @@
         scratch_shapes=[
             pltpu.VMEM((slots, query_width), BF16),
             pltpu.VMEM((2, slots, key_width), BF16),
-            pltpu.VMEM((total + 2 * SPAN, width), BF16),
+            pltpu.VMEM((total + TILE + ALIGN, width), BF16),
             pltpu.VMEM((key_heads, tall, HEAD_SIZE), BF16),
-            pltpu.VMEM((slots // SPAN + 1, tall, SPAN), F32),
-            pltpu.VMEM((tall, SPAN), F32),
+            pltpu.VMEM((key_heads, slots // TILE + 1, tall, TILE), F32),
+            pltpu.VMEM((key_heads, tall, TILE), F32),
             pltpu.SemaphoreType.DMA((copies,)),
             pltpu.SemaphoreType.DMA((slots // SPAN + 1,)),
         ],
@@ -576,6 +566,9 @@
     late = [piece for piece in range(len(owned)) if depth[piece] == max(depth)]
     direct = [piece for piece in range(len(owned)) if depth[piece] == 1]
 
+    sources = {source + 1 for source, _ in routes} - {0}
+    awaited = [piece for piece in direct if piece in sources or owned[piece][0] >= 0]
+
     def relay(line):
         for index, (source, pairs) in enumerate(routes):
             if index + 1 not in direct:
@@ -584,7 +577,7 @@
     lines = []
     for chunk in range(len(sizes)):
         arrived = [shift_chips(aways[chunk][hop - 1], hop, chips) for hop in range(1, chips)]
-        places = [(chunk - 1, piece) for piece in direct if chunk]
+        places = [(chunk - 1, piece) for piece in awaited if chunk]
         places += [(chunk - 2, piece) for piece in late if chunk > 1]
         later = aways[chunk + 1 : chunk + 2] + [lines[at][piece] for at, piece in places]
         block, later = merge(homes[chunk], arrived, later)
@@ -611,9 +604,6 @@
     widths = w_query.shape[1], key_weight.shape[1]
     for chunks in GROUPS:
         if len(sizes) - 1 in chunks:
-            for source in {source + 1 for source, _ in routes} - {0}:
-                if depth[source] == 1:
-                    lines[-1][source] = after(lines[-1][source], blocks[:1])
             relay(lines[-1])
         span = [bases[chunk] for chunk in chunks], [sizes[chunk] for chunk in chunks]
         groups.append(span)

time: 140 us -> 130 us (0.929)
  Pallas kernels: 50.5 us -> 47.5 us
  waiting for transfers between devices: 50.2 us -> 47.6 us
  starting transfers between devices: 31 us -> 28.8 us
    ppermute x3, waiting for transfers between devices: 21.6 us -> 1.99 us  [relay(): line[index + 1] = lax.ppermute(line[source + 1], 'tp', pairs)]
    ppermute x9, waiting for transfers between devices: 19.6 us -> 34.5 us  [local(): line[index + 1] = lax.ppermute(block, 'tp', pairs)]
    pallas_call x2, Pallas kernels: 14.4 us -> 11.4 us  [attend(): pl.pallas_call(functools.partial(attend_kernel, chips, groups, known, pri...]
    ppermute x9, starting transfers between devices: 18.6 us -> 16.3 us  [local(): line[index + 1] = lax.ppermute(block, 'tp', pairs)]
    ppermute x5, waiting for transfers between devices: 8.91 us -> 11 us  [shift_chips(): return lax.ppermute(value, 'req', pairs)]
    unnamed x16 -> x14, local copies, waits for them, and re-layouts: 3.23 us -> 2.27 us
  transfers between devices with their start and end apart: 22 -> 22, of which waited for: 6 -> 10; matrix products, arithmetic and copies ran while one was open for 1% -> 1% of each run, Pallas kernels for 31% -> 32%
where the time goes in v1:
time: 130 us; the launch traced here: 128 us
  waiting for transfers between devices  47.6 us (37%)
  Pallas kernels  47.5 us (37%)
  starting transfers between devices  28.8 us (22%)
  local copies, waits for them, and re-layouts  3.04 us (2%)
    ppermute x9, waiting for transfers between devices, local(): line[index + 1] = lax.ppermute(block, 'tp', pairs)  34.5 us
    pallas_call x4, Pallas kernels, project(): pl.pallas_call(functools.partial(project_kernel, len(lines[0]), bool(carr...  28.9 us
    ppermute x9, starting transfers between devices, local(): line[index + 1] = lax.ppermute(block, 'tp', pairs)  16.3 us
    pallas_call x2, Pallas kernels, attend(): pl.pallas_call(functools.partial(attend_kernel, chips, groups, known, pri...  11.4 us
    ppermute x5, waiting for transfers between devices, shift_chips(): return lax.ppermute(value, 'req', pairs)  11 us
    ppermute x5, starting transfers between devices, shift_chips(): return lax.ppermute(value, 'req', pairs)  7.55 us
    pallas_call x3, Pallas kernels, deal(): pl.pallas_call(functools.partial(deal_kernel, chips, bases, sizes, twins)...  7.05 us
    ppermute x3, starting transfers between devices, relay(): line[index + 1] = lax.ppermute(line[source + 1], 'tp', pairs)  3.86 us
  transfers between devices with their start and end apart: 22, of which 10 were waited for; matrix products, arithmetic and copies ran while one was open for 1% of the time, Pallas kernels for 32%

profile of v1, /device:TPU:0, one launch (start us, length us, event | category | flops | bytes accessed | tf_op | source)
XLA Modules:
  0.0 127.8 jit_solution(2790892748204766360)
XLA Ops:
  0.6 0.5 collective-permute-start
  1.1 1.6 %copy-done = bf16[512,2048]{1,0:T(8,128)(2,1)S(1)} copy-done((bf16[512,2048]{1,0:T(8,128)(2,1)S(1)}, bf16[512,2048]{1,0:T(8,128)(2,1)}, u32[]{:S(2)}) %copy-start) | copy-done | bytes 2097176
  2.7 0.7 copy-done.2
  3.4 1.6 %deal.4 = (bf16[64,2048]{1,0:T(8,128)(2,1)S(1)}, bf16[1,64,2048]{2,1,0:T(8,128)(2,1)S(1)}) custom-call(s32[4]{0:T(128)S(1)} %copy-done.2, bf16[512,2048]{1,0:T(8,128)(2,1)S(1)} %copy-done), custom_call_target="tpu_custom_call" | custom-call | flops 268435456 | bytes 2621440 | tf_op jit(solution)/shard_map/deal/pallas_call | solution.py:79
  5.0 0.1 collective-permute-done.refs_1_.refs_0_
  5.1 1.7 %deal.5 = (bf16[64,2048]{1,0:T(8,128)(2,1)S(1)}, bf16[1,64,2048]{2,1,0:T(8,128)(2,1)S(1)}) custom-call(s32[4]{0:T(128)S(1)} %copy-done.2, bf16[512,2048]{1,0:T(8,128)(2,1)S(1)} %collective-permute-done.refs_1_.refs_0_, bf16[64,2048]{1,0:T(8,128)(2,1)S(1)} %get-tuple-element.28.refs_1_, bf16[1,64,2048]{2,1,0:T(8,128)(2,1)S(1)} %get-tuple-element.29.refs_2_), custom_call_target="tpu_custom_call" | custom-call | flops 268435456 | bytes 2621440 | tf_op jit(solution)/shard_map/deal/pallas_call | solution.py:79
  6.8 0.0 copy-start.6
  6.8 0.0 copy-start.3
  6.8 0.0 copy-start.4
  6.9 2.9 %collective-permute-start.1 = (bf16[64,2048]{1,0:T(8,128)(2,1)S(1)}, bf16[64,2048]{1,0:T(8,128)(2,1)S(1)}, u32[]{:S(2)}, u32[]{:S(2)}) collective-permute-start(bf16[64,2048]{1,0:T(8,128)(2,1)S(1)} %bitcast.14), channel_id=1, source_target_pairs={{0,8},{4,12},{8,0},{12,4},{1,9},{5,13},{9,1},{13,5},{2,10},{6,14},... | collective-permute-start | bytes 786440 | tf_op jit(solution)/shard_map/ppermute | solution.py:532
  9.8 0.0 copy-done.1
  9.8 3.7 %deal.3 = (bf16[96,2048]{1,0:T(8,128)(2,1)S(1)}, bf16[1,96,2048]{2,1,0:T(8,128)(2,1)S(1)}, bf16[96,2048]{1,0:T(8,128)(2,1)S(1)}, bf16[1,96,2048]{2,1,0:T(8,128)(2,1)S(1)}) custom-call(s32[4]{0:T(128)S(1)} %copy-done.2, bf16[512,2048]{1,0:T(8,128)(2,1)S(1)} %copy-done.1, bf16[512,2048]{1,0:T(8,128)(2,1)S(1)} %collective-permute-done.refs_1_.refs_0_), custom_call_target="tpu_custom_call" | custom-call | flops 1610612736 | bytes 5767168 | tf_op jit(solution)/shard_map/deal/pallas_call | solution.py:79
  13.5 2.9 %collective-permute-done.1.refs_0_ = bf16[64,2048]{1,0:T(8,128)(2,1)S(1)} collective-permute-done((bf16[64,2048]{1,0:T(8,128)(2,1)S(1)}, bf16[64,2048]{1,0:T(8,128)(2,1)S(1)}, u32[]{:S(2)}, u32[]{:S(2)}) %collective-permute-start.1) | collective-permute-done | bytes 262176 | tf_op jit(solution)/shard_map/ppermute | solution.py:532
  16.4 1.8 %collective-permute-start.2 = (bf16[96,2048]{1,0:T(8,128)(2,1)S(1)}, bf16[96,2048]{1,0:T(8,128)(2,1)S(1)}, u32[]{:S(2)}, u32[]{:S(2)}) collective-permute-start(bf16[96,2048]{1,0:T(8,128)(2,1)S(1)} %bitcast.12), channel_id=1, source_target_pairs={{0,8},{4,12},{8,0},{12,4},{1,9},{5,13},{9,1},{13,5},{2,10},{6,14},... | collective-permute-start | bytes 1179656 | tf_op jit(solution)/shard_map/ppermute | solution.py:532
  18.2 2.6 %collective-permute-start.4 = (bf16[64,2048]{1,0:T(8,128)(2,1)S(1)}, bf16[64,2048]{1,0:T(8,128)(2,1)S(1)}, u32[]{:S(2)}, u32[]{:S(2)}) collective-permute-start(bf16[64,2048]{1,0:T(8,128)(2,1)S(1)} %get-tuple-element.35.refs_0_), channel_id=1, source_target_pairs={{0,2},{1,3},{2,0},{3,1},{4,6},{5,7},{6,4},{7,5},{8,10},{9,11},{10,... | collective-permute-start | bytes 786440 | tf_op jit(solution)/shard_map/ppermute | solution.py:591
  20.8 1.6 %collective-permute-start.3 = (bf16[64,2048]{1,0:T(8,128)(2,1)S(1)}, bf16[64,2048]{1,0:T(8,128)(2,1)S(1)}, u32[]{:S(2)}, u32[]{:S(2)}) collective-permute-start(bf16[64,2048]{1,0:T(8,128)(2,1)S(1)} %get-tuple-element.35.refs_0_), channel_id=1, source_target_pairs={{0,1},{1,0},{2,3},{3,2},{4,5},{5,4},{6,7},{7,6},{8,9},{9,8},{10,11... | collective-permute-start | bytes 786440 | tf_op jit(solution)/shard_map/ppermute | solution.py:591
  22.4 9.7 %collective-permute-done.4.refs_3_ = bf16[64,2048]{1,0:T(8,128)(2,1)S(1)} collective-permute-done((bf16[64,2048]{1,0:T(8,128)(2,1)S(1)}, bf16[64,2048]{1,0:T(8,128)(2,1)S(1)}, u32[]{:S(2)}, u32[]{:S(2)}) %collective-permute-start.4) | collective-permute-done | bytes 262176 | tf_op jit(solution)/shard_map/ppermute | solution.py:591
  32.1 0.2 collective-permute-done.3.refs_2_
  32.3 0.0 collective-permute-done.2.refs_0_
  32.3 1.3 %collective-permute-start.8 = (bf16[64,2048]{1,0:T(8,128)(2,1)S(1)}, bf16[64,2048]{1,0:T(8,128)(2,1)S(1)}, u32[]{:S(2)}, u32[]{:S(2)}) collective-permute-start(bf16[64,2048]{1,0:T(8,128)(2,1)S(1)} %get-tuple-element.38.refs_3_), channel_id=1, source_target_pairs={{2,3},{1,0},{6,7},{5,4},{10,11},{9,8},{14,15},{13,12},{18,19},{17,... | collective-permute-start | bytes 786440 | tf_op jit(solution)/shard_map/ppermute | solution.py:575
  33.6 0.7 collective-permute-start.5
  34.3 4.3 %collective-permute-start.7 = (bf16[96,2048]{1,0:T(8,128)(2,1)S(1)}, bf16[96,2048]{1,0:T(8,128)(2,1)S(1)}, u32[]{:S(2)}, u32[]{:S(2)}) collective-permute-start(bf16[96,2048]{1,0:T(8,128)(2,1)S(1)} %get-tuple-element.37.refs_4_), channel_id=1, source_target_pairs={{0,2},{1,3},{2,0},{3,1},{4,6},{5,7},{6,4},{7,5},{8,10},{9,11},{10,... | collective-permute-start | bytes 1179656 | tf_op jit(solution)/shard_map/ppermute | solution.py:591
  38.6 0.0 collective-permute-start.6
  38.6 0.7 constant_dynamic-slice_fusion
  39.3 0.7 collective-permute-start.10
  40.0 2.0 %collective-permute-done.8.refs_3_ = bf16[64,2048]{1,0:T(8,128)(2,1)S(1)} collective-permute-done((bf16[64,2048]{1,0:T(8,128)(2,1)S(1)}, bf16[64,2048]{1,0:T(8,128)(2,1)S(1)}, u32[]{:S(2)}, u32[]{:S(2)}) %collective-permute-start.8) | collective-permute-done | bytes 262176 | tf_op jit(solution)/shard_map/ppermute | solution.py:575
  42.0 0.7 collective-permute-start.11
  42.7 0.7 collective-permute-done.5.refs_0_
  43.4 11.7 %collective-permute-done.7.refs_2_ = bf16[96,2048]{1,0:T(8,128)(2,1)S(1)} collective-permute-done((bf16[96,2048]{1,0:T(8,128)(2,1)S(1)}, bf16[96,2048]{1,0:T(8,128)(2,1)S(1)}, u32[]{:S(2)}, u32[]{:S(2)}) %collective-permute-start.7) | collective-permute-done | bytes 393248 | tf_op jit(solution)/shard_map/ppermute | solution.py:591
  55.1 2.9 %collective-permute-done.6.refs_1_ = bf16[96,2048]{1,0:T(8,128)(2,1)S(1)} collective-permute-done((bf16[96,2048]{1,0:T(8,128)(2,1)S(1)}, bf16[96,2048]{1,0:T(8,128)(2,1)S(1)}, u32[]{:S(2)}, u32[]{:S(2)}) %collective-permute-start.6) | collective-permute-done | bytes 393248 | tf_op jit(solution)/shard_map/ppermute | solution.py:591
  58.0 1.3 %collective-permute-start.9 = (bf16[96,2048]{1,0:T(8,128)(2,1)S(1)}, bf16[96,2048]{1,0:T(8,128)(2,1)S(1)}, u32[]{:S(2)}, u32[]{:S(2)}) collective-permute-start(bf16[96,2048]{1,0:T(8,128)(2,1)S(1)} %get-tuple-element.40.refs_7_), channel_id=1, source_target_pairs={{2,3},{1,0},{6,7},{5,4},{10,11},{9,8},{14,15},{13,12},{18,19},{17,... | collective-permute-start | bytes 1179656 | tf_op jit(solution)/shard_map/ppermute | solution.py:575
  59.3 5.8 %collective-permute-start.15 = (bf16[96,2048]{1,0:T(8,128)(2,1)S(1)}, bf16[96,2048]{1,0:T(8,128)(2,1)S(1)}, u32[]{:S(2)}, u32[]{:S(2)}) collective-permute-start(bf16[96,2048]{1,0:T(8,128)(2,1)S(1)} %get-tuple-element.45.refs_0_), channel_id=1, source_target_pairs={{0,2},{1,3},{2,0},{3,1},{4,6},{5,7},{6,4},{7,5},{8,10},{9,11},{10,... | collective-permute-start | bytes 1179656 | tf_op jit(solution)/shard_map/ppermute | solution.py:591
  65.1 0.1 slice_bitcast_fusion.1.place_ref
  65.2 0.0 collective-permute-start.18
  65.2 0.0 collective-permute-done.10.refs_1_
  65.2 0.7 collective-permute-start.17
  65.9 0.0 collective-permute-done.11.refs_5_
  65.9 0.0 copy-done.3
  66.0 0.0 copy-done.4
  66.0 10.0 %project.4 = (f32[160,1536]{1,0:T(8,128)S(1)}, f32[160,128]{1,0:T(8,128)S(1)}) custom-call(s32[8]{0:T(128)S(1)} %slice_bitcast_fusion.place_ref, s32[4]{0:T(128)S(1)} %copy-done.3, bf16[64,2048]{1,0:T(8,128)(2,1)S(1)} %get-tuple-element.35.refs_0_, bf16[64,2048]{1,0:T(8,128)(2,1)S(1)} %collective-permute-done.10.refs_1_, ...), custom_call_target="tpu_custom_call" | custom-call | flops 4026531840 | bytes 27131904 | tf_op jit(solution)/shard_map/project/pallas_call | solution.py:279
  76.0 10.0 %collective-permute-done.15.refs_3_ = bf16[96,2048]{1,0:T(8,128)(2,1)S(1)} collective-permute-done((bf16[96,2048]{1,0:T(8,128)(2,1)S(1)}, bf16[96,2048]{1,0:T(8,128)(2,1)S(1)}, u32[]{:S(2)}, u32[]{:S(2)}) %collective-permute-start.15) | collective-permute-done | bytes 393248 | tf_op jit(solution)/shard_map/ppermute | solution.py:591
  86.0 1.3 %collective-permute-start.16 = (bf16[96,2048]{1,0:T(8,128)(2,1)S(1)}, bf16[96,2048]{1,0:T(8,128)(2,1)S(1)}, u32[]{:S(2)}, u32[]{:S(2)}) collective-permute-start(bf16[96,2048]{1,0:T(8,128)(2,1)S(1)} %collective-permute-done.15.refs_3_), channel_id=1, source_target_pairs={{2,3},{1,0},{6,7},{5,4},{10,11},{9,8},{14,15},{13,12},{18,19},{17,... | collective-permute-start | bytes 1179656 | tf_op jit(solution)/shard_map/ppermute | solution.py:575
  87.3 0.0 collective-permute-done.9.refs_1_
  87.3 4.7 %project.5.refs_0_ = bf16[160,1536]{1,0:T(8,128)(2,1)S(1)} custom-call(s32[2]{0:T(128)S(1)} %slice_bitcast_fusion.1.place_ref, s32[4]{0:T(128)S(1)} %copy-done.3, bf16[64,2048]{1,0:T(8,128)(2,1)S(1)} %get-tuple-element.39.refs_0_, bf16[96,2048]{1,0:T(8,128)(2,1)S(1)} %collective-permute-done.9.refs_1_, f32[1,8192]{1,0:T(1,128)S(1)} %bitcast.9, ...), custom_call_target="tpu_custom_call" | custom-call | flops 1006632960 | bytes 8257536 | tf_op jit(solution)/shard_map/project/pallas_call | solution.py:279
  92.0 1.4 %collective-permute-start.13 = (bf16[160,1536]{1,0:T(8,128)(2,1)S(1)}, bf16[160,1536]{1,0:T(8,128)(2,1)S(1)}, u32[]{:S(2)}, u32[]{:S(2)}) collective-permute-start(bf16[160,1536]{1,0:T(8,128)(2,1)S(1)} %project.5.refs_0_), channel_id=1, source_target_pairs={{0,8},{4,12},{8,0},{12,4},{1,9},{5,13},{9,1},{13,5},{2,10},{6,14},... | collective-permute-start | bytes 1474568 | tf_op jit(solution)/shard_map/ppermute | solution.py:532
  93.5 0.0 collective-permute-done.18.refs_2_
  93.5 0.0 collective-permute-done.17.refs_1_
  93.5 9.8 %project.6 = (f32[96,1536]{1,0:T(8,128)S(1)}, f32[96,128]{1,0:T(8,128)S(1)}) custom-call(s32[8]{0:T(128)S(1)} %slice_bitcast_fusion.place_ref, s32[4]{0:T(128)S(1)} %copy-done.3, bf16[96,2048]{1,0:T(8,128)(2,1)S(1)} %get-tuple-element.45.refs_0_, bf16[96,2048]{1,0:T(8,128)(2,1)S(1)} %collective-permute-done.17.refs_1_, ...), custom_call_target="tpu_custom_call" | custom-call | flops 2415919104 | bytes 26345472 | tf_op jit(solution)/shard_map/project/pallas_call | solution.py:279
  103.3 0.0 collective-permute-done.16.refs_0_
  103.3 0.0 copy-start.5
  103.3 4.4 %project.7.refs_4_ = bf16[96,1536]{1,0:T(8,128)(2,1)S(1)} custom-call(s32[2]{0:T(128)S(1)} %slice_bitcast_fusion.1.place_ref, s32[4]{0:T(128)S(1)} %copy-done.3, bf16[96,2048]{1,0:T(8,128)(2,1)S(1)} %collective-permute-done.16.refs_0_, f32[1,8192]{1,0:T(1,128)S(1)} %bitcast.11, bf16[8192,1024]{1,0:T(8,128)(2,1)} %refs_2_.1, bf16[8192,256]{1,0:T(8,128)(2,1)} %refs_3_.3, ...), custom_call_target="tpu_custom_call" | custom-call | flops 603979776 | bytes 7471104 | tf_op jit(solution)/shard_map/project/pallas_call | solution.py:279
  107.7 0.7 collective-permute-start.20
  108.4 0.0 collective-permute-start.12
  108.5 0.0 collective-permute-done.13.refs_2_
  108.5 0.5 collective-permute-start.14
  109.0 0.0 collective-permute-start.19
  109.0 7.4 %collective-permute-done.20.refs_6_ = bf16[96,1536]{1,0:T(8,128)(2,1)S(1)} collective-permute-done((bf16[96,1536]{1,0:T(8,128)(2,1)S(1)}, bf16[96,1536]{1,0:T(8,128)(2,1)S(1)}, u32[]{:S(2)}, u32[]{:S(2)}) %collective-permute-start.20) | collective-permute-done | bytes 294944 | tf_op jit(solution)/shard_map/ppermute | solution.py:532
  116.4 0.0 collective-permute-start.21
  116.4 0.0 collective-permute-done.12.refs_1_
  116.4 0.0 collective-permute-done.14.refs_3_
  116.4 6.2 %attend.2 = (bf16[512,1024]{1,0:T(8,128)(2,1)}, bf16[2,512,256]{2,1,0:T(8,128)(2,1)}) custom-call(s32[4]{0:T(128)S(1)} %copy-done.3, s32[16]{0:T(128)S(1)} %copy-done.5, bf16[160,1536]{1,0:T(8,128)(2,1)S(1)} %project.5.refs_0_, bf16[160,1536]{1,0:T(8,128)(2,1)S(1)} %collective-permute-done.12.refs_1_, bf16[160,1536]{1,0:T(8,128)(2,1)S(1)} %collective-permute-done.13.refs_2_, ...), custom_call_target="tpu_custom_call" | custom-call | tf_op jit(solution)/shard_map/attend/pallas_call | solution.py:505
  122.5 0.0 collective-permute-done.19.refs_5_
  122.6 0.0 collective-permute-done.21.refs_7_
  122.6 5.3 %attend.3 = (bf16[512,1024]{1,0:T(8,128)(2,1)}, bf16[2,512,256]{2,1,0:T(8,128)(2,1)}) custom-call(s32[4]{0:T(128)S(1)} %copy-done.3, s32[16]{0:T(128)S(1)} %copy-done.5, bf16[160,1536]{1,0:T(8,128)(2,1)S(1)} %project.5.refs_0_, bf16[160,1536]{1,0:T(8,128)(2,1)S(1)} %collective-permute-done.12.refs_1_, ...), custom_call_target="tpu_custom_call", output_to_operand_aliasing={{0}: (10, {}), {1}: (11, {})} | custom-call | tf_op jit(solution)/shard_map/attend/pallas_call | solution.py:505
  (10 shorter events, 0.1 us)
Async XLA Ops:
  0.6 4.5 %collective-permute-start = (bf16[512,2048]{1,0:T(8,128)(2,1)}, bf16[512,2048]{1,0:T(8,128)(2,1)S(1)}, u32[]{:S(2)}, u32[]{:S(2)}) collective-permute-start(bf16[512,2048]{1,0:T(8,128)(2,1)} %refs_0_.3), channel_id=1, source_target_pairs={{0,4},{4,0},{8,12},{12,8},{1,5},{5,1},{9,13},{13,9},{2,6},{6,2},{1... | collective-permute-start | bytes 6291464 | tf_op jit(solution)/shard_map/ppermute | solution.py:536
  1.1 1.6 %copy-start = (bf16[512,2048]{1,0:T(8,128)(2,1)S(1)}, bf16[512,2048]{1,0:T(8,128)(2,1)}, u32[]{:S(2)}) copy-start(bf16[512,2048]{1,0:T(8,128)(2,1)} %refs_0_.3) | copy-start | bytes 6291460
  2.7 0.7 copy-start.2
  3.4 6.4 %copy-start.1 = (bf16[512,2048]{1,0:T(8,128)(2,1)S(1)}, bf16[512,2048]{1,0:T(8,128)(2,1)}, u32[]{:S(2)}) copy-start(bf16[512,2048]{1,0:T(8,128)(2,1)} %refs_0_.3) | copy-start | bytes 6291460
  6.8 58.4 %copy-start.6 = (bf16[8192]{0:T(1024)(128)(2,1)S(1)}, bf16[8192]{0:T(1024)(128)(2,1)}, u32[]{:S(2)}) copy-start(bf16[8192]{0:T(1024)(128)(2,1)} %param.10) | copy-start | bytes 49156
  6.8 59.1 %copy-start.3 = (s32[4]{0:T(128)S(1)}, s32[4]{0:T(128)}, u32[]{:S(2)}) copy-start(s32[4]{0:T(128)} %lengths_ref.17) | copy-start | bytes 52
  6.8 59.1 %copy-start.4 = (f32[1,128]{1,0:T(1,128)S(1)}, f32[1,128]{1,0:T(1,128)}, u32[]{:S(2)}) copy-start(f32[1,128]{1,0:T(1,128)} %constant.14.clone.refs_12_.refs_8_.refs_7_) | copy-start | bytes 1540
  6.9 9.5 %collective-permute-start.1 = (bf16[64,2048]{1,0:T(8,128)(2,1)S(1)}, bf16[64,2048]{1,0:T(8,128)(2,1)S(1)}, u32[]{:S(2)}, u32[]{:S(2)}) collective-permute-start(bf16[64,2048]{1,0:T(8,128)(2,1)S(1)} %bitcast.14), channel_id=1, source_target_pairs={{0,8},{4,12},{8,0},{12,4},{1,9},{5,13},{9,1},{13,5},{2,10},{6,14},... | collective-permute-start | bytes 786440 | tf_op jit(solution)/shard_map/ppermute | solution.py:532
  16.4 15.9 %collective-permute-start.2 = (bf16[96,2048]{1,0:T(8,128)(2,1)S(1)}, bf16[96,2048]{1,0:T(8,128)(2,1)S(1)}, u32[]{:S(2)}, u32[]{:S(2)}) collective-permute-start(bf16[96,2048]{1,0:T(8,128)(2,1)S(1)} %bitcast.12), channel_id=1, source_target_pairs={{0,8},{4,12},{8,0},{12,4},{1,9},{5,13},{9,1},{13,5},{2,10},{6,14},... | collective-permute-start | bytes 1179656 | tf_op jit(solution)/shard_map/ppermute | solution.py:532
  18.2 13.9 %collective-permute-start.4 = (bf16[64,2048]{1,0:T(8,128)(2,1)S(1)}, bf16[64,2048]{1,0:T(8,128)(2,1)S(1)}, u32[]{:S(2)}, u32[]{:S(2)}) collective-permute-start(bf16[64,2048]{1,0:T(8,128)(2,1)S(1)} %get-tuple-element.35.refs_0_), channel_id=1, source_target_pairs={{0,2},{1,3},{2,0},{3,1},{4,6},{5,7},{6,4},{7,5},{8,10},{9,11},{10,... | collective-permute-start | bytes 786440 | tf_op jit(solution)/shard_map/ppermute | solution.py:591
  20.8 11.5 %collective-permute-start.3 = (bf16[64,2048]{1,0:T(8,128)(2,1)S(1)}, bf16[64,2048]{1,0:T(8,128)(2,1)S(1)}, u32[]{:S(2)}, u32[]{:S(2)}) collective-permute-start(bf16[64,2048]{1,0:T(8,128)(2,1)S(1)} %get-tuple-element.35.refs_0_), channel_id=1, source_target_pairs={{0,1},{1,0},{2,3},{3,2},{4,5},{5,4},{6,7},{7,6},{8,9},{9,8},{10,11... | collective-permute-start | bytes 786440 | tf_op jit(solution)/shard_map/ppermute | solution.py:591
  32.3 9.6 %collective-permute-start.8 = (bf16[64,2048]{1,0:T(8,128)(2,1)S(1)}, bf16[64,2048]{1,0:T(8,128)(2,1)S(1)}, u32[]{:S(2)}, u32[]{:S(2)}) collective-permute-start(bf16[64,2048]{1,0:T(8,128)(2,1)S(1)} %get-tuple-element.38.refs_3_), channel_id=1, source_target_pairs={{2,3},{1,0},{6,7},{5,4},{10,11},{9,8},{14,15},{13,12},{18,19},{17,... | collective-permute-start | bytes 786440 | tf_op jit(solution)/shard_map/ppermute | solution.py:575
  33.6 9.8 %collective-permute-start.5 = (bf16[96,2048]{1,0:T(8,128)(2,1)S(1)}, bf16[96,2048]{1,0:T(8,128)(2,1)S(1)}, u32[]{:S(2)}, u32[]{:S(2)}) collective-permute-start(bf16[96,2048]{1,0:T(8,128)(2,1)S(1)} %bitcast.13), channel_id=1, source_target_pairs={{0,8},{4,12},{8,0},{12,4},{1,9},{5,13},{9,1},{13,5},{2,10},{6,14},... | collective-permute-start | bytes 1179656 | tf_op jit(solution)/shard_map/ppermute | solution.py:532
  34.3 20.8 %collective-permute-start.7 = (bf16[96,2048]{1,0:T(8,128)(2,1)S(1)}, bf16[96,2048]{1,0:T(8,128)(2,1)S(1)}, u32[]{:S(2)}, u32[]{:S(2)}) collective-permute-start(bf16[96,2048]{1,0:T(8,128)(2,1)S(1)} %get-tuple-element.37.refs_4_), channel_id=1, source_target_pairs={{0,2},{1,3},{2,0},{3,1},{4,6},{5,7},{6,4},{7,5},{8,10},{9,11},{10,... | collective-permute-start | bytes 1179656 | tf_op jit(solution)/shard_map/ppermute | solution.py:591
  38.6 19.4 %collective-permute-start.6 = (bf16[96,2048]{1,0:T(8,128)(2,1)S(1)}, bf16[96,2048]{1,0:T(8,128)(2,1)S(1)}, u32[]{:S(2)}, u32[]{:S(2)}) collective-permute-start(bf16[96,2048]{1,0:T(8,128)(2,1)S(1)} %get-tuple-element.37.refs_4_), channel_id=1, source_target_pairs={{0,1},{1,0},{2,3},{3,2},{4,5},{5,4},{6,7},{7,6},{8,9},{9,8},{10,11... | collective-permute-start | bytes 1179656 | tf_op jit(solution)/shard_map/ppermute | solution.py:591
  39.3 25.9 %collective-permute-start.10 = (bf16[64,2048]{1,0:T(8,128)(2,1)S(1)}, bf16[64,2048]{1,0:T(8,128)(2,1)S(1)}, u32[]{:S(2)}, u32[]{:S(2)}) collective-permute-start(bf16[64,2048]{1,0:T(8,128)(2,1)S(1)} %get-tuple-element.35.refs_0_), channel_id=1, source_target_pairs={{1,2},{2,1},{5,6},{6,5},{9,10},{10,9},{13,14},{14,13},{17,18},{18,... | collective-permute-start | bytes 786440 | tf_op jit(solution)/shard_map/ppermute | solution.py:591
  42.0 24.0 %collective-permute-start.11 = (bf16[96,2048]{1,0:T(8,128)(2,1)S(1)}, bf16[96,2048]{1,0:T(8,128)(2,1)S(1)}, u32[]{:S(2)}, u32[]{:S(2)}) collective-permute-start(bf16[96,2048]{1,0:T(8,128)(2,1)S(1)} %get-tuple-element.37.refs_4_), channel_id=1, source_target_pairs={{1,2},{2,1},{5,6},{6,5},{9,10},{10,9},{13,14},{14,13},{17,18},{18,... | collective-permute-start | bytes 1179656 | tf_op jit(solution)/shard_map/ppermute | solution.py:591
  58.0 29.3 %collective-permute-start.9 = (bf16[96,2048]{1,0:T(8,128)(2,1)S(1)}, bf16[96,2048]{1,0:T(8,128)(2,1)S(1)}, u32[]{:S(2)}, u32[]{:S(2)}) collective-permute-start(bf16[96,2048]{1,0:T(8,128)(2,1)S(1)} %get-tuple-element.40.refs_7_), channel_id=1, source_target_pairs={{2,3},{1,0},{6,7},{5,4},{10,11},{9,8},{14,15},{13,12},{18,19},{17,... | collective-permute-start | bytes 1179656 | tf_op jit(solution)/shard_map/ppermute | solution.py:575
  59.3 26.7 %collective-permute-start.15 = (bf16[96,2048]{1,0:T(8,128)(2,1)S(1)}, bf16[96,2048]{1,0:T(8,128)(2,1)S(1)}, u32[]{:S(2)}, u32[]{:S(2)}) collective-permute-start(bf16[96,2048]{1,0:T(8,128)(2,1)S(1)} %get-tuple-element.45.refs_0_), channel_id=1, source_target_pairs={{0,2},{1,3},{2,0},{3,1},{4,6},{5,7},{6,4},{7,5},{8,10},{9,11},{10,... | collective-permute-start | bytes 1179656 | tf_op jit(solution)/shard_map/ppermute | solution.py:591
  65.2 28.3 %collective-permute-start.18 = (bf16[96,2048]{1,0:T(8,128)(2,1)S(1)}, bf16[96,2048]{1,0:T(8,128)(2,1)S(1)}, u32[]{:S(2)}, u32[]{:S(2)}) collective-permute-start(bf16[96,2048]{1,0:T(8,128)(2,1)S(1)} %get-tuple-element.45.refs_0_), channel_id=1, source_target_pairs={{0,1},{1,0},{2,3},{3,2},{4,5},{5,4},{6,7},{7,6},{8,9},{9,8},{10,11... | collective-permute-start | bytes 1179656 | tf_op jit(solution)/shard_map/ppermute | solution.py:591
  65.2 28.2 %collective-permute-start.17 = (bf16[96,2048]{1,0:T(8,128)(2,1)S(1)}, bf16[96,2048]{1,0:T(8,128)(2,1)S(1)}, u32[]{:S(2)}, u32[]{:S(2)}) collective-permute-start(bf16[96,2048]{1,0:T(8,128)(2,1)S(1)} %get-tuple-element.45.refs_0_), channel_id=1, source_target_pairs={{1,2},{2,1},{5,6},{6,5},{9,10},{10,9},{13,14},{14,13},{17,18},{18,... | collective-permute-start | bytes 1179656 | tf_op jit(solution)/shard_map/ppermute | solution.py:591
  86.0 17.3 %collective-permute-start.16 = (bf16[96,2048]{1,0:T(8,128)(2,1)S(1)}, bf16[96,2048]{1,0:T(8,128)(2,1)S(1)}, u32[]{:S(2)}, u32[]{:S(2)}) collective-permute-start(bf16[96,2048]{1,0:T(8,128)(2,1)S(1)} %collective-permute-done.15.refs_3_), channel_id=1, source_target_pairs={{2,3},{1,0},{6,7},{5,4},{10,11},{9,8},{14,15},{13,12},{18,19},{17,... | collective-permute-start | bytes 1179656 | tf_op jit(solution)/shard_map/ppermute | solution.py:575
  92.0 16.4 %collective-permute-start.13 = (bf16[160,1536]{1,0:T(8,128)(2,1)S(1)}, bf16[160,1536]{1,0:T(8,128)(2,1)S(1)}, u32[]{:S(2)}, u32[]{:S(2)}) collective-permute-start(bf16[160,1536]{1,0:T(8,128)(2,1)S(1)} %project.5.refs_0_), channel_id=1, source_target_pairs={{0,8},{4,12},{8,0},{12,4},{1,9},{5,13},{9,1},{13,5},{2,10},{6,14},... | collective-permute-start | bytes 1474568 | tf_op jit(solution)/shard_map/ppermute | solution.py:532
  103.3 13.1 %copy-start.5 = (s32[16]{0:T(128)S(1)}, s32[16]{0:T(128)}, u32[]{:S(2)}) copy-start(s32[16]{0:T(128)} %plan_ref.3) | copy-start | bytes 196
  107.7 8.6 %collective-permute-start.20 = (bf16[96,1536]{1,0:T(8,128)(2,1)S(1)}, bf16[96,1536]{1,0:T(8,128)(2,1)S(1)}, u32[]{:S(2)}, u32[]{:S(2)}) collective-permute-start(bf16[96,1536]{1,0:T(8,128)(2,1)S(1)} %project.7.refs_4_), channel_id=1, source_target_pairs={{0,8},{4,12},{8,0},{12,4},{1,9},{5,13},{9,1},{13,5},{2,10},{6,14},... | collective-permute-start | bytes 884744 | tf_op jit(solution)/shard_map/ppermute | solution.py:532
  108.4 7.9 %collective-permute-start.12 = (bf16[160,1536]{1,0:T(8,128)(2,1)S(1)}, bf16[160,1536]{1,0:T(8,128)(2,1)S(1)}, u32[]{:S(2)}, u32[]{:S(2)}) collective-permute-start(bf16[160,1536]{1,0:T(8,128)(2,1)S(1)} %project.5.refs_0_), channel_id=1, source_target_pairs={{0,4},{4,0},{8,12},{12,8},{1,5},{5,1},{9,13},{13,9},{2,6},{6,2},{1... | collective-permute-start | bytes 1474568 | tf_op jit(solution)/shard_map/ppermute | solution.py:536
  108.5 7.9 %collective-permute-start.14 = (bf16[160,1536]{1,0:T(8,128)(2,1)S(1)}, bf16[160,1536]{1,0:T(8,128)(2,1)S(1)}, u32[]{:S(2)}, u32[]{:S(2)}) collective-permute-start(bf16[160,1536]{1,0:T(8,128)(2,1)S(1)} %collective-permute-done.13.refs_2_), channel_id=1, source_target_pairs={{0,4},{4,0},{8,12},{12,8},{1,5},{5,1},{9,13},{13,9},{2,6},{6,2},{1... | collective-permute-start | bytes 1474568 | tf_op jit(solution)/shard_map/ppermute | solution.py:536
  109.0 13.6 %collective-permute-start.19 = (bf16[96,1536]{1,0:T(8,128)(2,1)S(1)}, bf16[96,1536]{1,0:T(8,128)(2,1)S(1)}, u32[]{:S(2)}, u32[]{:S(2)}) collective-permute-start(bf16[96,1536]{1,0:T(8,128)(2,1)S(1)} %project.7.refs_4_), channel_id=1, source_target_pairs={{0,4},{4,0},{8,12},{12,8},{1,5},{5,1},{9,13},{13,9},{2,6},{6,2},{1... | collective-permute-start | bytes 884744 | tf_op jit(solution)/shard_map/ppermute | solution.py:536
  116.4 6.2 %collective-permute-start.21 = (bf16[96,1536]{1,0:T(8,128)(2,1)S(1)}, bf16[96,1536]{1,0:T(8,128)(2,1)S(1)}, u32[]{:S(2)}, u32[]{:S(2)}) collective-permute-start(bf16[96,1536]{1,0:T(8,128)(2,1)S(1)} %collective-permute-done.20.refs_6_), channel_id=1, source_target_pairs={{0,4},{4,0},{8,12},{12,8},{1,5},{5,1},{9,13},{13,9},{2,6},{6,2},{1... | collective-permute-start | bytes 884744 | tf_op jit(solution)/shard_map/ppermute | solution.py:536

commit v2 on v1

--- a/solution.py
+++ b/solution.py
@@ -13,8 +13,7 @@
 SPAN = 128
 ALIGN = 16
 TILE = 2 * SPAN
-SHARES = (4, 6, 6)
-GROUPS = ((0, 1), (2,))
+SHARES = (4, 8, 4)
 DEPTH = 1024
 MEBI = 1024 * 1024
 F32, BF16 = jnp.float32, jnp.bfloat16
@@ -85,39 +84,46 @@
         out_specs=out_specs,
         out_shape=out_shape,
         compiler_params=pltpu.CompilerParams(vmem_limit_bytes=24 * MEBI),
-        cost_estimate=pl.CostEstimate(
-            flops=2 * len(sources) * chips * sum(sizes) * slots * width,
-            bytes_accessed=2 * len(sources) * slots * width + 2 * chips * sum(sizes) * width,
-            transcendentals=0,
-        ),
         name="deal",
     )(lengths, *sources, *priors)
 
 
-def merge_kernel(count, home_ref, *refs):
+def merge_kernel(count, passed, home_ref, *refs):
     total = home_ref[...]
     for ref in refs[:count]:
         total = total + ref[...]
-    passed = (len(refs) - count - 1) // 2
-    refs[count + passed][...] = total
-
-
-def merge(home, arrived, later):
+    refs[len(refs) - 1 - passed][...] = total
+
+
+def merge(home, arrived, later, anchors):
     count = len(arrived)
     vmem, anywhere = pl.BlockSpec(memory_space=pltpu.VMEM), pl.BlockSpec(memory_space=pl.ANY)
     block, *later = pl.pallas_call(
-        functools.partial(merge_kernel, count),
-        in_specs=[vmem] * (count + 1) + [anywhere] * len(later),
+        functools.partial(merge_kernel, count, len(later)),
+        in_specs=[vmem] * (count + 1) + [anywhere] * (len(later) + len(anchors)),
         out_specs=[vmem] + [anywhere] * len(later),
         out_shape=[jax.ShapeDtypeStruct(leaf.shape, leaf.dtype) for leaf in (home, *later)],
         input_output_aliases={count + 1 + at: 1 + at for at in range(len(later))},
         compiler_params=pltpu.CompilerParams(vmem_limit_bytes=8 * MEBI),
-        cost_estimate=pl.CostEstimate(
-            flops=home.size, bytes_accessed=2 * home.size * (count + 2), transcendentals=0
-        ),
         name="merge",
-    )(home, *arrived, *later)
+    )(home, *arrived, *later, *anchors)
     return block, later
+
+
+def after(arrays, anchors):
+    def kernel(*refs):
+        pass
+
+    anywhere = pl.BlockSpec(memory_space=pl.ANY)
+    return pl.pallas_call(
+        kernel,
+        in_specs=[anywhere] * (len(arrays) + len(anchors)),
+        out_specs=[anywhere] * len(arrays),
+        out_shape=[jax.ShapeDtypeStruct(leaf.shape, leaf.dtype) for leaf in arrays],
+        input_output_aliases={at: at for at in range(len(arrays))},
+        compiler_params=pltpu.CompilerParams(vmem_limit_bytes=MEBI),
+        name="after",
+    )(*arrays, *anchors)
 
 
 def routes_of(shards):
@@ -159,18 +165,57 @@
     return np.array(table, np.int32), count
 
 
+def angles_kernel(groups, members, lengths_ref, frequency_ref, anchor_ref, *out_refs):
+    me = lax.axis_index("req")
+    for group, (bases, sizes) in enumerate(groups):
+        first = 0
+        for base, rows in zip(bases, sizes):
+            number = base + me * rows + iota((rows, HEAD_SIZE), 0)
+            start = jnp.zeros((rows, HEAD_SIZE), jnp.int32)
+            before = jnp.int32(0)
+            for other in range(members):
+                before = before + lengths_ref[other]
+                start = jnp.where(number >= before, before, start)
+            angle = (number - start).astype(F32) * frequency_ref[...]
+            sine = jnp.sin(angle)
+            lower = iota((rows, HEAD_SIZE), 1) < HEAD_SIZE // 2
+            out_refs[2 * group][first : first + rows, :] = jnp.cos(angle)
+            out_refs[2 * group + 1][first : first + rows, :] = jnp.where(lower, -sine, sine)
+            first += rows
+
+
+def angles(groups, lengths, frequency, anchor):
+    shapes = [
+        jax.ShapeDtypeStruct((sum(sizes), HEAD_SIZE), F32) for _, sizes in groups for _ in range(2)
+    ]
+    vmem = pl.BlockSpec(memory_space=pltpu.VMEM)
+    tables = pl.pallas_call(
+        functools.partial(angles_kernel, groups, lengths.shape[0]),
+        in_specs=[
+            pl.BlockSpec(memory_space=pltpu.SMEM),
+            vmem,
+            pl.BlockSpec(memory_space=pl.ANY),
+        ],
+        out_specs=[vmem] * len(shapes),
+        out_shape=shapes,
+        compiler_params=pltpu.CompilerParams(vmem_limit_bytes=8 * MEBI),
+        name="angles",
+    )(lengths, frequency, anchor)
+    return [tables[at : at + 2] for at in range(0, len(tables), 2)]
+
+
 def project_kernel(
-    count, carries, final, shards, steps, bases, sizes, members, place_ref, lengths_ref, *refs
+    count, carries, final, shards, steps, sizes, anchored, place_ref, *refs
 ):
+    refs = refs[anchored:]
     pieces, refs = refs[: count * len(sizes)], refs[count * len(sizes) :]
     gain_ref, query_ref, key_ref, value_ref = refs[:4]
     refs = refs[4:]
     if carries:
         sums_in, squares_in = refs[:2]
         refs = refs[2:]
-    frequency_ref, refs = refs[0], refs[1:]
     if final:
-        out_ref, refs = refs[0], refs[1:]
+        cosine_ref, sine_ref, out_ref, *refs = refs
     sums, squares, chosen = refs
     visit, step = pl.program_id(0), pl.program_id(1)
     visits = pl.num_programs(0)
@@ -211,22 +256,6 @@
 
         @pl.when((visit == visits - 1) & (step == steps - 1))
         def _():
-            me = lax.axis_index("req")
-            number = jnp.concatenate(
-                [
-                    base + me * size + iota((size, HEAD_SIZE), 0)
-                    for base, size in zip(bases, sizes)
-                ],
-                axis=0,
-            )
-            start = jnp.zeros((rows, HEAD_SIZE), jnp.int32)
-            before = jnp.int32(0)
-            for other in range(members):
-                before = before + lengths_ref[other]
-                start = jnp.where(number >= before, before, start)
-            angle = (number - start).astype(F32) * frequency_ref[...]
-            cosine, sine = jnp.cos(angle), jnp.sin(angle)
-            sine = jnp.where(iota((rows, HEAD_SIZE), 1) < HEAD_SIZE // 2, -sine, sine)
             mean = jnp.sum(squares[...], axis=1, keepdims=True) / (shards * steps * depth)
             scale = lax.rsqrt(mean + 1e-05)
             turned = query_ref.shape[1] + key_ref.shape[1]
@@ -234,12 +263,14 @@
                 columns = slice(at, at + HEAD_SIZE)
                 head = sums[:, columns] * scale
                 if at < turned:
-                    head = head * cosine + pltpu.roll(head, HEAD_SIZE // 2, 1) * sine
+                    head = head * cosine_ref[...] + pltpu.roll(
+                        head, HEAD_SIZE // 2, 1
+                    ) * sine_ref[...]
                 out_ref[:, columns] = head.astype(BF16)
 
 
 def project(
-    final, shards, bases, sizes, place, visits, lengths, lines, gain, weights, carried, frequency
+    final, shards, sizes, place, visits, lines, gain, weights, carried, tables, anchors
 ):
     pieces = [piece for line in lines for piece in line]
     rows, width = sum(sizes), pieces[0].shape[1]
@@ -252,21 +283,22 @@
         return place_ref[visits + visit] * steps + step
 
     def whole(shape):
-        return pl.BlockSpec(shape, lambda visit, step, place_ref, lengths_ref: (0, 0))
+        return pl.BlockSpec(shape, lambda visit, step, place_ref: (0, 0))
 
     def deep(block, dimension):
-        def where(visit, step, place_ref, lengths_ref):
+        def where(visit, step, place_ref):
             at = block_of(visit, step, place_ref)
             return (at, 0) if dimension == 0 else (0, at)
 
         return pl.BlockSpec(block, where)
 
-    operands = [*pieces, gain, *weights, *carried, frequency]
-    in_specs = [whole(piece.shape) for piece in pieces]
+    extra = [*carried, *tables] if final else carried
+    operands = [*anchors, *pieces, gain, *weights, *extra]
+    in_specs = [pl.BlockSpec(memory_space=pl.ANY)] * len(anchors)
+    in_specs += [whole(piece.shape) for piece in pieces]
     in_specs += [deep((1, depth), 1)]
     in_specs += [deep((depth, weight.shape[1]), 0) for weight in weights]
-    in_specs += [whole(leaf.shape) for leaf in carried]
-    in_specs += [whole((1, HEAD_SIZE))]
+    in_specs += [whole(leaf.shape) for leaf in extra]
     scratch = [pltpu.VMEM((rows, depth), BF16)]
     if final:
         out_shape = [jax.ShapeDtypeStruct((rows, columns), BF16)]
@@ -284,12 +316,11 @@
             final,
             shards,
             steps,
-            bases,
             sizes,
-            lengths.shape[0],
+            len(anchors),
         ),
         grid_spec=pltpu.PrefetchScalarGridSpec(
-            num_scalar_prefetch=2,
+            num_scalar_prefetch=1,
             grid=(visits, steps),
             in_specs=in_specs,
             out_specs=[whole(leaf.shape) for leaf in out_shape],
@@ -297,13 +328,8 @@
         ),
         out_shape=out_shape,
         compiler_params=pltpu.CompilerParams(vmem_limit_bytes=32 * MEBI),
-        cost_estimate=pl.CostEstimate(
-            flops=2 * rows * width * columns * visits,
-            bytes_accessed=2 * width * columns * visits + 8 * rows * columns,
-            transcendentals=0,
-        ),
         name="project",
-    )(place, lengths, *operands)
+    )(place, *operands)
 
 
 def attend_kernel(
@@ -562,36 +588,12 @@
     ]
     homes, aways = dealt[::2], dealt[1::2]
     routes, owned, depth = routes_of(shards)
-    early = [piece for piece in range(len(owned)) if depth[piece] < max(depth)]
-    late = [piece for piece in range(len(owned)) if depth[piece] == max(depth)]
     direct = [piece for piece in range(len(owned)) if depth[piece] == 1]
 
     sources = {source + 1 for source, _ in routes} - {0}
     awaited = [piece for piece in direct if piece in sources or owned[piece][0] >= 0]
-
-    def relay(line):
-        for index, (source, pairs) in enumerate(routes):
-            if index + 1 not in direct:
-                line[index + 1] = lax.ppermute(line[source + 1], "tp", pairs)
-
-    lines = []
-    for chunk in range(len(sizes)):
-        arrived = [shift_chips(aways[chunk][hop - 1], hop, chips) for hop in range(1, chips)]
-        places = [(chunk - 1, piece) for piece in awaited if chunk]
-        places += [(chunk - 2, piece) for piece in late if chunk > 1]
-        later = aways[chunk + 1 : chunk + 2] + [lines[at][piece] for at, piece in places]
-        block, later = merge(homes[chunk], arrived, later)
-        if chunk + 1 < len(sizes):
-            aways[chunk + 1] = later.pop(0)
-        for (at, piece), leaf in zip(places, later):
-            lines[at][piece] = leaf
-        line = {0: block}
-        for index, (source, pairs) in enumerate(routes):
-            if index + 1 in direct:
-                line[index + 1] = lax.ppermute(block, "tp", pairs)
-        lines.append(line)
-        for line in lines[-2:-1]:
-            relay(line)
+    early = [0, *awaited]
+    late = [piece for piece in range(len(owned)) if piece not in early]
 
     tables, counts = zip(
         *(visits_of([owned[piece] for piece in group], shards) for group in (early, late))
@@ -600,37 +602,64 @@
     table = lax.dynamic_index_in_dim(table, lax.axis_index("tp"), 0, keepdims=False)
     places = table[: 2 * counts[0]], table[2 * counts[0] :]
 
-    blocks, groups, outputs, known = [], [], (), 0
+    groups = [([base], [rows]) for base, rows in zip(bases, sizes)]
     widths = w_query.shape[1], key_weight.shape[1]
-    for chunks in GROUPS:
-        if len(sizes) - 1 in chunks:
-            relay(lines[-1])
-        span = [bases[chunk] for chunk in chunks], [sizes[chunk] for chunk in chunks]
-        groups.append(span)
-        carried = ()
-        for place, count, chosen in zip(places, counts, (early, late)):
-            carried = project(
-                chosen is late,
-                shards,
-                *span,
-                place,
-                count,
-                lengths,
-                [[lines[chunk][piece] for piece in chosen] for chunk in chunks],
-                gain,
-                weights,
-                carried,
-                frequency,
-            )
-        block = carried[0]
-        here = [block] + [shift_chips(block, hop, chips) for hop in range(1, chips)]
-        for piece in here:
-            blocks += [piece, swap_cores(piece, chips)]
-        prior, known = known, known + workers * sum(span[1])
-        outputs = attend(
-            chips, tuple(groups), known, prior, widths, slots, lengths, plan, blocks, outputs
-        )
-    return tuple(outputs)
+
+    def first_sums(at):
+        lists = [[lines[at][piece] for piece in early]]
+        shape = shards, sizes[at : at + 1], places[0], counts[0]
+        return project(False, *shape, lists, gain, weights, (), (), ())
+
+    def finished(at, sums, anchors):
+        lists = [[lines[at][piece] for piece in late]]
+        shape = shards, sizes[at : at + 1], places[1], counts[1]
+        return project(True, *shape, lists, gain, weights, sums, turns[at], anchors)[0]
+
+    def from_chips(block):
+        return [shift_chips(block, hop, chips) for hop in range(1, chips)]
+
+    def all_blocks(block, arrived):
+        return [leaf for piece in (block, *arrived) for leaf in (piece, swap_cores(piece, chips))]
+
+    lines, own, sent = [], [], []
+    last = len(sizes) - 1
+    for chunk in range(len(sizes) + 1):
+        passed = [0, *(piece for piece in awaited if piece in sources)] if chunk else []
+        later = [lines[-1][piece] for piece in passed] + aways[chunk + 1 : chunk + 2]
+        anchors = [lines[-1][piece] for piece in awaited if piece not in passed] if chunk else []
+        if chunk > 1:
+            own.append(finished(chunk - 2, first_sums(chunk - 2), ()))
+            sent.append(from_chips(own[-1]))
+            anchors.append(own[-1])
+        if chunk <= last:
+            arrived = [shift_chips(aways[chunk][hop - 1], hop, chips) for hop in range(1, chips)]
+            block, later = merge(homes[chunk], arrived, later, anchors)
+        else:
+            later = after(later, [*anchors, *sent[-2]])
+        aways[chunk + 1 : chunk + 2] = later[len(passed) :]
+        if chunk:
+            lines[-1].update(zip(passed, later))
+            for index, (source, pairs) in enumerate(routes):
+                if index + 1 in late:
+                    lines[-1][index + 1] = lax.ppermute(lines[-1][source + 1], "tp", pairs)
+        if chunk <= last:
+            line = {0: block}
+            for index, (source, pairs) in enumerate(routes):
+                if index + 1 in awaited:
+                    line[index + 1] = lax.ppermute(block, "tp", pairs)
+            lines.append(line)
+        if chunk == 1:
+            turns = angles(groups, lengths, frequency, block)
+    own.append(finished(last, first_sums(last), sent[-1]))
+    blocks = []
+    for at in range(last):
+        blocks += all_blocks(own[at], after(sent[at], own[at + 1 : at + 2]))
+    sent.append(from_chips(own[last]))
+    known = workers * sum(sizes[:-1])
+    common = widths, slots, lengths, plan
+    outputs = attend(chips, groups[:-1], known, 0, *common, blocks, ())
+    blocks += all_blocks(own[last], after(sent[last], outputs[:1]))
+    return tuple(attend(chips, groups, workers * live, known, *common, blocks, outputs))
 
 
 def solution(mesh):

time: 130 us -> 131 us (level)
  the two profiles are of different devices: /device:TPU:0 before, /device:TPU:15 now
where the time goes in v2:
time: 131 us; the launch traced here: 130 us
  Pallas kernels  64.2 us (49%)
  starting transfers between devices  33.2 us (25%)
  waiting for transfers between devices  27.1 us (21%)
  local copies, waits for them, and re-layouts  4.26 us (3%)
    pallas_call x6, Pallas kernels, project(): pl.pallas_call(functools.partial(project_kernel, len(lines[0]), bool(carr...  41.5 us
    pallas_call x2, Pallas kernels, attend(): pl.pallas_call(functools.partial(attend_kernel, chips, groups, known, pri...  14.5 us
    ppermute x6, starting transfers between devices, local(): lines[-1][index + 1] = lax.ppermute(lines[-1][source + 1], 'tp', pairs)  12.4 us
    ppermute x7, starting transfers between devices, swap_cores(): return lax.ppermute(value, 'req', [(d, d ^ 1) for d in range(2 * chips)])  10.6 us
    ppermute x6, waiting for transfers between devices, local(): line[index + 1] = lax.ppermute(block, 'tp', pairs)  10.5 us
    ppermute x6, waiting for transfers between devices, local(): lines[-1][index + 1] = lax.ppermute(lines[-1][source + 1], 'tp', pairs)  9.99 us
    pallas_call x3, Pallas kernels, deal(): pl.pallas_call(functools.partial(deal_kernel, chips, bases, sizes, twins)...  6.92 us
    ppermute x6, starting transfers between devices, local(): line[index + 1] = lax.ppermute(block, 'tp', pairs)  6.81 us
  transfers between devices with their start and end apart: 25, of which 8 were waited for; matrix products, arithmetic and copies ran while one was open for 1% of the time, Pallas kernels for 42%

profile of v2, /device:TPU:15, one launch (start us, length us, event | category | flops | bytes accessed | tf_op | source)
XLA Modules:
  0.0 129.7 jit_solution(1387595963222873183)
XLA Ops:
  0.6 0.7 collective-permute-start
  1.4 1.6 %copy-done = bf16[512,2048]{1,0:T(8,128)(2,1)S(1)} copy-done((bf16[512,2048]{1,0:T(8,128)(2,1)S(1)}, bf16[512,2048]{1,0:T(8,128)(2,1)}, u32[]{:S(2)}) %copy-start) | copy-done | bytes 2097176
  3.0 0.7 copy-done.3
  3.6 1.6 %deal.4 = (bf16[64,2048]{1,0:T(8,128)(2,1)S(1)}, bf16[1,64,2048]{2,1,0:T(8,128)(2,1)S(1)}) custom-call(s32[4]{0:T(128)S(1)} %copy-done.3, bf16[512,2048]{1,0:T(8,128)(2,1)S(1)} %copy-done), custom_call_target="tpu_custom_call" | custom-call | tf_op jit(solution)/shard_map/deal/pallas_call | solution.py:78
  5.3 0.1 collective-permute-done.refs_1_.refs_0_
  5.4 1.7 %deal.5 = (bf16[64,2048]{1,0:T(8,128)(2,1)S(1)}, bf16[1,64,2048]{2,1,0:T(8,128)(2,1)S(1)}) custom-call(s32[4]{0:T(128)S(1)} %copy-done.3, bf16[512,2048]{1,0:T(8,128)(2,1)S(1)} %collective-permute-done.refs_1_.refs_0_, bf16[64,2048]{1,0:T(8,128)(2,1)S(1)} %get-tuple-element.36.refs_1_, bf16[1,64,2048]{2,1,0:T(8,128)(2,1)S(1)} %get-tuple-element.37.refs_2_), custom_call_target="tpu_custom_call" | custom-call | tf_op jit(solution)/shard_map/deal/pallas_call | solution.py:78
  7.0 0.0 copy-start.7
  7.1 0.0 copy-start.4
  7.1 0.0 copy-start.6
  7.1 0.3 collective-permute-start.1
  7.4 3.6 %deal.3 = (bf16[128,2048]{1,0:T(8,128)(2,1)S(1)}, bf16[1,128,2048]{2,1,0:T(8,128)(2,1)S(1)}, bf16[64,2048]{1,0:T(8,128)(2,1)S(1)}, bf16[1,64,2048]{2,1,0:T(8,128)(2,1)S(1)}) custom-call(s32[4]{0:T(128)S(1)} %copy-done.3, bf16[512,2048]{1,0:T(8,128)(2,1)S(1)} %copy-done.1, bf16[512,2048]{1,0:T(8,128)(2,1)S(1)} %collective-permute-done.refs_1_.refs_0_), custom_call_target="tpu_custom_call" | custom-call | tf_op jit(solution)/shard_map/deal/pallas_call | solution.py:78
  11.0 3.6 %collective-permute-done.1.refs_0_ = bf16[64,2048]{1,0:T(8,128)(2,1)S(1)} collective-permute-done((bf16[64,2048]{1,0:T(8,128)(2,1)S(1)}, bf16[64,2048]{1,0:T(8,128)(2,1)S(1)}, u32[]{:S(2)}, u32[]{:S(2)}) %collective-permute-start.1) | collective-permute-done | bytes 262176 | tf_op jit(solution)/shard_map/ppermute | solution.py:558
  14.7 0.3 collective-permute-start.2
  15.0 0.2 collective-permute-start.4
  15.2 2.3 %collective-permute-start.3 = (bf16[64,2048]{1,0:T(8,128)(2,1)S(1)}, bf16[64,2048]{1,0:T(8,128)(2,1)S(1)}, u32[]{:S(2)}, u32[]{:S(2)}) collective-permute-start(bf16[64,2048]{1,0:T(8,128)(2,1)S(1)} %get-tuple-element.42.refs_1_), channel_id=1, source_target_pairs={{0,2},{1,3},{2,0},{3,1},{4,6},{5,7},{6,4},{7,5},{8,10},{9,11},{10,... | collective-permute-start | bytes 786440 | tf_op jit(solution)/shard_map/ppermute | solution.py:649
  17.5 6.1 %collective-permute-done.4.refs_4_.refs_1_ = bf16[64,2048]{1,0:T(8,128)(2,1)S(1)} collective-permute-done((bf16[64,2048]{1,0:T(8,128)(2,1)S(1)}, bf16[64,2048]{1,0:T(8,128)(2,1)S(1)}, u32[]{:S(2)}, u32[]{:S(2)}) %collective-permute-start.4) | collective-permute-done | bytes 262176 | tf_op jit(solution)/shard_map/ppermute | solution.py:649
  23.6 4.5 %collective-permute-done.3.refs_2_ = bf16[64,2048]{1,0:T(8,128)(2,1)S(1)} collective-permute-done((bf16[64,2048]{1,0:T(8,128)(2,1)S(1)}, bf16[64,2048]{1,0:T(8,128)(2,1)S(1)}, u32[]{:S(2)}, u32[]{:S(2)}) %collective-permute-start.3) | collective-permute-done | bytes 262176 | tf_op jit(solution)/shard_map/ppermute | solution.py:649
  28.0 0.1 merge.4
  28.1 0.1 collective-permute-start.11
  28.2 1.4 %collective-permute-start.10 = (bf16[128,2048]{1,0:T(8,128)(2,1)S(1)}, bf16[128,2048]{1,0:T(8,128)(2,1)S(1)}, u32[]{:S(2)}, u32[]{:S(2)}) collective-permute-start(bf16[128,2048]{1,0:T(8,128)(2,1)S(1)} %get-tuple-element.48.anchor_ref.refs_1_), channel_id=1, source_target_pairs={{0,2},{1,3},{2,0},{3,1},{4,6},{5,7},{6,4},{7,5},{8,10},{9,11},{10,... | collective-permute-start | bytes 1572872 | tf_op jit(solution)/shard_map/ppermute | solution.py:649
  29.6 0.7 constant_dynamic-slice_fusion
  30.3 1.1 collective-permute-start.9
  31.4 3.2 %collective-permute-start.5 = (bf16[64,2048]{1,0:T(8,128)(2,1)S(1)}, bf16[64,2048]{1,0:T(8,128)(2,1)S(1)}, u32[]{:S(2)}, u32[]{:S(2)}) collective-permute-start(bf16[64,2048]{1,0:T(8,128)(2,1)S(1)} %get-tuple-element.44.refs_0_), channel_id=1, source_target_pairs={{1,2},{2,1},{5,6},{6,5},{9,10},{10,9},{13,14},{14,13},{17,18},{18,... | collective-permute-start | bytes 786440 | tf_op jit(solution)/shard_map/ppermute | solution.py:644
  34.6 1.3 %collective-permute-start.6 = (bf16[64,2048]{1,0:T(8,128)(2,1)S(1)}, bf16[64,2048]{1,0:T(8,128)(2,1)S(1)}, u32[]{:S(2)}, u32[]{:S(2)}) collective-permute-start(bf16[64,2048]{1,0:T(8,128)(2,1)S(1)} %get-tuple-element.45.refs_2_), channel_id=1, source_target_pairs={{2,3},{1,0},{6,7},{5,4},{10,11},{9,8},{14,15},{13,12},{18,19},{17,... | collective-permute-start | bytes 786440 | tf_op jit(solution)/shard_map/ppermute | solution.py:644
  35.9 0.1 slice_bitcast_fusion.1.place_ref
  36.0 1.1 angles.1
  37.1 9.6 %project.6 = (f32[64,1536]{1,0:T(8,128)S(1)}, f32[64,128]{1,0:T(8,128)S(1)}) custom-call(s32[6]{0:T(128)S(1)} %slice_bitcast_fusion.place_ref, bf16[64,2048]{1,0:T(8,128)(2,1)S(1)} %get-tuple-element.44.refs_0_, bf16[64,2048]{1,0:T(8,128)(2,1)S(1)} %collective-permute-done.4.refs_4_.refs_1_, bf16[64,2048]{1,0:T(8,128)(2,1)S(1)} %get-tuple-element.45.refs_2_, ...), custom_call_target="tpu_custom_call" | custom-call | tf_op jit(solution)/shard_map/project/pallas_call | solution.py:311
  46.7 10.0 %collective-permute-done.5.refs_0_ = bf16[64,2048]{1,0:T(8,128)(2,1)S(1)} collective-permute-done((bf16[64,2048]{1,0:T(8,128)(2,1)S(1)}, bf16[64,2048]{1,0:T(8,128)(2,1)S(1)}, u32[]{:S(2)}, u32[]{:S(2)}) %collective-permute-start.5) | collective-permute-done | bytes 262176 | tf_op jit(solution)/shard_map/ppermute | solution.py:644
  56.7 4.3 %project.7.refs_4_.refs_0_ = bf16[64,1536]{1,0:T(8,128)(2,1)S(1)} custom-call(s32[2]{0:T(128)S(1)} %slice_bitcast_fusion.1.place_ref, bf16[64,2048]{1,0:T(8,128)(2,1)S(1)} %collective-permute-done.5.refs_0_, bf16[64,2048]{1,0:T(8,128)(2,1)S(1)} %collective-permute-done.6.refs_1_, f32[1,8192]{1,0:T(1,128)S(1)} %bitcast.9, bf16[8192,1024]{1,0:T(8,128)(2,1)} %refs_4_.11, ...), custom_call_target="tpu_custom_call" | custom-call | tf_op jit(solution)/shard_map/project/pallas_call | solution.py:311
  60.9 0.0 collective-permute-done.9.refs_0_
  61.0 0.0 collective-permute-done.10.refs_2_
  61.0 2.8 %collective-permute-start.12 = (bf16[128,2048]{1,0:T(8,128)(2,1)S(1)}, bf16[128,2048]{1,0:T(8,128)(2,1)S(1)}, u32[]{:S(2)}, u32[]{:S(2)}) collective-permute-start(bf16[128,2048]{1,0:T(8,128)(2,1)S(1)} %get-tuple-element.53.refs_0_), channel_id=1, source_target_pairs={{1,2},{2,1},{5,6},{6,5},{9,10},{10,9},{13,14},{14,13},{17,18},{18,... | collective-permute-start | bytes 1572872 | tf_op jit(solution)/shard_map/ppermute | solution.py:644
  63.9 1.3 %collective-permute-start.13 = (bf16[128,2048]{1,0:T(8,128)(2,1)S(1)}, bf16[128,2048]{1,0:T(8,128)(2,1)S(1)}, u32[]{:S(2)}, u32[]{:S(2)}) collective-permute-start(bf16[128,2048]{1,0:T(8,128)(2,1)S(1)} %get-tuple-element.54.refs_2_), channel_id=1, source_target_pairs={{2,3},{1,0},{6,7},{5,4},{10,11},{9,8},{14,15},{13,12},{18,19},{17,... | collective-permute-start | bytes 1572872 | tf_op jit(solution)/shard_map/ppermute | solution.py:644
  65.2 0.1 collective-permute-start.18
  65.3 2.8 %collective-permute-start.17 = (bf16[64,2048]{1,0:T(8,128)(2,1)S(1)}, bf16[64,2048]{1,0:T(8,128)(2,1)S(1)}, u32[]{:S(2)}, u32[]{:S(2)}) collective-permute-start(bf16[64,2048]{1,0:T(8,128)(2,1)S(1)} %get-tuple-element.59.refs_0_), channel_id=1, source_target_pairs={{0,2},{1,3},{2,0},{3,1},{4,6},{5,7},{6,4},{7,5},{8,10},{9,11},{10,... | collective-permute-start | bytes 786440 | tf_op jit(solution)/shard_map/ppermute | solution.py:649
  68.0 1.3 collective-permute-start.8
  69.3 9.5 %project.8 = (f32[128,1536]{1,0:T(8,128)S(1)}, f32[128,128]{1,0:T(8,128)S(1)}) custom-call(s32[6]{0:T(128)S(1)} %slice_bitcast_fusion.place_ref, bf16[128,2048]{1,0:T(8,128)(2,1)S(1)} %get-tuple-element.53.refs_0_, bf16[128,2048]{1,0:T(8,128)(2,1)S(1)} %collective-permute-done.11.refs_3_.refs_1_, bf16[128,2048]{1,0:T(8,128)(2,1)S(1)} %get-tuple-element.54.refs_2_, ...), custom_call_target="tpu_custom_call" | custom-call | tf_op jit(solution)/shard_map/project/pallas_call | solution.py:311
  78.8 0.0 collective-permute-done.12.refs_0_
  78.8 4.3 %project.9.refs_1_.refs_3_.refs_4_ = bf16[128,1536]{1,0:T(8,128)(2,1)S(1)} custom-call(s32[2]{0:T(128)S(1)} %slice_bitcast_fusion.1.place_ref, bf16[128,2048]{1,0:T(8,128)(2,1)S(1)} %collective-permute-done.12.refs_0_, bf16[128,2048]{1,0:T(8,128)(2,1)S(1)} %collective-permute-done.13.refs_1_, f32[1,8192]{1,0:T(1,128)S(1)} %bitcast.11, ...), custom_call_target="tpu_custom_call" | custom-call | tf_op jit(solution)/shard_map/project/pallas_call | solution.py:311
  83.2 0.2 collective-permute-start.16
  83.4 0.0 collective-permute-done.17.refs_1_
  83.4 1.9 %collective-permute-start.19 = (bf16[64,2048]{1,0:T(8,128)(2,1)S(1)}, bf16[64,2048]{1,0:T(8,128)(2,1)S(1)}, u32[]{:S(2)}, u32[]{:S(2)}) collective-permute-start(bf16[64,2048]{1,0:T(8,128)(2,1)S(1)} %get-tuple-element.60.refs_0_), channel_id=1, source_target_pairs={{1,2},{2,1},{5,6},{6,5},{9,10},{10,9},{13,14},{14,13},{17,18},{18,... | collective-permute-start | bytes 786440 | tf_op jit(solution)/shard_map/ppermute | solution.py:644
  85.3 1.8 %collective-permute-start.20 = (bf16[64,2048]{1,0:T(8,128)(2,1)S(1)}, bf16[64,2048]{1,0:T(8,128)(2,1)S(1)}, u32[]{:S(2)}, u32[]{:S(2)}) collective-permute-start(bf16[64,2048]{1,0:T(8,128)(2,1)S(1)} %get-tuple-element.61.refs_2_), channel_id=1, source_target_pairs={{2,3},{1,0},{6,7},{5,4},{10,11},{9,8},{14,15},{13,12},{18,19},{17,... | collective-permute-start | bytes 786440 | tf_op jit(solution)/shard_map/ppermute | solution.py:644
  87.1 9.0 %collective-permute-start.15 = (bf16[128,1536]{1,0:T(8,128)(2,1)S(1)}, bf16[128,1536]{1,0:T(8,128)(2,1)S(1)}, u32[]{:S(2)}, u32[]{:S(2)}) collective-permute-start(bf16[128,1536]{1,0:T(8,128)(2,1)S(1)} %project.9.refs_1_.refs_3_.refs_4_), channel_id=1, source_target_pairs={{0,4},{4,0},{8,12},{12,8},{1,5},{5,1},{9,13},{13,9},{2,6},{6,2},{1... | collective-permute-start | bytes 1179656 | tf_op jit(solution)/shard_map/ppermute | solution.py:562
  96.2 9.6 %project.10 = (f32[64,1536]{1,0:T(8,128)S(1)}, f32[64,128]{1,0:T(8,128)S(1)}) custom-call(s32[6]{0:T(128)S(1)} %slice_bitcast_fusion.place_ref, bf16[64,2048]{1,0:T(8,128)(2,1)S(1)} %get-tuple-element.60.refs_0_, bf16[64,2048]{1,0:T(8,128)(2,1)S(1)} %collective-permute-done.18.refs_2_.refs_1_, bf16[64,2048]{1,0:T(8,128)(2,1)S(1)} %get-tuple-element.61.refs_2_, ...), custom_call_target="tpu_custom_call" | custom-call | tf_op jit(solution)/shard_map/project/pallas_call | solution.py:311
  105.8 0.0 collective-permute-done.19.refs_1_
  105.8 0.0 copy-start.5
  105.8 4.3 %project.11.refs_1_.refs_8_ = bf16[64,1536]{1,0:T(8,128)(2,1)S(1)} custom-call(s32[2]{0:T(128)S(1)} %slice_bitcast_fusion.1.place_ref, bf16[128,1536]{1,0:T(8,128)(2,1)S(1)} %collective-permute-done.16.refs_0_, bf16[64,2048]{1,0:T(8,128)(2,1)S(1)} %collective-permute-done.19.refs_1_, bf16[64,2048]{1,0:T(8,128)(2,1)S(1)} %collective-permute-done.20.refs_2_, ...), custom_call_target="tpu_custom_call" | custom-call | tf_op jit(solution)/shard_map/project/pallas_call | solution.py:311
  110.1 0.1 collective-permute-start.21
  110.2 0.5 collective-permute-start.7
  110.7 0.1 collective-permute-start.14
  110.8 0.2 collective-permute-start.23
  110.9 1.2 collective-permute-done.7.refs_1_
  112.2 0.1 collective-permute-start.22
  112.3 0.1 collective-permute-done.14.refs_3_
  112.5 0.0 collective-permute-done.15.refs_5_
  112.5 0.0 collective-permute-done.21.refs_7_
  112.5 6.9 %attend.2 = (bf16[512,1024]{1,0:T(8,128)(2,1)}, bf16[2,512,256]{2,1,0:T(8,128)(2,1)}) custom-call(s32[4]{0:T(128)S(1)} %copy-done.4, s32[16]{0:T(128)S(1)} %copy-done.5, bf16[64,1536]{1,0:T(8,128)(2,1)S(1)} %project.7.refs_4_.refs_0_, bf16[64,1536]{1,0:T(8,128)(2,1)S(1)} %collective-permute-done.7.refs_1_, bf16[64,1536]{1,0:T(8,128)(2,1)S(1)} %after.4.refs_2_, ...), custom_call_target="tpu_custom_call" | custom-call | tf_op jit(solution)/shard_map/attend/pallas_call | solution.py:531
  119.4 0.0 collective-permute-done.23.refs_0_
  119.4 0.0 copy-start.2
  119.4 1.2 copy-done.2
  120.7 0.0 collective-permute-start.24
  120.7 1.4 %collective-permute-done.24.refs_11_ = bf16[64,1536]{1,0:T(8,128)(2,1)S(1)} collective-permute-done((bf16[64,1536]{1,0:T(8,128)(2,1)S(1)}, bf16[64,1536]{1,0:T(8,128)(2,1)S(1)}, u32[]{:S(2)}, u32[]{:S(2)}) %collective-permute-start.24) | collective-permute-done | bytes 196640 | tf_op jit(solution)/shard_map/ppermute | solution.py:562
  122.1 7.6 %attend.3 = (bf16[512,1024]{1,0:T(8,128)(2,1)}, bf16[2,512,256]{2,1,0:T(8,128)(2,1)}) custom-call(s32[4]{0:T(128)S(1)} %copy-done.4, s32[16]{0:T(128)S(1)} %copy-done.5, bf16[64,1536]{1,0:T(8,128)(2,1)S(1)} %project.7.refs_4_.refs_0_, bf16[64,1536]{1,0:T(8,128)(2,1)S(1)} %collective-permute-done.7.refs_1_, ...), custom_call_target="tpu_custom_call", output_to_operand_aliasing={{0}: (14, {}), {1}: (15, {})} | custom-call | tf_op jit(solution)/shard_map/attend/pallas_call | solution.py:531
  (25 shorter events, 0.1 us)
Async XLA Ops:
  0.6 4.7 %collective-permute-start = (bf16[512,2048]{1,0:T(8,128)(2,1)}, bf16[512,2048]{1,0:T(8,128)(2,1)S(1)}, u32[]{:S(2)}, u32[]{:S(2)}) collective-permute-start(bf16[512,2048]{1,0:T(8,128)(2,1)} %refs_0_.3), channel_id=1, source_target_pairs={{0,4},{4,0},{8,12},{12,8},{1,5},{5,1},{9,13},{13,9},{2,6},{6,2},{1... | collective-permute-start | bytes 6291464 | tf_op jit(solution)/shard_map/ppermute | solution.py:562
  1.4 1.6 %copy-start = (bf16[512,2048]{1,0:T(8,128)(2,1)S(1)}, bf16[512,2048]{1,0:T(8,128)(2,1)}, u32[]{:S(2)}) copy-start(bf16[512,2048]{1,0:T(8,128)(2,1)} %refs_0_.3) | copy-start | bytes 6291460
  3.0 0.7 copy-start.3
  3.6 3.8 %copy-start.1 = (bf16[512,2048]{1,0:T(8,128)(2,1)S(1)}, bf16[512,2048]{1,0:T(8,128)(2,1)}, u32[]{:S(2)}) copy-start(bf16[512,2048]{1,0:T(8,128)(2,1)} %refs_0_.3) | copy-start | bytes 6291460
  7.0 28.9 %copy-start.7 = (bf16[8192]{0:T(1024)(128)(2,1)S(1)}, bf16[8192]{0:T(1024)(128)(2,1)}, u32[]{:S(2)}) copy-start(bf16[8192]{0:T(1024)(128)(2,1)} %param.10) | copy-start | bytes 49156
  7.1 28.9 %copy-start.4 = (s32[4]{0:T(128)S(1)}, s32[4]{0:T(128)}, u32[]{:S(2)}) copy-start(s32[4]{0:T(128)} %lengths_ref.11) | copy-start | bytes 52
  7.1 28.9 %copy-start.6 = (f32[1,128]{1,0:T(1,128)S(1)}, f32[1,128]{1,0:T(1,128)}, u32[]{:S(2)}) copy-start(f32[1,128]{1,0:T(1,128)} %constant.14.clone.frequency_ref) | copy-start | bytes 1540
  7.1 7.6 %collective-permute-start.1 = (bf16[64,2048]{1,0:T(8,128)(2,1)S(1)}, bf16[64,2048]{1,0:T(8,128)(2,1)S(1)}, u32[]{:S(2)}, u32[]{:S(2)}) collective-permute-start(bf16[64,2048]{1,0:T(8,128)(2,1)S(1)} %bitcast.16), channel_id=1, source_target_pairs={{0,8},{4,12},{8,0},{12,4},{1,9},{5,13},{9,1},{13,5},{2,10},{6,14},... | collective-permute-start | bytes 786440 | tf_op jit(solution)/shard_map/ppermute | solution.py:558
  14.7 13.3 %collective-permute-start.2 = (bf16[128,2048]{1,0:T(8,128)(2,1)S(1)}, bf16[128,2048]{1,0:T(8,128)(2,1)S(1)}, u32[]{:S(2)}, u32[]{:S(2)}) collective-permute-start(bf16[128,2048]{1,0:T(8,128)(2,1)S(1)} %bitcast.14), channel_id=1, source_target_pairs={{0,8},{4,12},{8,0},{12,4},{1,9},{5,13},{9,1},{13,5},{2,10},{6,14},... | collective-permute-start | bytes 1572872 | tf_op jit(solution)/shard_map/ppermute | solution.py:558
  15.0 8.6 %collective-permute-start.4 = (bf16[64,2048]{1,0:T(8,128)(2,1)S(1)}, bf16[64,2048]{1,0:T(8,128)(2,1)S(1)}, u32[]{:S(2)}, u32[]{:S(2)}) collective-permute-start(bf16[64,2048]{1,0:T(8,128)(2,1)S(1)} %get-tuple-element.42.refs_1_), channel_id=1, source_target_pairs={{0,1},{1,0},{2,3},{3,2},{4,5},{5,4},{6,7},{7,6},{8,9},{9,8},{10,11... | collective-permute-start | bytes 786440 | tf_op jit(solution)/shard_map/ppermute | solution.py:649
  15.2 12.8 %collective-permute-start.3 = (bf16[64,2048]{1,0:T(8,128)(2,1)S(1)}, bf16[64,2048]{1,0:T(8,128)(2,1)S(1)}, u32[]{:S(2)}, u32[]{:S(2)}) collective-permute-start(bf16[64,2048]{1,0:T(8,128)(2,1)S(1)} %get-tuple-element.42.refs_1_), channel_id=1, source_target_pairs={{0,2},{1,3},{2,0},{3,1},{4,6},{5,7},{6,4},{7,5},{8,10},{9,11},{10,... | collective-permute-start | bytes 786440 | tf_op jit(solution)/shard_map/ppermute | solution.py:649
  28.1 32.9 %collective-permute-start.11 = (bf16[128,2048]{1,0:T(8,128)(2,1)S(1)}, bf16[128,2048]{1,0:T(8,128)(2,1)S(1)}, u32[]{:S(2)}, u32[]{:S(2)}) collective-permute-start(bf16[128,2048]{1,0:T(8,128)(2,1)S(1)} %get-tuple-element.48.anchor_ref.refs_1_), channel_id=1, source_target_pairs={{0,1},{1,0},{2,3},{3,2},{4,5},{5,4},{6,7},{7,6},{8,9},{9,8},{10,11... | collective-permute-start | bytes 1572872 | tf_op jit(solution)/shard_map/ppermute | solution.py:649
  28.2 32.8 %collective-permute-start.10 = (bf16[128,2048]{1,0:T(8,128)(2,1)S(1)}, bf16[128,2048]{1,0:T(8,128)(2,1)S(1)}, u32[]{:S(2)}, u32[]{:S(2)}) collective-permute-start(bf16[128,2048]{1,0:T(8,128)(2,1)S(1)} %get-tuple-element.48.anchor_ref.refs_1_), channel_id=1, source_target_pairs={{0,2},{1,3},{2,0},{3,1},{4,6},{5,7},{6,4},{7,5},{8,10},{9,11},{10,... | collective-permute-start | bytes 1572872 | tf_op jit(solution)/shard_map/ppermute | solution.py:649
  30.3 30.7 %collective-permute-start.9 = (bf16[64,2048]{1,0:T(8,128)(2,1)S(1)}, bf16[64,2048]{1,0:T(8,128)(2,1)S(1)}, u32[]{:S(2)}, u32[]{:S(2)}) collective-permute-start(bf16[64,2048]{1,0:T(8,128)(2,1)S(1)} %bitcast.15), channel_id=1, source_target_pairs={{0,8},{4,12},{8,0},{12,4},{1,9},{5,13},{9,1},{13,5},{2,10},{6,14},... | collective-permute-start | bytes 786440 | tf_op jit(solution)/shard_map/ppermute | solution.py:558
  31.4 25.3 %collective-permute-start.5 = (bf16[64,2048]{1,0:T(8,128)(2,1)S(1)}, bf16[64,2048]{1,0:T(8,128)(2,1)S(1)}, u32[]{:S(2)}, u32[]{:S(2)}) collective-permute-start(bf16[64,2048]{1,0:T(8,128)(2,1)S(1)} %get-tuple-element.44.refs_0_), channel_id=1, source_target_pairs={{1,2},{2,1},{5,6},{6,5},{9,10},{10,9},{13,14},{14,13},{17,18},{18,... | collective-permute-start | bytes 786440 | tf_op jit(solution)/shard_map/ppermute | solution.py:644
  34.6 22.1 %collective-permute-start.6 = (bf16[64,2048]{1,0:T(8,128)(2,1)S(1)}, bf16[64,2048]{1,0:T(8,128)(2,1)S(1)}, u32[]{:S(2)}, u32[]{:S(2)}) collective-permute-start(bf16[64,2048]{1,0:T(8,128)(2,1)S(1)} %get-tuple-element.45.refs_2_), channel_id=1, source_target_pairs={{2,3},{1,0},{6,7},{5,4},{10,11},{9,8},{14,15},{13,12},{18,19},{17,... | collective-permute-start | bytes 786440 | tf_op jit(solution)/shard_map/ppermute | solution.py:644
  61.0 17.8 %collective-permute-start.12 = (bf16[128,2048]{1,0:T(8,128)(2,1)S(1)}, bf16[128,2048]{1,0:T(8,128)(2,1)S(1)}, u32[]{:S(2)}, u32[]{:S(2)}) collective-permute-start(bf16[128,2048]{1,0:T(8,128)(2,1)S(1)} %get-tuple-element.53.refs_0_), channel_id=1, source_target_pairs={{1,2},{2,1},{5,6},{6,5},{9,10},{10,9},{13,14},{14,13},{17,18},{18,... | collective-permute-start | bytes 1572872 | tf_op jit(solution)/shard_map/ppermute | solution.py:644
  63.9 15.0 %collective-permute-start.13 = (bf16[128,2048]{1,0:T(8,128)(2,1)S(1)}, bf16[128,2048]{1,0:T(8,128)(2,1)S(1)}, u32[]{:S(2)}, u32[]{:S(2)}) collective-permute-start(bf16[128,2048]{1,0:T(8,128)(2,1)S(1)} %get-tuple-element.54.refs_2_), channel_id=1, source_target_pairs={{2,3},{1,0},{6,7},{5,4},{10,11},{9,8},{14,15},{13,12},{18,19},{17,... | collective-permute-start | bytes 1572872 | tf_op jit(solution)/shard_map/ppermute | solution.py:644
  65.2 18.2 %collective-permute-start.18 = (bf16[64,2048]{1,0:T(8,128)(2,1)S(1)}, bf16[64,2048]{1,0:T(8,128)(2,1)S(1)}, u32[]{:S(2)}, u32[]{:S(2)}) collective-permute-start(bf16[64,2048]{1,0:T(8,128)(2,1)S(1)} %get-tuple-element.59.refs_0_), channel_id=1, source_target_pairs={{0,1},{1,0},{2,3},{3,2},{4,5},{5,4},{6,7},{7,6},{8,9},{9,8},{10,11... | collective-permute-start | bytes 786440 | tf_op jit(solution)/shard_map/ppermute | solution.py:649
  65.3 18.1 %collective-permute-start.17 = (bf16[64,2048]{1,0:T(8,128)(2,1)S(1)}, bf16[64,2048]{1,0:T(8,128)(2,1)S(1)}, u32[]{:S(2)}, u32[]{:S(2)}) collective-permute-start(bf16[64,2048]{1,0:T(8,128)(2,1)S(1)} %get-tuple-element.59.refs_0_), channel_id=1, source_target_pairs={{0,2},{1,3},{2,0},{3,1},{4,6},{5,7},{6,4},{7,5},{8,10},{9,11},{10,... | collective-permute-start | bytes 786440 | tf_op jit(solution)/shard_map/ppermute | solution.py:649
  68.0 15.4 %collective-permute-start.8 = (bf16[64,1536]{1,0:T(8,128)(2,1)S(1)}, bf16[64,1536]{1,0:T(8,128)(2,1)S(1)}, u32[]{:S(2)}, u32[]{:S(2)}) collective-permute-start(bf16[64,1536]{1,0:T(8,128)(2,1)S(1)} %project.7.refs_4_.refs_0_), channel_id=1, source_target_pairs={{0,8},{4,12},{8,0},{12,4},{1,9},{5,13},{9,1},{13,5},{2,10},{6,14},... | collective-permute-start | bytes 589832 | tf_op jit(solution)/shard_map/ppermute | solution.py:558
  83.2 22.6 %collective-permute-start.16 = (bf16[128,1536]{1,0:T(8,128)(2,1)S(1)}, bf16[128,1536]{1,0:T(8,128)(2,1)S(1)}, u32[]{:S(2)}, u32[]{:S(2)}) collective-permute-start(bf16[128,1536]{1,0:T(8,128)(2,1)S(1)} %project.9.refs_1_.refs_3_.refs_4_), channel_id=1, source_target_pairs={{0,8},{4,12},{8,0},{12,4},{1,9},{5,13},{9,1},{13,5},{2,10},{6,14},... | collective-permute-start | bytes 1179656 | tf_op jit(solution)/shard_map/ppermute | solution.py:558
  83.4 22.3 %collective-permute-start.19 = (bf16[64,2048]{1,0:T(8,128)(2,1)S(1)}, bf16[64,2048]{1,0:T(8,128)(2,1)S(1)}, u32[]{:S(2)}, u32[]{:S(2)}) collective-permute-start(bf16[64,2048]{1,0:T(8,128)(2,1)S(1)} %get-tuple-element.60.refs_0_), channel_id=1, source_target_pairs={{1,2},{2,1},{5,6},{6,5},{9,10},{10,9},{13,14},{14,13},{17,18},{18,... | collective-permute-start | bytes 786440 | tf_op jit(solution)/shard_map/ppermute | solution.py:644
  85.3 20.4 %collective-permute-start.20 = (bf16[64,2048]{1,0:T(8,128)(2,1)S(1)}, bf16[64,2048]{1,0:T(8,128)(2,1)S(1)}, u32[]{:S(2)}, u32[]{:S(2)}) collective-permute-start(bf16[64,2048]{1,0:T(8,128)(2,1)S(1)} %get-tuple-element.61.refs_2_), channel_id=1, source_target_pairs={{2,3},{1,0},{6,7},{5,4},{10,11},{9,8},{14,15},{13,12},{18,19},{17,... | collective-permute-start | bytes 786440 | tf_op jit(solution)/shard_map/ppermute | solution.py:644
  87.1 25.3 %collective-permute-start.15 = (bf16[128,1536]{1,0:T(8,128)(2,1)S(1)}, bf16[128,1536]{1,0:T(8,128)(2,1)S(1)}, u32[]{:S(2)}, u32[]{:S(2)}) collective-permute-start(bf16[128,1536]{1,0:T(8,128)(2,1)S(1)} %project.9.refs_1_.refs_3_.refs_4_), channel_id=1, source_target_pairs={{0,4},{4,0},{8,12},{12,8},{1,5},{5,1},{9,13},{13,9},{2,6},{6,2},{1... | collective-permute-start | bytes 1179656 | tf_op jit(solution)/shard_map/ppermute | solution.py:562
  105.8 6.7 %copy-start.5 = (s32[16]{0:T(128)S(1)}, s32[16]{0:T(128)}, u32[]{:S(2)}) copy-start(s32[16]{0:T(128)} %plan_ref.3) | copy-start | bytes 196
  110.1 2.4 %collective-permute-start.21 = (bf16[128,1536]{1,0:T(8,128)(2,1)S(1)}, bf16[128,1536]{1,0:T(8,128)(2,1)S(1)}, u32[]{:S(2)}, u32[]{:S(2)}) collective-permute-start(bf16[128,1536]{1,0:T(8,128)(2,1)S(1)} %after.6.refs_6_), channel_id=1, source_target_pairs={{0,4},{4,0},{8,12},{12,8},{1,5},{5,1},{9,13},{13,9},{2,6},{6,2},{1... | collective-permute-start | bytes 1179656 | tf_op jit(solution)/shard_map/ppermute | solution.py:562
  110.2 2.0 %collective-permute-start.7 = (bf16[64,1536]{1,0:T(8,128)(2,1)S(1)}, bf16[64,1536]{1,0:T(8,128)(2,1)S(1)}, u32[]{:S(2)}, u32[]{:S(2)}) collective-permute-start(bf16[64,1536]{1,0:T(8,128)(2,1)S(1)} %project.7.refs_4_.refs_0_), channel_id=1, source_target_pairs={{0,4},{4,0},{8,12},{12,8},{1,5},{5,1},{9,13},{13,9},{2,6},{6,2},{1... | collective-permute-start | bytes 589832 | tf_op jit(solution)/shard_map/ppermute | solution.py:562
  110.7 1.8 %collective-permute-start.14 = (bf16[64,1536]{1,0:T(8,128)(2,1)S(1)}, bf16[64,1536]{1,0:T(8,128)(2,1)S(1)}, u32[]{:S(2)}, u32[]{:S(2)}) collective-permute-start(bf16[64,1536]{1,0:T(8,128)(2,1)S(1)} %after.4.refs_2_), channel_id=1, source_target_pairs={{0,4},{4,0},{8,12},{12,8},{1,5},{5,1},{9,13},{13,9},{2,6},{6,2},{1... | collective-permute-start | bytes 589832 | tf_op jit(solution)/shard_map/ppermute | solution.py:562
  110.8 8.7 %collective-permute-start.23 = (bf16[64,1536]{1,0:T(8,128)(2,1)S(1)}, bf16[64,1536]{1,0:T(8,128)(2,1)S(1)}, u32[]{:S(2)}, u32[]{:S(2)}) collective-permute-start(bf16[64,1536]{1,0:T(8,128)(2,1)S(1)} %project.11.refs_1_.refs_8_), channel_id=1, source_target_pairs={{0,8},{4,12},{8,0},{12,4},{1,9},{5,13},{9,1},{13,5},{2,10},{6,14},... | collective-permute-start | bytes 589832 | tf_op jit(solution)/shard_map/ppermute | solution.py:558
  112.2 8.5 %collective-permute-start.22 = (bf16[64,1536]{1,0:T(8,128)(2,1)S(1)}, bf16[64,1536]{1,0:T(8,128)(2,1)S(1)}, u32[]{:S(2)}, u32[]{:S(2)}) collective-permute-start(bf16[64,1536]{1,0:T(8,128)(2,1)S(1)} %project.11.refs_1_.refs_8_), channel_id=1, source_target_pairs={{0,4},{4,0},{8,12},{12,8},{1,5},{5,1},{9,13},{13,9},{2,6},{6,2},{1... | collective-permute-start | bytes 589832 | tf_op jit(solution)/shard_map/ppermute | solution.py:562
  119.4 1.2 copy-start.2
  120.7 1.4 %collective-permute-start.24 = (bf16[64,1536]{1,0:T(8,128)(2,1)S(1)}, bf16[64,1536]{1,0:T(8,128)(2,1)S(1)}, u32[]{:S(2)}, u32[]{:S(2)}) collective-permute-start(bf16[64,1536]{1,0:T(8,128)(2,1)S(1)} %after.7.refs_10_), channel_id=1, source_target_pairs={{0,4},{4,0},{8,12},{12,8},{1,5},{5,1},{9,13},{13,9},{2,6},{6,2},{1... | collective-permute-start | bytes 589832 | tf_op jit(solution)/shard_map/ppermute | solution.py:562

commit v3 on v2

--- a/solution.py
+++ b/solution.py
@@ -205,12 +205,15 @@
 
 
 def project_kernel(
-    count, carries, final, shards, steps, sizes, anchored, place_ref, *refs
+    count, carries, final, shards, steps, sizes, anchored, streams, place_ref, *refs
 ):
     refs = refs[anchored:]
     pieces, refs = refs[: count * len(sizes)], refs[count * len(sizes) :]
-    gain_ref, query_ref, key_ref, value_ref = refs[:4]
-    refs = refs[4:]
+    gain_ref, refs = refs[0], refs[1:]
+    weights = []
+    for parts in streams:
+        weights.append(refs[:parts])
+        refs = refs[parts:]
     if carries:
         sums_in, squares_in = refs[:2]
         refs = refs[2:]
@@ -247,10 +250,15 @@
         squares[...] += part
         scaled = (wide * gain_ref[...]).astype(BF16)
         at = 0
-        for weight in (query_ref, key_ref, value_ref):
-            columns = slice(at, at + weight.shape[1])
-            sums[:, columns] += jnp.dot(scaled, weight[...], preferred_element_type=F32)
-            at += weight.shape[1]
+        for weight in weights:
+            columns = slice(at, at + weight[0].shape[1])
+            share = depth // len(weight)
+            total = sums[:, columns]
+            for part, ref in enumerate(weight):
+                deep = scaled[:, part * share : (part + 1) * share]
+                total += jnp.dot(deep, ref[...], preferred_element_type=F32)
+            sums[:, columns] = total
+            at += weight[0].shape[1]
 
     if final:
 
@@ -258,7 +266,7 @@
         def _():
             mean = jnp.sum(squares[...], axis=1, keepdims=True) / (shards * steps * depth)
             scale = lax.rsqrt(mean + 1e-05)
-            turned = query_ref.shape[1] + key_ref.shape[1]
+            turned = sums.shape[1] - weights[-1][0].shape[1]
             for at in range(0, sums.shape[1], HEAD_SIZE):
                 columns = slice(at, at + HEAD_SIZE)
                 head = sums[:, columns] * scale
@@ -285,19 +293,25 @@
     def whole(shape):
         return pl.BlockSpec(shape, lambda visit, step, place_ref: (0, 0))
 
-    def deep(block, dimension):
+    def deep(block, dimension, part=0, parts=1):
         def where(visit, step, place_ref):
-            at = block_of(visit, step, place_ref)
+            at = block_of(visit, step, place_ref) * parts + part
             return (at, 0) if dimension == 0 else (0, at)
 
         return pl.BlockSpec(block, where)
 
     extra = [*carried, *tables] if final else carried
-    operands = [*anchors, *pieces, gain, *weights, *extra]
+    streams = [weight.shape[1] // weights[-1].shape[1] for weight in weights]
+    cut = [weight for weight, parts in zip(weights, streams) for _ in range(parts)]
+    operands = [*anchors, *pieces, gain, *cut, *extra]
     in_specs = [pl.BlockSpec(memory_space=pl.ANY)] * len(anchors)
     in_specs += [whole(piece.shape) for piece in pieces]
     in_specs += [deep((1, depth), 1)]
-    in_specs += [deep((depth, weight.shape[1]), 0) for weight in weights]
+    in_specs += [
+        deep((depth // parts, weight.shape[1]), 0, part, parts)
+        for weight, parts in zip(weights, streams)
+        for part in range(parts)
+    ]
     in_specs += [whole(leaf.shape) for leaf in extra]
     scratch = [pltpu.VMEM((rows, depth), BF16)]
     if final:
@@ -318,6 +332,7 @@
             steps,
             sizes,
             len(anchors),
+            streams,
         ),
         grid_spec=pltpu.PrefetchScalarGridSpec(
             num_scalar_prefetch=1,
@@ -335,15 +350,20 @@
 def attend_kernel(
     chips, groups, known, prior, query_width, key_width, lengths_ref, plan_ref, *refs
 ):
-    blocks, refs = refs[: -12 if prior else -10], refs[-10:]
-    attended_out, cache_out, attended_ref, cache_ref, rows_ref, queries_ref = refs[:6]
-    scores_ref, top_ref, sems, out_sems = refs[6:]
+    blocks, refs = refs[: -13 if prior else -11], refs[-11:]
+    attended_out, cache_out, token_ref, attended_ref, cache_ref, rows_ref, queries_ref = refs[:7]
+    scores_ref, top_ref, sems, out_sems = refs[7:]
+    token_ref[...] = jnp.zeros_like(token_ref)
     workers = 2 * chips
     me = lax.axis_index("req")
     chip, core = lax.div(me, 2), lax.rem(me, 2)
     slots = cache_ref.shape[1]
     spans = slots // SPAN
     total = workers * sum(sum(sizes) for _, sizes in groups)
+    end = needed = jnp.int32(0)
+    for other in range(workers):
+        end = end + lengths_ref[other]
+        needed = jnp.where(end <= prior, end, needed)
     copies = []
     for group, (bases, sizes) in enumerate(groups):
         for hop in range(chips):
@@ -354,19 +374,25 @@
                 first = 0
                 for base, rows in zip(bases, sizes):
                     at = pl.multiple_of(base + owner * rows, ALIGN)
-                    copies.append(
-                        pltpu.make_async_copy(
-                            block.at[pl.ds(first, rows), :],
-                            rows_ref.at[pl.ds(at, rows), :],
-                            sems.at[len(copies)],
-                        )
+                    copy = pltpu.make_async_copy(
+                        block.at[pl.ds(first, rows), :],
+                        rows_ref.at[pl.ds(at, rows), :],
+                        sems.at[len(copies)],
                     )
+                    copies.append((at + rows > needed, copy))
                     first += rows
-    for copy in copies:
-        copy.start()
+    for wanted, copy in copies:
+
+        @pl.when(wanted)
+        def _():
+            copy.start()
+
     rows_ref[total:, :] = jnp.zeros((rows_ref.shape[0] - total, rows_ref.shape[1]), BF16)
-    for copy in copies:
-        copy.wait()
+    for wanted, copy in copies:
+
+        @pl.when(wanted)
+        def _():
+            copy.wait()
 
     def window(row, columns):
         first = pl.multiple_of(lax.div(row, ALIGN) * ALIGN, ALIGN)
@@ -532,10 +558,12 @@
         functools.partial(attend_kernel, chips, groups, known, prior, query_width, key_width),
         in_specs=[pl.BlockSpec(memory_space=pltpu.SMEM)] * 2
         + [pl.BlockSpec(memory_space=pl.ANY)] * (len(blocks) + len(outputs)),
-        out_specs=[pl.BlockSpec(memory_space=pl.ANY)] * 2,
+        out_specs=[pl.BlockSpec(memory_space=pl.ANY)] * 2
+        + [pl.BlockSpec(memory_space=pltpu.VMEM)],
         out_shape=[
             jax.ShapeDtypeStruct((slots, query_width), BF16),
             jax.ShapeDtypeStruct((2, slots, key_width), BF16),
+            jax.ShapeDtypeStruct((8, 128), F32),
         ],
         input_output_aliases={at + index: index for index in range(len(outputs))},
         scratch_shapes=[
@@ -628,14 +656,13 @@
         later = [lines[-1][piece] for piece in passed] + aways[chunk + 1 : chunk + 2]
         anchors = [lines[-1][piece] for piece in awaited if piece not in passed] if chunk else []
         if chunk > 1:
-            own.append(finished(chunk - 2, first_sums(chunk - 2), ()))
-            sent.append(from_chips(own[-1]))
-            anchors.append(own[-1])
+            sums = first_sums(chunk - 2)
+            anchors += [sums[1], *(lines[-2][piece] for piece in late)]
         if chunk <= last:
             arrived = [shift_chips(aways[chunk][hop - 1], hop, chips) for hop in range(1, chips)]
             block, later = merge(homes[chunk], arrived, later, anchors)
         else:
-            later = after(later, [*anchors, *sent[-2]])
+            later = after(later, [*anchors, *sent[-1]])
         aways[chunk + 1 : chunk + 2] = later[len(passed) :]
         if chunk:
             lines[-1].update(zip(passed, later))
@@ -648,18 +675,21 @@
                 if index + 1 in awaited:
                     line[index + 1] = lax.ppermute(block, "tp", pairs)
             lines.append(line)
+        if chunk > 1:
+            own.append(finished(chunk - 2, sums, ()))
+            sent.append(from_chips(own[-1]))
         if chunk == 1:
             turns = angles(groups, lengths, frequency, block)
-    own.append(finished(last, first_sums(last), sent[-1]))
+    own.append(finished(last, first_sums(last), ()))
     blocks = []
     for at in range(last):
         blocks += all_blocks(own[at], after(sent[at], own[at + 1 : at + 2]))
     sent.append(from_chips(own[last]))
     known = workers * sum(sizes[:-1])
     common = widths, slots, lengths, plan
-    outputs = attend(chips, groups[:-1], known, 0, *common, blocks, ())
-    blocks += all_blocks(own[last], after(sent[last], outputs[:1]))
-    return tuple(attend(chips, groups, workers * live, known, *common, blocks, outputs))
+    *outputs, token = attend(chips, groups[:-1], known, 0, *common, blocks, ())
+    blocks += all_blocks(own[last], after(sent[last], [token]))
+    return tuple(attend(chips, groups, workers * live, known, *common, blocks, outputs)[:2])
 
 
 def solution(mesh):

time: 131 us -> 125 us (0.954)
  the two profiles are of different devices: /device:TPU:15 before, /device:TPU:11 now
where the time goes in v3:
time: 125 us; the launch traced here: 123 us
  Pallas kernels  61.9 us (50%)
  starting transfers between devices  31.7 us (25%)
  waiting for transfers between devices  25.6 us (20%)
  local copies, waits for them, and re-layouts  3.04 us (2%)
    pallas_call x6, Pallas kernels, project(): pl.pallas_call(functools.partial(project_kernel, len(lines[0]), bool(carr...  42.1 us
    ppermute x6, starting transfers between devices, local(): lines[-1][index + 1] = lax.ppermute(lines[-1][source + 1], 'tp', pairs)  11.9 us
    pallas_call x2, Pallas kernels, attend(): pl.pallas_call(functools.partial(attend_kernel, chips, groups, known, pri...  11.7 us
    ppermute x6, waiting for transfers between devices, local(): line[index + 1] = lax.ppermute(block, 'tp', pairs)  10.5 us
    ppermute x6, waiting for transfers between devices, local(): lines[-1][index + 1] = lax.ppermute(lines[-1][source + 1], 'tp', pairs)  9.92 us
    ppermute x7, starting transfers between devices, swap_cores(): return lax.ppermute(value, 'req', [(d, d ^ 1) for d in range(2 * chips)])  8.51 us
    pallas_call x3, Pallas kernels, deal(): pl.pallas_call(functools.partial(deal_kernel, chips, bases, sizes, twins)...  6.93 us
    ppermute x6, starting transfers between devices, local(): line[index + 1] = lax.ppermute(block, 'tp', pairs)  6.81 us
  transfers between devices with their start and end apart: 25, of which 7 were waited for; matrix products, arithmetic and copies ran while one was open for 1% of the time, Pallas kernels for 43%

profile of v3, /device:TPU:11, one launch (start us, length us, event | category | flops | bytes accessed | tf_op | source)
XLA Modules:
  0.0 123.2 jit_solution(7262826299255191759)
XLA Ops:
  0.6 0.7 collective-permute-start
  1.4 1.6 %copy-done = bf16[512,2048]{1,0:T(8,128)(2,1)S(1)} copy-done((bf16[512,2048]{1,0:T(8,128)(2,1)S(1)}, bf16[512,2048]{1,0:T(8,128)(2,1)}, u32[]{:S(2)}) %copy-start) | copy-done | bytes 2097176
  3.0 0.7 copy-done.2
  3.6 1.6 %deal.4 = (bf16[64,2048]{1,0:T(8,128)(2,1)S(1)}, bf16[1,64,2048]{2,1,0:T(8,128)(2,1)S(1)}) custom-call(s32[4]{0:T(128)S(1)} %copy-done.2, bf16[512,2048]{1,0:T(8,128)(2,1)S(1)} %copy-done), custom_call_target="tpu_custom_call" | custom-call | tf_op jit(solution)/shard_map/deal/pallas_call | solution.py:78
  5.3 0.1 collective-permute-done.refs_1_.refs_0_
  5.4 1.7 %deal.5 = (bf16[64,2048]{1,0:T(8,128)(2,1)S(1)}, bf16[1,64,2048]{2,1,0:T(8,128)(2,1)S(1)}) custom-call(s32[4]{0:T(128)S(1)} %copy-done.2, bf16[512,2048]{1,0:T(8,128)(2,1)S(1)} %collective-permute-done.refs_1_.refs_0_, bf16[64,2048]{1,0:T(8,128)(2,1)S(1)} %get-tuple-element.39.refs_1_, bf16[1,64,2048]{2,1,0:T(8,128)(2,1)S(1)} %get-tuple-element.40.refs_2_), custom_call_target="tpu_custom_call" | custom-call | tf_op jit(solution)/shard_map/deal/pallas_call | solution.py:78
  7.0 0.0 copy-start.6
  7.1 0.0 copy-start.3
  7.1 0.0 copy-start.5
  7.1 0.3 collective-permute-start.1
  7.4 3.6 %deal.3 = (bf16[128,2048]{1,0:T(8,128)(2,1)S(1)}, bf16[1,128,2048]{2,1,0:T(8,128)(2,1)S(1)}, bf16[64,2048]{1,0:T(8,128)(2,1)S(1)}, bf16[1,64,2048]{2,1,0:T(8,128)(2,1)S(1)}) custom-call(s32[4]{0:T(128)S(1)} %copy-done.2, bf16[512,2048]{1,0:T(8,128)(2,1)S(1)} %copy-done.1, bf16[512,2048]{1,0:T(8,128)(2,1)S(1)} %collective-permute-done.refs_1_.refs_0_), custom_call_target="tpu_custom_call" | custom-call | tf_op jit(solution)/shard_map/deal/pallas_call | solution.py:78
  11.0 3.6 %collective-permute-done.1.refs_0_ = bf16[64,2048]{1,0:T(8,128)(2,1)S(1)} collective-permute-done((bf16[64,2048]{1,0:T(8,128)(2,1)S(1)}, bf16[64,2048]{1,0:T(8,128)(2,1)S(1)}, u32[]{:S(2)}, u32[]{:S(2)}) %collective-permute-start.1) | collective-permute-done | bytes 262176 | tf_op jit(solution)/shard_map/ppermute | solution.py:586
  14.7 0.3 collective-permute-start.2
  15.0 0.2 collective-permute-start.4
  15.3 2.2 %collective-permute-start.3 = (bf16[64,2048]{1,0:T(8,128)(2,1)S(1)}, bf16[64,2048]{1,0:T(8,128)(2,1)S(1)}, u32[]{:S(2)}, u32[]{:S(2)}) collective-permute-start(bf16[64,2048]{1,0:T(8,128)(2,1)S(1)} %get-tuple-element.45.refs_1_), channel_id=1, source_target_pairs={{0,2},{1,3},{2,0},{3,1},{4,6},{5,7},{6,4},{7,5},{8,10},{9,11},{10,... | collective-permute-start | bytes 786440 | tf_op jit(solution)/shard_map/ppermute | solution.py:676
  17.5 6.8 %collective-permute-done.4.refs_4_.refs_1_ = bf16[64,2048]{1,0:T(8,128)(2,1)S(1)} collective-permute-done((bf16[64,2048]{1,0:T(8,128)(2,1)S(1)}, bf16[64,2048]{1,0:T(8,128)(2,1)S(1)}, u32[]{:S(2)}, u32[]{:S(2)}) %collective-permute-start.4) | collective-permute-done | bytes 262176 | tf_op jit(solution)/shard_map/ppermute | solution.py:676
  24.3 3.7 %collective-permute-done.3.refs_2_ = bf16[64,2048]{1,0:T(8,128)(2,1)S(1)} collective-permute-done((bf16[64,2048]{1,0:T(8,128)(2,1)S(1)}, bf16[64,2048]{1,0:T(8,128)(2,1)S(1)}, u32[]{:S(2)}, u32[]{:S(2)}) %collective-permute-start.3) | collective-permute-done | bytes 262176 | tf_op jit(solution)/shard_map/ppermute | solution.py:676
  28.0 0.0 collective-permute-done.2.refs_0_
  28.0 0.1 merge.4
  28.1 0.1 collective-permute-start.11
  28.2 1.4 %collective-permute-start.10 = (bf16[128,2048]{1,0:T(8,128)(2,1)S(1)}, bf16[128,2048]{1,0:T(8,128)(2,1)S(1)}, u32[]{:S(2)}, u32[]{:S(2)}) collective-permute-start(bf16[128,2048]{1,0:T(8,128)(2,1)S(1)} %get-tuple-element.51.anchor_ref.refs_1_), channel_id=1, source_target_pairs={{0,2},{1,3},{2,0},{3,1},{4,6},{5,7},{6,4},{7,5},{8,10},{9,11},{10,... | collective-permute-start | bytes 1572872 | tf_op jit(solution)/shard_map/ppermute | solution.py:676
  29.6 1.1 collective-permute-start.9
  30.7 3.2 %collective-permute-start.5 = (bf16[64,2048]{1,0:T(8,128)(2,1)S(1)}, bf16[64,2048]{1,0:T(8,128)(2,1)S(1)}, u32[]{:S(2)}, u32[]{:S(2)}) collective-permute-start(bf16[64,2048]{1,0:T(8,128)(2,1)S(1)} %get-tuple-element.47.refs_0_), channel_id=1, source_target_pairs={{1,2},{2,1},{5,6},{6,5},{9,10},{10,9},{13,14},{14,13},{17,18},{18,... | collective-permute-start | bytes 786440 | tf_op jit(solution)/shard_map/ppermute | solution.py:671
  33.9 1.3 %collective-permute-start.6 = (bf16[64,2048]{1,0:T(8,128)(2,1)S(1)}, bf16[64,2048]{1,0:T(8,128)(2,1)S(1)}, u32[]{:S(2)}, u32[]{:S(2)}) collective-permute-start(bf16[64,2048]{1,0:T(8,128)(2,1)S(1)} %get-tuple-element.48.refs_2_), channel_id=1, source_target_pairs={{2,3},{1,0},{6,7},{5,4},{10,11},{9,8},{14,15},{13,12},{18,19},{17,... | collective-permute-start | bytes 786440 | tf_op jit(solution)/shard_map/ppermute | solution.py:671
  35.2 0.7 constant_dynamic-slice_fusion
  35.9 1.1 angles.1
  37.0 9.7 %project.6 = (f32[64,1536]{1,0:T(8,128)S(1)}, f32[64,128]{1,0:T(8,128)S(1)}) custom-call(s32[6]{0:T(128)S(1)} %slice_bitcast_fusion.place_ref, bf16[64,2048]{1,0:T(8,128)(2,1)S(1)} %get-tuple-element.47.refs_0_, bf16[64,2048]{1,0:T(8,128)(2,1)S(1)} %collective-permute-done.4.refs_4_.refs_1_, bf16[64,2048]{1,0:T(8,128)(2,1)S(1)} %get-tuple-element.48.refs_2_, ...), custom_call_target="tpu_custom_call" | custom-call | tf_op jit(solution)/shard_map/project/pallas_call | solution.py:325
  46.7 9.9 %collective-permute-done.5.refs_0_.refs_5_ = bf16[64,2048]{1,0:T(8,128)(2,1)S(1)} collective-permute-done((bf16[64,2048]{1,0:T(8,128)(2,1)S(1)}, bf16[64,2048]{1,0:T(8,128)(2,1)S(1)}, u32[]{:S(2)}, u32[]{:S(2)}) %collective-permute-start.5) | collective-permute-done | bytes 262176 | tf_op jit(solution)/shard_map/ppermute | solution.py:671
  56.7 0.0 collective-permute-done.6.refs_1_.refs_6_
  56.7 0.0 collective-permute-done.11.refs_3_.refs_1_
  56.7 0.0 collective-permute-done.10.refs_2_
  56.7 2.8 %collective-permute-start.12 = (bf16[128,2048]{1,0:T(8,128)(2,1)S(1)}, bf16[128,2048]{1,0:T(8,128)(2,1)S(1)}, u32[]{:S(2)}, u32[]{:S(2)}) collective-permute-start(bf16[128,2048]{1,0:T(8,128)(2,1)S(1)} %get-tuple-element.56.refs_0_), channel_id=1, source_target_pairs={{1,2},{2,1},{5,6},{6,5},{9,10},{10,9},{13,14},{14,13},{17,18},{18,... | collective-permute-start | bytes 1572872 | tf_op jit(solution)/shard_map/ppermute | solution.py:671
  59.6 1.3 %collective-permute-start.13 = (bf16[128,2048]{1,0:T(8,128)(2,1)S(1)}, bf16[128,2048]{1,0:T(8,128)(2,1)S(1)}, u32[]{:S(2)}, u32[]{:S(2)}) collective-permute-start(bf16[128,2048]{1,0:T(8,128)(2,1)S(1)} %get-tuple-element.57.refs_2_), channel_id=1, source_target_pairs={{2,3},{1,0},{6,7},{5,4},{10,11},{9,8},{14,15},{13,12},{18,19},{17,... | collective-permute-start | bytes 1572872 | tf_op jit(solution)/shard_map/ppermute | solution.py:671
  60.9 0.1 collective-permute-start.18
  61.0 2.8 %collective-permute-start.17 = (bf16[64,2048]{1,0:T(8,128)(2,1)S(1)}, bf16[64,2048]{1,0:T(8,128)(2,1)S(1)}, u32[]{:S(2)}, u32[]{:S(2)}) collective-permute-start(bf16[64,2048]{1,0:T(8,128)(2,1)S(1)} %get-tuple-element.62.refs_0_), channel_id=1, source_target_pairs={{0,2},{1,3},{2,0},{3,1},{4,6},{5,7},{6,4},{7,5},{8,10},{9,11},{10,... | collective-permute-start | bytes 786440 | tf_op jit(solution)/shard_map/ppermute | solution.py:676
  63.7 0.1 slice_bitcast_fusion.1.place_ref
  63.8 4.3 %project.7.refs_0_ = bf16[64,1536]{1,0:T(8,128)(2,1)S(1)} custom-call(s32[2]{0:T(128)S(1)} %slice_bitcast_fusion.1.place_ref, bf16[64,2048]{1,0:T(8,128)(2,1)S(1)} %collective-permute-done.5.refs_0_.refs_5_, bf16[64,2048]{1,0:T(8,128)(2,1)S(1)} %collective-permute-done.6.refs_1_.refs_6_, f32[1,8192]{1,0:T(1,128)S(1)} %bitcast.9, ...), custom_call_target="tpu_custom_call" | custom-call | tf_op jit(solution)/shard_map/project/pallas_call | solution.py:325
  68.2 1.4 %collective-permute-start.8 = (bf16[64,1536]{1,0:T(8,128)(2,1)S(1)}, bf16[64,1536]{1,0:T(8,128)(2,1)S(1)}, u32[]{:S(2)}, u32[]{:S(2)}) collective-permute-start(bf16[64,1536]{1,0:T(8,128)(2,1)S(1)} %project.7.refs_0_), channel_id=1, source_target_pairs={{0,8},{4,12},{8,0},{12,4},{1,9},{5,13},{9,1},{13,5},{2,10},{6,14},... | collective-permute-start | bytes 589832 | tf_op jit(solution)/shard_map/ppermute | solution.py:586
  69.5 9.6 %project.8 = (f32[128,1536]{1,0:T(8,128)S(1)}, f32[128,128]{1,0:T(8,128)S(1)}) custom-call(s32[6]{0:T(128)S(1)} %slice_bitcast_fusion.place_ref, bf16[128,2048]{1,0:T(8,128)(2,1)S(1)} %get-tuple-element.56.refs_0_, bf16[128,2048]{1,0:T(8,128)(2,1)S(1)} %collective-permute-done.11.refs_3_.refs_1_, bf16[128,2048]{1,0:T(8,128)(2,1)S(1)} %get-tuple-element.57.refs_2_, ...), custom_call_target="tpu_custom_call" | custom-call | tf_op jit(solution)/shard_map/project/pallas_call | solution.py:325
  79.1 0.0 collective-permute-done.12.refs_0_.refs_4_
  79.1 4.4 %project.9.refs_1_.refs_4_ = bf16[128,1536]{1,0:T(8,128)(2,1)S(1)} custom-call(s32[2]{0:T(128)S(1)} %slice_bitcast_fusion.1.place_ref, bf16[128,2048]{1,0:T(8,128)(2,1)S(1)} %collective-permute-done.12.refs_0_.refs_4_, bf16[128,2048]{1,0:T(8,128)(2,1)S(1)} %collective-permute-done.13.refs_1_.refs_5_, f32[1,8192]{1,0:T(1,128)S(1)} %bitcast.11, ...), custom_call_target="tpu_custom_call" | custom-call | tf_op jit(solution)/shard_map/project/pallas_call | solution.py:325
  83.5 0.3 collective-permute-start.16
  83.8 0.0 collective-permute-done.8.refs_0_.refs_6_
  83.8 0.0 collective-permute-done.18.refs_2_.refs_1_
  83.8 1.9 %collective-permute-start.19 = (bf16[64,2048]{1,0:T(8,128)(2,1)S(1)}, bf16[64,2048]{1,0:T(8,128)(2,1)S(1)}, u32[]{:S(2)}, u32[]{:S(2)}) collective-permute-start(bf16[64,2048]{1,0:T(8,128)(2,1)S(1)} %get-tuple-element.63.refs_0_), channel_id=1, source_target_pairs={{1,2},{2,1},{5,6},{6,5},{9,10},{10,9},{13,14},{14,13},{17,18},{18,... | collective-permute-start | bytes 786440 | tf_op jit(solution)/shard_map/ppermute | solution.py:671
  85.7 1.3 %collective-permute-start.20 = (bf16[64,2048]{1,0:T(8,128)(2,1)S(1)}, bf16[64,2048]{1,0:T(8,128)(2,1)S(1)}, u32[]{:S(2)}, u32[]{:S(2)}) collective-permute-start(bf16[64,2048]{1,0:T(8,128)(2,1)S(1)} %get-tuple-element.64.refs_2_), channel_id=1, source_target_pairs={{2,3},{1,0},{6,7},{5,4},{10,11},{9,8},{14,15},{13,12},{18,19},{17,... | collective-permute-start | bytes 786440 | tf_op jit(solution)/shard_map/ppermute | solution.py:671
  87.1 4.9 %collective-permute-start.15 = (bf16[128,1536]{1,0:T(8,128)(2,1)S(1)}, bf16[128,1536]{1,0:T(8,128)(2,1)S(1)}, u32[]{:S(2)}, u32[]{:S(2)}) collective-permute-start(bf16[128,1536]{1,0:T(8,128)(2,1)S(1)} %project.9.refs_1_.refs_4_), channel_id=1, source_target_pairs={{0,4},{4,0},{8,12},{12,8},{1,5},{5,1},{9,13},{13,9},{2,6},{6,2},{1... | collective-permute-start | bytes 1179656 | tf_op jit(solution)/shard_map/ppermute | solution.py:590
  91.9 9.7 %project.10 = (f32[64,1536]{1,0:T(8,128)S(1)}, f32[64,128]{1,0:T(8,128)S(1)}) custom-call(s32[6]{0:T(128)S(1)} %slice_bitcast_fusion.place_ref, bf16[64,2048]{1,0:T(8,128)(2,1)S(1)} %get-tuple-element.63.refs_0_, bf16[64,2048]{1,0:T(8,128)(2,1)S(1)} %collective-permute-done.18.refs_2_.refs_1_, bf16[64,2048]{1,0:T(8,128)(2,1)S(1)} %get-tuple-element.64.refs_2_, ...), custom_call_target="tpu_custom_call" | custom-call | tf_op jit(solution)/shard_map/project/pallas_call | solution.py:325
  101.6 0.0 collective-permute-done.20.refs_1_
  101.7 0.0 copy-start.4
  101.7 4.4 %project.11.refs_1_.refs_8_ = bf16[64,1536]{1,0:T(8,128)(2,1)S(1)} custom-call(s32[2]{0:T(128)S(1)} %slice_bitcast_fusion.1.place_ref, bf16[64,2048]{1,0:T(8,128)(2,1)S(1)} %collective-permute-done.19.refs_0_, bf16[64,2048]{1,0:T(8,128)(2,1)S(1)} %collective-permute-done.20.refs_1_, f32[1,8192]{1,0:T(1,128)S(1)} %bitcast.13, bf16[8192,1024]{1,0:T(8,128)(2,1)} %refs_6_.11, ...), custom_call_target="tpu_custom_call" | custom-call | tf_op jit(solution)/shard_map/project/pallas_call | solution.py:325
  106.0 0.0 collective-permute-done.16.refs_0_
  106.1 0.1 collective-permute-start.21
  106.1 0.5 collective-permute-start.7
  106.6 0.1 collective-permute-start.14
  106.7 1.1 collective-permute-start.23
  107.8 0.3 collective-permute-done.7.refs_1_
  108.1 0.4 collective-permute-start.22
  108.5 0.0 collective-permute-done.14.refs_3_
  108.5 0.0 collective-permute-done.15.refs_5_
  108.6 4.9 %attend.2 = (bf16[512,1024]{1,0:T(8,128)(2,1)}, bf16[2,512,256]{2,1,0:T(8,128)(2,1)}, f32[8,128]{1,0:T(8,128)S(1)}) custom-call(s32[4]{0:T(128)S(1)} %copy-done.3, s32[16]{0:T(128)S(1)} %copy-done.4, bf16[64,1536]{1,0:T(8,128)(2,1)S(1)} %project.7.refs_0_, bf16[64,1536]{1,0:T(8,128)(2,1)S(1)} %collective-permute-done.7.refs_1_, ...), custom_call_target="tpu_custom_call" | custom-call | tf_op jit(solution)/shard_map/attend/pallas_call | solution.py:557
  113.5 1.8 %collective-permute-start.24 = (bf16[64,1536]{1,0:T(8,128)(2,1)S(1)}, bf16[64,1536]{1,0:T(8,128)(2,1)S(1)}, u32[]{:S(2)}, u32[]{:S(2)}) collective-permute-start(bf16[64,1536]{1,0:T(8,128)(2,1)S(1)} %after.7.refs_10_), channel_id=1, source_target_pairs={{0,4},{4,0},{8,12},{12,8},{1,5},{5,1},{9,13},{13,9},{2,6},{6,2},{1... | collective-permute-start | bytes 589832 | tf_op jit(solution)/shard_map/ppermute | solution.py:590
  115.3 1.1 collective-permute-done.24.refs_11_
  116.4 6.8 %attend.3 = (bf16[512,1024]{1,0:T(8,128)(2,1)}, bf16[2,512,256]{2,1,0:T(8,128)(2,1)}, f32[8,128]{1,0:T(8,128)}) custom-call(s32[4]{0:T(128)S(1)} %copy-done.3, s32[16]{0:T(128)S(1)} %copy-done.4, bf16[64,1536]{1,0:T(8,128)(2,1)S(1)} %project.7.refs_0_, ...), custom_call_target="tpu_custom_call", output_to_operand_aliasing={{0}: (14, {}), {1}: (15, {})} | custom-call | tf_op jit(solution)/shard_map/attend/pallas_call | solution.py:557
  (23 shorter events, 0.1 us)
Async XLA Ops:
  0.6 4.7 %collective-permute-start = (bf16[512,2048]{1,0:T(8,128)(2,1)}, bf16[512,2048]{1,0:T(8,128)(2,1)S(1)}, u32[]{:S(2)}, u32[]{:S(2)}) collective-permute-start(bf16[512,2048]{1,0:T(8,128)(2,1)} %refs_0_.3), channel_id=1, source_target_pairs={{0,4},{4,0},{8,12},{12,8},{1,5},{5,1},{9,13},{13,9},{2,6},{6,2},{1... | collective-permute-start | bytes 6291464 | tf_op jit(solution)/shard_map/ppermute | solution.py:590
  1.4 1.6 %copy-start = (bf16[512,2048]{1,0:T(8,128)(2,1)S(1)}, bf16[512,2048]{1,0:T(8,128)(2,1)}, u32[]{:S(2)}) copy-start(bf16[512,2048]{1,0:T(8,128)(2,1)} %refs_0_.3) | copy-start | bytes 6291460
  3.0 0.7 copy-start.2
  3.6 3.8 %copy-start.1 = (bf16[512,2048]{1,0:T(8,128)(2,1)S(1)}, bf16[512,2048]{1,0:T(8,128)(2,1)}, u32[]{:S(2)}) copy-start(bf16[512,2048]{1,0:T(8,128)(2,1)} %refs_0_.3) | copy-start | bytes 6291460
  7.0 28.9 %copy-start.6 = (bf16[8192]{0:T(1024)(128)(2,1)S(1)}, bf16[8192]{0:T(1024)(128)(2,1)}, u32[]{:S(2)}) copy-start(bf16[8192]{0:T(1024)(128)(2,1)} %param.10) | copy-start | bytes 49156
  7.1 28.9 %copy-start.3 = (s32[4]{0:T(128)S(1)}, s32[4]{0:T(128)}, u32[]{:S(2)}) copy-start(s32[4]{0:T(128)} %lengths_ref.11) | copy-start | bytes 52
  7.1 28.9 %copy-start.5 = (f32[1,128]{1,0:T(1,128)S(1)}, f32[1,128]{1,0:T(1,128)}, u32[]{:S(2)}) copy-start(f32[1,128]{1,0:T(1,128)} %constant.14.clone.frequency_ref) | copy-start | bytes 1540
  7.1 7.6 %collective-permute-start.1 = (bf16[64,2048]{1,0:T(8,128)(2,1)S(1)}, bf16[64,2048]{1,0:T(8,128)(2,1)S(1)}, u32[]{:S(2)}, u32[]{:S(2)}) collective-permute-start(bf16[64,2048]{1,0:T(8,128)(2,1)S(1)} %bitcast.16), channel_id=1, source_target_pairs={{0,8},{4,12},{8,0},{12,4},{1,9},{5,13},{9,1},{13,5},{2,10},{6,14},... | collective-permute-start | bytes 786440 | tf_op jit(solution)/shard_map/ppermute | solution.py:586
  14.7 13.3 %collective-permute-start.2 = (bf16[128,2048]{1,0:T(8,128)(2,1)S(1)}, bf16[128,2048]{1,0:T(8,128)(2,1)S(1)}, u32[]{:S(2)}, u32[]{:S(2)}) collective-permute-start(bf16[128,2048]{1,0:T(8,128)(2,1)S(1)} %bitcast.14), channel_id=1, source_target_pairs={{0,8},{4,12},{8,0},{12,4},{1,9},{5,13},{9,1},{13,5},{2,10},{6,14},... | collective-permute-start | bytes 1572872 | tf_op jit(solution)/shard_map/ppermute | solution.py:586
  15.0 9.3 %collective-permute-start.4 = (bf16[64,2048]{1,0:T(8,128)(2,1)S(1)}, bf16[64,2048]{1,0:T(8,128)(2,1)S(1)}, u32[]{:S(2)}, u32[]{:S(2)}) collective-permute-start(bf16[64,2048]{1,0:T(8,128)(2,1)S(1)} %get-tuple-element.45.refs_1_), channel_id=1, source_target_pairs={{0,1},{1,0},{2,3},{3,2},{4,5},{5,4},{6,7},{7,6},{8,9},{9,8},{10,11... | collective-permute-start | bytes 786440 | tf_op jit(solution)/shard_map/ppermute | solution.py:676
  15.3 12.8 %collective-permute-start.3 = (bf16[64,2048]{1,0:T(8,128)(2,1)S(1)}, bf16[64,2048]{1,0:T(8,128)(2,1)S(1)}, u32[]{:S(2)}, u32[]{:S(2)}) collective-permute-start(bf16[64,2048]{1,0:T(8,128)(2,1)S(1)} %get-tuple-element.45.refs_1_), channel_id=1, source_target_pairs={{0,2},{1,3},{2,0},{3,1},{4,6},{5,7},{6,4},{7,5},{8,10},{9,11},{10,... | collective-permute-start | bytes 786440 | tf_op jit(solution)/shard_map/ppermute | solution.py:676
  28.1 28.6 %collective-permute-start.11 = (bf16[128,2048]{1,0:T(8,128)(2,1)S(1)}, bf16[128,2048]{1,0:T(8,128)(2,1)S(1)}, u32[]{:S(2)}, u32[]{:S(2)}) collective-permute-start(bf16[128,2048]{1,0:T(8,128)(2,1)S(1)} %get-tuple-element.51.anchor_ref.refs_1_), channel_id=1, source_target_pairs={{0,1},{1,0},{2,3},{3,2},{4,5},{5,4},{6,7},{7,6},{8,9},{9,8},{10,11... | collective-permute-start | bytes 1572872 | tf_op jit(solution)/shard_map/ppermute | solution.py:676
  28.2 28.5 %collective-permute-start.10 = (bf16[128,2048]{1,0:T(8,128)(2,1)S(1)}, bf16[128,2048]{1,0:T(8,128)(2,1)S(1)}, u32[]{:S(2)}, u32[]{:S(2)}) collective-permute-start(bf16[128,2048]{1,0:T(8,128)(2,1)S(1)} %get-tuple-element.51.anchor_ref.refs_1_), channel_id=1, source_target_pairs={{0,2},{1,3},{2,0},{3,1},{4,6},{5,7},{6,4},{7,5},{8,10},{9,11},{10,... | collective-permute-start | bytes 1572872 | tf_op jit(solution)/shard_map/ppermute | solution.py:676
  29.6 17.2 %collective-permute-start.9 = (bf16[64,2048]{1,0:T(8,128)(2,1)S(1)}, bf16[64,2048]{1,0:T(8,128)(2,1)S(1)}, u32[]{:S(2)}, u32[]{:S(2)}) collective-permute-start(bf16[64,2048]{1,0:T(8,128)(2,1)S(1)} %bitcast.15), channel_id=1, source_target_pairs={{0,8},{4,12},{8,0},{12,4},{1,9},{5,13},{9,1},{13,5},{2,10},{6,14},... | collective-permute-start | bytes 786440 | tf_op jit(solution)/shard_map/ppermute | solution.py:586
  30.7 26.0 %collective-permute-start.5 = (bf16[64,2048]{1,0:T(8,128)(2,1)S(1)}, bf16[64,2048]{1,0:T(8,128)(2,1)S(1)}, u32[]{:S(2)}, u32[]{:S(2)}) collective-permute-start(bf16[64,2048]{1,0:T(8,128)(2,1)S(1)} %get-tuple-element.47.refs_0_), channel_id=1, source_target_pairs={{1,2},{2,1},{5,6},{6,5},{9,10},{10,9},{13,14},{14,13},{17,18},{18,... | collective-permute-start | bytes 786440 | tf_op jit(solution)/shard_map/ppermute | solution.py:671
  33.9 22.8 %collective-permute-start.6 = (bf16[64,2048]{1,0:T(8,128)(2,1)S(1)}, bf16[64,2048]{1,0:T(8,128)(2,1)S(1)}, u32[]{:S(2)}, u32[]{:S(2)}) collective-permute-start(bf16[64,2048]{1,0:T(8,128)(2,1)S(1)} %get-tuple-element.48.refs_2_), channel_id=1, source_target_pairs={{2,3},{1,0},{6,7},{5,4},{10,11},{9,8},{14,15},{13,12},{18,19},{17,... | collective-permute-start | bytes 786440 | tf_op jit(solution)/shard_map/ppermute | solution.py:671
  56.7 22.4 %collective-permute-start.12 = (bf16[128,2048]{1,0:T(8,128)(2,1)S(1)}, bf16[128,2048]{1,0:T(8,128)(2,1)S(1)}, u32[]{:S(2)}, u32[]{:S(2)}) collective-permute-start(bf16[128,2048]{1,0:T(8,128)(2,1)S(1)} %get-tuple-element.56.refs_0_), channel_id=1, source_target_pairs={{1,2},{2,1},{5,6},{6,5},{9,10},{10,9},{13,14},{14,13},{17,18},{18,... | collective-permute-start | bytes 1572872 | tf_op jit(solution)/shard_map/ppermute | solution.py:671
  59.6 19.6 %collective-permute-start.13 = (bf16[128,2048]{1,0:T(8,128)(2,1)S(1)}, bf16[128,2048]{1,0:T(8,128)(2,1)S(1)}, u32[]{:S(2)}, u32[]{:S(2)}) collective-permute-start(bf16[128,2048]{1,0:T(8,128)(2,1)S(1)} %get-tuple-element.57.refs_2_), channel_id=1, source_target_pairs={{2,3},{1,0},{6,7},{5,4},{10,11},{9,8},{14,15},{13,12},{18,19},{17,... | collective-permute-start | bytes 1572872 | tf_op jit(solution)/shard_map/ppermute | solution.py:671
  60.9 22.9 %collective-permute-start.18 = (bf16[64,2048]{1,0:T(8,128)(2,1)S(1)}, bf16[64,2048]{1,0:T(8,128)(2,1)S(1)}, u32[]{:S(2)}, u32[]{:S(2)}) collective-permute-start(bf16[64,2048]{1,0:T(8,128)(2,1)S(1)} %get-tuple-element.62.refs_0_), channel_id=1, source_target_pairs={{0,1},{1,0},{2,3},{3,2},{4,5},{5,4},{6,7},{7,6},{8,9},{9,8},{10,11... | collective-permute-start | bytes 786440 | tf_op jit(solution)/shard_map/ppermute | solution.py:676
  61.0 22.8 %collective-permute-start.17 = (bf16[64,2048]{1,0:T(8,128)(2,1)S(1)}, bf16[64,2048]{1,0:T(8,128)(2,1)S(1)}, u32[]{:S(2)}, u32[]{:S(2)}) collective-permute-start(bf16[64,2048]{1,0:T(8,128)(2,1)S(1)} %get-tuple-element.62.refs_0_), channel_id=1, source_target_pairs={{0,2},{1,3},{2,0},{3,1},{4,6},{5,7},{6,4},{7,5},{8,10},{9,11},{10,... | collective-permute-start | bytes 786440 | tf_op jit(solution)/shard_map/ppermute | solution.py:676
  68.2 15.6 %collective-permute-start.8 = (bf16[64,1536]{1,0:T(8,128)(2,1)S(1)}, bf16[64,1536]{1,0:T(8,128)(2,1)S(1)}, u32[]{:S(2)}, u32[]{:S(2)}) collective-permute-start(bf16[64,1536]{1,0:T(8,128)(2,1)S(1)} %project.7.refs_0_), channel_id=1, source_target_pairs={{0,8},{4,12},{8,0},{12,4},{1,9},{5,13},{9,1},{13,5},{2,10},{6,14},... | collective-permute-start | bytes 589832 | tf_op jit(solution)/shard_map/ppermute | solution.py:586
  83.5 22.5 %collective-permute-start.16 = (bf16[128,1536]{1,0:T(8,128)(2,1)S(1)}, bf16[128,1536]{1,0:T(8,128)(2,1)S(1)}, u32[]{:S(2)}, u32[]{:S(2)}) collective-permute-start(bf16[128,1536]{1,0:T(8,128)(2,1)S(1)} %project.9.refs_1_.refs_4_), channel_id=1, source_target_pairs={{0,8},{4,12},{8,0},{12,4},{1,9},{5,13},{9,1},{13,5},{2,10},{6,14},... | collective-permute-start | bytes 1179656 | tf_op jit(solution)/shard_map/ppermute | solution.py:586
  83.8 17.8 %collective-permute-start.19 = (bf16[64,2048]{1,0:T(8,128)(2,1)S(1)}, bf16[64,2048]{1,0:T(8,128)(2,1)S(1)}, u32[]{:S(2)}, u32[]{:S(2)}) collective-permute-start(bf16[64,2048]{1,0:T(8,128)(2,1)S(1)} %get-tuple-element.63.refs_0_), channel_id=1, source_target_pairs={{1,2},{2,1},{5,6},{6,5},{9,10},{10,9},{13,14},{14,13},{17,18},{18,... | collective-permute-start | bytes 786440 | tf_op jit(solution)/shard_map/ppermute | solution.py:671
  85.7 15.9 %collective-permute-start.20 = (bf16[64,2048]{1,0:T(8,128)(2,1)S(1)}, bf16[64,2048]{1,0:T(8,128)(2,1)S(1)}, u32[]{:S(2)}, u32[]{:S(2)}) collective-permute-start(bf16[64,2048]{1,0:T(8,128)(2,1)S(1)} %get-tuple-element.64.refs_2_), channel_id=1, source_target_pairs={{2,3},{1,0},{6,7},{5,4},{10,11},{9,8},{14,15},{13,12},{18,19},{17,... | collective-permute-start | bytes 786440 | tf_op jit(solution)/shard_map/ppermute | solution.py:671
  87.1 21.5 %collective-permute-start.15 = (bf16[128,1536]{1,0:T(8,128)(2,1)S(1)}, bf16[128,1536]{1,0:T(8,128)(2,1)S(1)}, u32[]{:S(2)}, u32[]{:S(2)}) collective-permute-start(bf16[128,1536]{1,0:T(8,128)(2,1)S(1)} %project.9.refs_1_.refs_4_), channel_id=1, source_target_pairs={{0,4},{4,0},{8,12},{12,8},{1,5},{5,1},{9,13},{13,9},{2,6},{6,2},{1... | collective-permute-start | bytes 1179656 | tf_op jit(solution)/shard_map/ppermute | solution.py:590
  101.7 6.9 %copy-start.4 = (s32[16]{0:T(128)S(1)}, s32[16]{0:T(128)}, u32[]{:S(2)}) copy-start(s32[16]{0:T(128)} %plan_ref.3) | copy-start | bytes 196
  106.1 2.5 %collective-permute-start.21 = (bf16[128,1536]{1,0:T(8,128)(2,1)S(1)}, bf16[128,1536]{1,0:T(8,128)(2,1)S(1)}, u32[]{:S(2)}, u32[]{:S(2)}) collective-permute-start(bf16[128,1536]{1,0:T(8,128)(2,1)S(1)} %after.6.refs_6_), channel_id=1, source_target_pairs={{0,4},{4,0},{8,12},{12,8},{1,5},{5,1},{9,13},{13,9},{2,6},{6,2},{1... | collective-permute-start | bytes 1179656 | tf_op jit(solution)/shard_map/ppermute | solution.py:590
  106.1 2.0 %collective-permute-start.7 = (bf16[64,1536]{1,0:T(8,128)(2,1)S(1)}, bf16[64,1536]{1,0:T(8,128)(2,1)S(1)}, u32[]{:S(2)}, u32[]{:S(2)}) collective-permute-start(bf16[64,1536]{1,0:T(8,128)(2,1)S(1)} %project.7.refs_0_), channel_id=1, source_target_pairs={{0,4},{4,0},{8,12},{12,8},{1,5},{5,1},{9,13},{13,9},{2,6},{6,2},{1... | collective-permute-start | bytes 589832 | tf_op jit(solution)/shard_map/ppermute | solution.py:590
  106.6 1.9 %collective-permute-start.14 = (bf16[64,1536]{1,0:T(8,128)(2,1)S(1)}, bf16[64,1536]{1,0:T(8,128)(2,1)S(1)}, u32[]{:S(2)}, u32[]{:S(2)}) collective-permute-start(bf16[64,1536]{1,0:T(8,128)(2,1)S(1)} %after.4.refs_2_), channel_id=1, source_target_pairs={{0,4},{4,0},{8,12},{12,8},{1,5},{5,1},{9,13},{13,9},{2,6},{6,2},{1... | collective-permute-start | bytes 589832 | tf_op jit(solution)/shard_map/ppermute | solution.py:590
  106.7 6.8 %collective-permute-start.23 = (bf16[64,1536]{1,0:T(8,128)(2,1)S(1)}, bf16[64,1536]{1,0:T(8,128)(2,1)S(1)}, u32[]{:S(2)}, u32[]{:S(2)}) collective-permute-start(bf16[64,1536]{1,0:T(8,128)(2,1)S(1)} %project.11.refs_1_.refs_8_), channel_id=1, source_target_pairs={{0,8},{4,12},{8,0},{12,4},{1,9},{5,13},{9,1},{13,5},{2,10},{6,14},... | collective-permute-start | bytes 589832 | tf_op jit(solution)/shard_map/ppermute | solution.py:586
  108.1 7.2 %collective-permute-start.22 = (bf16[64,1536]{1,0:T(8,128)(2,1)S(1)}, bf16[64,1536]{1,0:T(8,128)(2,1)S(1)}, u32[]{:S(2)}, u32[]{:S(2)}) collective-permute-start(bf16[64,1536]{1,0:T(8,128)(2,1)S(1)} %project.11.refs_1_.refs_8_), channel_id=1, source_target_pairs={{0,4},{4,0},{8,12},{12,8},{1,5},{5,1},{9,13},{13,9},{2,6},{6,2},{1... | collective-permute-start | bytes 589832 | tf_op jit(solution)/shard_map/ppermute | solution.py:590
  113.5 2.9 %collective-permute-start.24 = (bf16[64,1536]{1,0:T(8,128)(2,1)S(1)}, bf16[64,1536]{1,0:T(8,128)(2,1)S(1)}, u32[]{:S(2)}, u32[]{:S(2)}) collective-permute-start(bf16[64,1536]{1,0:T(8,128)(2,1)S(1)} %after.7.refs_10_), channel_id=1, source_target_pairs={{0,4},{4,0},{8,12},{12,8},{1,5},{5,1},{9,13},{13,9},{2,6},{6,2},{1... | collective-permute-start | bytes 589832 | tf_op jit(solution)/shard_map/ppermute | solution.py:590

commit v4 on v3

--- a/solution.py
+++ b/solution.py
@@ -95,18 +95,18 @@
     refs[len(refs) - 1 - passed][...] = total
 
 
-def merge(home, arrived, later, anchors):
+def merge(home, arrived, later):
     count = len(arrived)
     vmem, anywhere = pl.BlockSpec(memory_space=pltpu.VMEM), pl.BlockSpec(memory_space=pl.ANY)
     block, *later = pl.pallas_call(
         functools.partial(merge_kernel, count, len(later)),
-        in_specs=[vmem] * (count + 1) + [anywhere] * (len(later) + len(anchors)),
+        in_specs=[vmem] * (count + 1) + [anywhere] * len(later),
         out_specs=[vmem] + [anywhere] * len(later),
         out_shape=[jax.ShapeDtypeStruct(leaf.shape, leaf.dtype) for leaf in (home, *later)],
         input_output_aliases={count + 1 + at: 1 + at for at in range(len(later))},
         compiler_params=pltpu.CompilerParams(vmem_limit_bytes=8 * MEBI),
         name="merge",
-    )(home, *arrived, *later, *anchors)
+    )(home, *arrived, *later)
     return block, later
 
 
@@ -204,41 +204,37 @@
     return [tables[at : at + 2] for at in range(0, len(tables), 2)]
 
 
-def project_kernel(
-    count, carries, final, shards, steps, sizes, anchored, streams, place_ref, *refs
-):
-    refs = refs[anchored:]
-    pieces, refs = refs[: count * len(sizes)], refs[count * len(sizes) :]
-    gain_ref, refs = refs[0], refs[1:]
-    weights = []
-    for parts in streams:
-        weights.append(refs[:parts])
-        refs = refs[parts:]
+def project_kernel(count, carries, final, shards, steps, sizes, place_ref, *refs):
+    chunks = len(sizes)
+    pieces, refs = refs[: count * chunks], refs[count * chunks :]
+    (gain_ref, *weights), refs = refs[:4], refs[4:]
     if carries:
-        sums_in, squares_in = refs[:2]
-        refs = refs[2:]
+        carried, refs = refs[: 2 * chunks], refs[2 * chunks :]
     if final:
         cosine_ref, sine_ref, out_ref, *refs = refs
-    sums, squares, chosen = refs
+    sums, squares, chosen = refs[: 2 * chunks : 2], refs[1 : 2 * chunks : 2], refs[-1]
     visit, step = pl.program_id(0), pl.program_id(1)
     visits = pl.num_programs(0)
-    rows, depth = chosen.shape
+    depth = chosen.shape[1]
     piece = place_ref[visit]
+    spans, first = [], 0
+    for size in sizes:
+        spans.append(slice(first, first + size))
+        first += size
 
     @pl.when((visit == 0) & (step == 0))
     def _():
-        sums[...] = sums_in[...] if carries else jnp.zeros_like(sums)
-        squares[...] = squares_in[...] if carries else jnp.zeros_like(squares)
+        for at in range(chunks):
+            sums[at][...] = carried[2 * at][...] if carries else jnp.zeros_like(sums[at])
+            squares[at][...] = carried[2 * at + 1][...] if carries else jnp.zeros_like(squares[at])
 
     for index in range(count):
 
         @pl.when(piece == index)
         def _():
             columns = pl.ds(pl.multiple_of(step * depth, depth), depth)
-            at = 0
-            for chunk, size in enumerate(sizes):
-                chosen[at : at + size, :] = pieces[chunk * count + index][:, columns]
-                at += size
+            for chunk, span in enumerate(spans):
+                chosen[span, :] = pieces[chunk * count + index][:, columns]
 
     @pl.when(piece >= 0)
     def _():
@@ -247,39 +243,36 @@
         part = square[:, :128]
         for at in range(128, depth, 128):
             part = part + square[:, at : at + 128]
-        squares[...] += part
+        for at, span in enumerate(spans):
+            squares[at][...] += part[span]
         scaled = (wide * gain_ref[...]).astype(BF16)
-        at = 0
+        left = 0
         for weight in weights:
-            columns = slice(at, at + weight[0].shape[1])
-            share = depth // len(weight)
-            total = sums[:, columns]
-            for part, ref in enumerate(weight):
-                deep = scaled[:, part * share : (part + 1) * share]
-                total += jnp.dot(deep, ref[...], preferred_element_type=F32)
-            sums[:, columns] = total
-            at += weight[0].shape[1]
+            columns = slice(left, left + weight.shape[1])
+            product = jnp.dot(scaled, weight[...], preferred_element_type=F32)
+            for at, span in enumerate(spans):
+                sums[at][:, columns] += product[span]
+            left += weight.shape[1]
 
     if final:
 
         @pl.when((visit == visits - 1) & (step == steps - 1))
         def _():
-            mean = jnp.sum(squares[...], axis=1, keepdims=True) / (shards * steps * depth)
+            mean = jnp.sum(squares[0][...], axis=1, keepdims=True) / (shards * steps * depth)
             scale = lax.rsqrt(mean + 1e-05)
-            turned = sums.shape[1] - weights[-1][0].shape[1]
-            for at in range(0, sums.shape[1], HEAD_SIZE):
-                columns = slice(at, at + HEAD_SIZE)
-                head = sums[:, columns] * scale
-                if at < turned:
+            turned = sums[0].shape[1] - weights[-1].shape[1]
+            for left in range(0, sums[0].shape[1], HEAD_SIZE):
+                columns = slice(left, left + HEAD_SIZE)
+                head = sums[0][:, columns] * scale
+                if left < turned:
                     head = head * cosine_ref[...] + pltpu.roll(
                         head, HEAD_SIZE // 2, 1
                     ) * sine_ref[...]
                 out_ref[:, columns] = head.astype(BF16)
 
 
-def project(
-    final, shards, sizes, place, visits, lines, gain, weights, carried, tables, anchors
-):
+def project(final, shards, sizes, place, lines, gain, weights, carried, tables):
+    place, visits = place
     pieces = [piece for line in lines for piece in line]
     rows, width = sum(sizes), pieces[0].shape[1]
     depth = min(DEPTH, width)
@@ -293,25 +286,18 @@
     def whole(shape):
         return pl.BlockSpec(shape, lambda visit, step, place_ref: (0, 0))
 
-    def deep(block, dimension, part=0, parts=1):
+    def deep(block, dimension):
         def where(visit, step, place_ref):
-            at = block_of(visit, step, place_ref) * parts + part
+            at = block_of(visit, step, place_ref)
             return (at, 0) if dimension == 0 else (0, at)
 
         return pl.BlockSpec(block, where)
 
-    extra = [*carried, *tables] if final else carried
-    streams = [weight.shape[1] // weights[-1].shape[1] for weight in weights]
-    cut = [weight for weight, parts in zip(weights, streams) for _ in range(parts)]
-    operands = [*anchors, *pieces, gain, *cut, *extra]
-    in_specs = [pl.BlockSpec(memory_space=pl.ANY)] * len(anchors)
-    in_specs += [whole(piece.shape) for piece in pieces]
+    extra = [*carried, *tables]
+    operands = [*pieces, gain, *weights, *extra]
+    in_specs = [whole(piece.shape) for piece in pieces]
     in_specs += [deep((1, depth), 1)]
-    in_specs += [
-        deep((depth // parts, weight.shape[1]), 0, part, parts)
-        for weight, parts in zip(weights, streams)
-        for part in range(parts)
-    ]
+    in_specs += [deep((depth, weight.shape[1]), 0) for weight in weights]
     in_specs += [whole(leaf.shape) for leaf in extra]
     scratch = [pltpu.VMEM((rows, depth), BF16)]
     if final:
@@ -319,20 +305,11 @@
         scratch = [pltpu.VMEM((rows, columns), F32), pltpu.VMEM((rows, 128), F32), *scratch]
     else:
         out_shape = [
-            jax.ShapeDtypeStruct((rows, columns), F32),
-            jax.ShapeDtypeStruct((rows, 128), F32),
+            jax.ShapeDtypeStruct((size, wide), F32) for size in sizes for wide in (columns, 128)
         ]
     return pl.pallas_call(
         functools.partial(
-            project_kernel,
-            len(lines[0]),
-            bool(carried),
-            final,
-            shards,
-            steps,
-            sizes,
-            len(anchors),
-            streams,
+            project_kernel, len(lines[0]), bool(carried), final, shards, steps, sizes
         ),
         grid_spec=pltpu.PrefetchScalarGridSpec(
             num_scalar_prefetch=1,
@@ -623,25 +600,28 @@
     early = [0, *awaited]
     late = [piece for piece in range(len(owned)) if piece not in early]
 
+    kinds = {"own": [0], "first": early, "direct": awaited, "late": late}
     tables, counts = zip(
-        *(visits_of([owned[piece] for piece in group], shards) for group in (early, late))
+        *(visits_of([owned[piece] for piece in kind], shards) for kind in kinds.values())
     )
     table = jnp.asarray(np.concatenate(tables, axis=1))
     table = lax.dynamic_index_in_dim(table, lax.axis_index("tp"), 0, keepdims=False)
-    places = table[: 2 * counts[0]], table[2 * counts[0] :]
+    ends = [2 * sum(counts[: at + 1]) for at in range(len(counts))]
+    places = {
+        kind: (table[end - 2 * count : end], count)
+        for kind, count, end in zip(kinds, counts, ends)
+    }
 
     groups = [([base], [rows]) for base, rows in zip(bases, sizes)]
     widths = w_query.shape[1], key_weight.shape[1]
 
-    def first_sums(at):
-        lists = [[lines[at][piece] for piece in early]]
-        shape = shards, sizes[at : at + 1], places[0], counts[0]
-        return project(False, *shape, lists, gain, weights, (), (), ())
-
-    def finished(at, sums, anchors):
-        lists = [[lines[at][piece] for piece in late]]
-        shape = shards, sizes[at : at + 1], places[1], counts[1]
-        return project(True, *shape, lists, gain, weights, sums, turns[at], anchors)[0]
+    def add(kind, chunks, carried=()):
+        held = [[lines[chunk][piece] for piece in kinds[kind]] for chunk in chunks]
+        rows = [sizes[chunk] for chunk in chunks]
+        turned = turns[chunks[0]] if kind == "late" else ()
+        return project(
+            kind == "late", shards, rows, places[kind], held, gain, weights, carried, turned
+        )
 
     def from_chips(block):
         return [shift_chips(block, hop, chips) for hop in range(1, chips)]
@@ -649,38 +629,53 @@
     def all_blocks(block, arrived):
         return [leaf for piece in (block, *arrived) for leaf in (piece, swap_cores(piece, chips))]
 
+    def start(line, group):
+        for index, (source, pairs) in enumerate(routes):
+            if index + 1 in group:
+                line[index + 1] = lax.ppermute(line[source + 1], "tp", pairs)
+
+    passed = [0, *(piece for piece in awaited if piece in sources)]
     lines, own, sent = [], [], []
     last = len(sizes) - 1
-    for chunk in range(len(sizes) + 1):
-        passed = [0, *(piece for piece in awaited if piece in sources)] if chunk else []
-        later = [lines[-1][piece] for piece in passed] + aways[chunk + 1 : chunk + 2]
-        anchors = [lines[-1][piece] for piece in awaited if piece not in passed] if chunk else []
-        if chunk > 1:
-            sums = first_sums(chunk - 2)
-            anchors += [sums[1], *(lines[-2][piece] for piece in late)]
+    sums, open_sums = {}, []
+    for chunk in range(last + 2):
+        fenced, anchors = [], []
+        if chunk:
+            fenced = [lines[-1][piece] for piece in passed]
+            anchors = [lines[-1][piece] for piece in awaited if piece not in passed]
         if chunk <= last:
             arrived = [shift_chips(aways[chunk][hop - 1], hop, chips) for hop in range(1, chips)]
-            block, later = merge(homes[chunk], arrived, later, anchors)
-        else:
-            later = after(later, [*anchors, *sent[-1]])
-        aways[chunk + 1 : chunk + 2] = later[len(passed) :]
+            later = aways[chunk + 1 : chunk + 2]
+            block, aways[chunk + 1 : chunk + 2] = merge(homes[chunk], arrived, later)
+            lines.append({0: block})
+            fenced.append(block)
+        if chunk == 2:
+            sums[0] = add("first", [0])
+            rest = list(range(1, last + 1))
+            shared = add("own", rest)
+            sums.update({at: shared[2 * index : 2 * index + 2] for index, at in enumerate(rest)})
+            anchors += [sums[0][1], shared[1], *(lines[0][piece] for piece in late)]
+        if chunk > 2:
+            sums[chunk - 2] = add("direct", [chunk - 2], sums[chunk - 2])
+            own.append(add("late", [chunk - 2], sums[chunk - 2])[0])
+            sent.append(from_chips(own[-1]))
+            anchors += [own[-1], *sent[-2]]
         if chunk:
-            lines[-1].update(zip(passed, later))
-            for index, (source, pairs) in enumerate(routes):
-                if index + 1 in late:
-                    lines[-1][index + 1] = lax.ppermute(lines[-1][source + 1], "tp", pairs)
+            fenced = after(fenced, anchors)
+            before = lines[chunk - 1]
+            before.update(zip(passed, fenced))
+            if chunk <= last:
+                lines[chunk][0] = fenced[-1]
+            start(before, late)
         if chunk <= last:
-            line = {0: block}
-            for index, (source, pairs) in enumerate(routes):
-                if index + 1 in awaited:
-                    line[index + 1] = lax.ppermute(block, "tp", pairs)
-            lines.append(line)
-        if chunk > 1:
-            own.append(finished(chunk - 2, sums, ()))
-            sent.append(from_chips(own[-1]))
+            start(lines[chunk], awaited)
         if chunk == 1:
-            turns = angles(groups, lengths, frequency, block)
-    own.append(finished(last, first_sums(last), ()))
+            turns = angles(groups, lengths, frequency, lines[1][0])
+        if chunk == 2:
+            own.append(add("late", [0], sums[0])[0])
+            sent.append(from_chips(own[0]))
+    sums[last] = add("direct", [last], sums[last])
+    own.append(add("late", [last], sums[last])[0])
     blocks = []
     for at in range(last):
         blocks += all_blocks(own[at], after(sent[at], own[at + 1 : at + 2]))

time: 125 us -> 121 us (0.968)
  the two profiles are of different devices: /device:TPU:11 before, /device:TPU:15 now
where the time goes in v4:
time: 121 us; the launch traced here: 120 us
  Pallas kernels  58.7 us (49%)
  starting transfers between devices  34.6 us (29%)
  waiting for transfers between devices  22.9 us (19%)
  local copies, waits for them, and re-layouts  3.18 us (3%)
    pallas_call x7, Pallas kernels, project(): pl.pallas_call(functools.partial(project_kernel, len(lines[0]), bool(carr...  40.3 us
    ppermute x12, starting transfers between devices, start(): line[index + 1] = lax.ppermute(line[source + 1], 'tp', pairs)  18.6 us
    ppermute x6, waiting for transfers between devices, shift_chips(): return lax.ppermute(value, 'req', pairs)  13.1 us
    ppermute x7, starting transfers between devices, swap_cores(): return lax.ppermute(value, 'req', [(d, d ^ 1) for d in range(2 * chips)])  12.4 us
    pallas_call x2, Pallas kernels, attend(): pl.pallas_call(functools.partial(attend_kernel, chips, groups, known, pri...  10.2 us
    ppermute x12, waiting for transfers between devices, start(): line[index + 1] = lax.ppermute(line[source + 1], 'tp', pairs)  7.07 us
    pallas_call x3, Pallas kernels, deal(): pl.pallas_call(functools.partial(deal_kernel, chips, bases, sizes, twins)...  6.94 us
    ppermute x6, starting transfers between devices, shift_chips(): return lax.ppermute(value, 'req', pairs)  3.56 us
  transfers between devices with their start and end apart: 25, of which 9 were waited for; matrix products, arithmetic and copies ran while one was open for 1% of the time, Pallas kernels for 44%

profile of v4, /device:TPU:15, one launch (start us, length us, event | category | flops | bytes accessed | tf_op | source)
XLA Modules:
  0.0 120.4 jit_solution(9507904277716575809)
XLA Ops:
  0.6 0.7 collective-permute-start
  1.4 1.6 %copy-done = bf16[512,2048]{1,0:T(8,128)(2,1)S(1)} copy-done((bf16[512,2048]{1,0:T(8,128)(2,1)S(1)}, bf16[512,2048]{1,0:T(8,128)(2,1)}, u32[]{:S(2)}) %copy-start) | copy-done | bytes 2097176
  3.0 0.7 copy-done.2
  3.6 1.6 %deal.3 = (bf16[64,2048]{1,0:T(8,128)(2,1)S(1)}, bf16[1,64,2048]{2,1,0:T(8,128)(2,1)S(1)}) custom-call(s32[4]{0:T(128)S(1)} %copy-done.2, bf16[512,2048]{1,0:T(8,128)(2,1)S(1)} %copy-done), custom_call_target="tpu_custom_call" | custom-call | tf_op jit(solution)/shard_map/deal/pallas_call | solution.py:78
  5.3 0.1 collective-permute-done.refs_0_.refs_1_
  5.4 1.7 %deal.4 = (bf16[64,2048]{1,0:T(8,128)(2,1)S(1)}, bf16[1,64,2048]{2,1,0:T(8,128)(2,1)S(1)}) custom-call(s32[4]{0:T(128)S(1)} %copy-done.2, bf16[512,2048]{1,0:T(8,128)(2,1)S(1)} %collective-permute-done.refs_0_.refs_1_, bf16[64,2048]{1,0:T(8,128)(2,1)S(1)} %get-tuple-element.43.refs_1_, bf16[1,64,2048]{2,1,0:T(8,128)(2,1)S(1)} %get-tuple-element.44.refs_2_), custom_call_target="tpu_custom_call" | custom-call | tf_op jit(solution)/shard_map/deal/pallas_call | solution.py:78
  7.0 0.0 copy-start.6
  7.1 0.0 copy-start.3
  7.1 0.0 copy-start.5
  7.1 0.3 collective-permute-start.1
  7.4 3.6 %deal.5 = (bf16[128,2048]{1,0:T(8,128)(2,1)S(1)}, bf16[1,128,2048]{2,1,0:T(8,128)(2,1)S(1)}, bf16[64,2048]{1,0:T(8,128)(2,1)S(1)}, bf16[1,64,2048]{2,1,0:T(8,128)(2,1)S(1)}) custom-call(s32[4]{0:T(128)S(1)} %copy-done.2, bf16[512,2048]{1,0:T(8,128)(2,1)S(1)} %copy-done.1, bf16[512,2048]{1,0:T(8,128)(2,1)S(1)} %collective-permute-done.refs_0_.refs_1_), custom_call_target="tpu_custom_call" | custom-call | tf_op jit(solution)/shard_map/deal/pallas_call | solution.py:78
  11.0 3.6 %collective-permute-done.1.refs_0_ = bf16[64,2048]{1,0:T(8,128)(2,1)S(1)} collective-permute-done((bf16[64,2048]{1,0:T(8,128)(2,1)S(1)}, bf16[64,2048]{1,0:T(8,128)(2,1)S(1)}, u32[]{:S(2)}, u32[]{:S(2)}) %collective-permute-start.1) | collective-permute-done | bytes 262176 | tf_op jit(solution)/shard_map/ppermute | solution.py:563
  14.7 0.3 collective-permute-start.3
  15.0 0.2 collective-permute-start.4
  15.2 2.3 %collective-permute-start.2 = (bf16[64,2048]{1,0:T(8,128)(2,1)S(1)}, bf16[64,2048]{1,0:T(8,128)(2,1)S(1)}, u32[]{:S(2)}, u32[]{:S(2)}) collective-permute-start(bf16[64,2048]{1,0:T(8,128)(2,1)S(1)} %get-tuple-element.48.refs_0_), channel_id=1, source_target_pairs={{0,2},{1,3},{2,0},{3,1},{4,6},{5,7},{6,4},{7,5},{8,10},{9,11},{10,... | collective-permute-start | bytes 786440 | tf_op jit(solution)/shard_map/ppermute | solution.py:635
  17.5 9.5 %collective-permute-done.3.refs_0_ = bf16[128,2048]{1,0:T(8,128)(2,1)S(1)} collective-permute-done((bf16[128,2048]{1,0:T(8,128)(2,1)S(1)}, bf16[128,2048]{1,0:T(8,128)(2,1)S(1)}, u32[]{:S(2)}, u32[]{:S(2)}) %collective-permute-start.3) | collective-permute-done | bytes 524320 | tf_op jit(solution)/shard_map/ppermute | solution.py:563
  27.0 0.1 merge.4
  27.0 1.0 collective-permute-done.2.refs_1_
  28.0 1.6 %collective-permute-start.9 = (bf16[128,2048]{1,0:T(8,128)(2,1)S(1)}, bf16[128,2048]{1,0:T(8,128)(2,1)S(1)}, u32[]{:S(2)}, u32[]{:S(2)}) collective-permute-start(bf16[128,2048]{1,0:T(8,128)(2,1)S(1)} %get-tuple-element.57.anchor_ref.refs_0_), channel_id=1, source_target_pairs={{0,2},{1,3},{2,0},{3,1},{4,6},{5,7},{6,4},{7,5},{8,10},{9,11},{10,... | collective-permute-start | bytes 1572872 | tf_op jit(solution)/shard_map/ppermute | solution.py:635
  29.6 0.7 constant_dynamic-slice_fusion
  30.3 2.9 %collective-permute-start.5 = (bf16[64,2048]{1,0:T(8,128)(2,1)S(1)}, bf16[64,2048]{1,0:T(8,128)(2,1)S(1)}, u32[]{:S(2)}, u32[]{:S(2)}) collective-permute-start(bf16[64,2048]{1,0:T(8,128)(2,1)S(1)} %get-tuple-element.53.refs_0_), channel_id=1, source_target_pairs={{1,2},{2,1},{5,6},{6,5},{9,10},{10,9},{13,14},{14,13},{17,18},{18,... | collective-permute-start | bytes 786440 | tf_op jit(solution)/shard_map/ppermute | solution.py:635
  33.2 1.3 %collective-permute-start.6 = (bf16[64,2048]{1,0:T(8,128)(2,1)S(1)}, bf16[64,2048]{1,0:T(8,128)(2,1)S(1)}, u32[]{:S(2)}, u32[]{:S(2)}) collective-permute-start(bf16[64,2048]{1,0:T(8,128)(2,1)S(1)} %get-tuple-element.54.refs_2_), channel_id=1, source_target_pairs={{2,3},{1,0},{6,7},{5,4},{10,11},{9,8},{14,15},{13,12},{18,19},{17,... | collective-permute-start | bytes 786440 | tf_op jit(solution)/shard_map/ppermute | solution.py:635
  34.6 1.3 %collective-permute-start.10 = (bf16[64,2048]{1,0:T(8,128)(2,1)S(1)}, bf16[64,2048]{1,0:T(8,128)(2,1)S(1)}, u32[]{:S(2)}, u32[]{:S(2)}) collective-permute-start(bf16[64,2048]{1,0:T(8,128)(2,1)S(1)} %bitcast.20), channel_id=1, source_target_pairs={{0,8},{4,12},{8,0},{12,4},{1,9},{5,13},{9,1},{13,5},{2,10},{6,14},... | collective-permute-start | bytes 786440 | tf_op jit(solution)/shard_map/ppermute | solution.py:563
  35.8 0.1 slice_bitcast_fusion.2.place_ref
  35.9 0.1 slice_bitcast_fusion.1
  36.0 1.1 angles.1
  37.1 9.6 %project.7 = (f32[64,1536]{1,0:T(8,128)S(1)}, f32[64,128]{1,0:T(8,128)S(1)}) custom-call(s32[6]{0:T(128)S(1)} %slice_bitcast_fusion.2.place_ref, bf16[64,2048]{1,0:T(8,128)(2,1)S(1)} %get-tuple-element.53.refs_0_, bf16[64,2048]{1,0:T(8,128)(2,1)S(1)} %collective-permute-done.4.refs_3_.refs_1_, bf16[64,2048]{1,0:T(8,128)(2,1)S(1)} %get-tuple-element.54.refs_2_, ...), custom_call_target="tpu_custom_call" | custom-call | tf_op jit(solution)/shard_map/project/pallas_call | solution.py:310
  46.7 0.0 collective-permute-done.10.refs_0_
  46.7 4.3 %project.9 = (f32[128,1536]{1,0:T(8,128)S(1)}, f32[128,128]{1,0:T(8,128)S(1)}, f32[64,1536]{1,0:T(8,128)S(1)}, f32[64,128]{1,0:T(8,128)S(1)}) custom-call(s32[2]{0:T(128)S(1)} %get-tuple-element.84.place_ref, bf16[128,2048]{1,0:T(8,128)(2,1)S(1)} %get-tuple-element.57.anchor_ref.refs_0_, bf16[64,2048]{1,0:T(8,128)(2,1)S(1)} %merge.5.refs_1_.refs_2_, ...), custom_call_target="tpu_custom_call" | custom-call | tf_op jit(solution)/shard_map/project/pallas_call | solution.py:310
  51.0 5.5 %collective-permute-done.5.refs_0_.refs_6_ = bf16[64,2048]{1,0:T(8,128)(2,1)S(1)} collective-permute-done((bf16[64,2048]{1,0:T(8,128)(2,1)S(1)}, bf16[64,2048]{1,0:T(8,128)(2,1)S(1)}, u32[]{:S(2)}, u32[]{:S(2)}) %collective-permute-start.5) | collective-permute-done | bytes 262176 | tf_op jit(solution)/shard_map/ppermute | solution.py:635
  56.5 0.0 collective-permute-done.6.refs_1_.refs_7_
  56.5 0.0 collective-permute-done.11.refs_3_.refs_0_
  56.5 0.0 collective-permute-done.9.refs_1_
  56.5 2.9 %collective-permute-start.12 = (bf16[128,2048]{1,0:T(8,128)(2,1)S(1)}, bf16[128,2048]{1,0:T(8,128)(2,1)S(1)}, u32[]{:S(2)}, u32[]{:S(2)}) collective-permute-start(bf16[128,2048]{1,0:T(8,128)(2,1)S(1)} %get-tuple-element.63), channel_id=1, source_target_pairs={{1,2},{2,1},{5,6},{6,5},{9,10},{10,9},{13,14},{14,13},{17,18},{18,... | collective-permute-start | bytes 1572872 | tf_op jit(solution)/shard_map/ppermute | solution.py:635
  59.5 1.3 %collective-permute-start.13 = (bf16[128,2048]{1,0:T(8,128)(2,1)S(1)}, bf16[128,2048]{1,0:T(8,128)(2,1)S(1)}, u32[]{:S(2)}, u32[]{:S(2)}) collective-permute-start(bf16[128,2048]{1,0:T(8,128)(2,1)S(1)} %get-tuple-element.64.refs_1_), channel_id=1, source_target_pairs={{2,3},{1,0},{6,7},{5,4},{10,11},{9,8},{14,15},{13,12},{18,19},{17,... | collective-permute-start | bytes 1572872 | tf_op jit(solution)/shard_map/ppermute | solution.py:635
  60.8 4.3 %project.8.refs_0_ = bf16[64,1536]{1,0:T(8,128)(2,1)S(1)} custom-call(s32[2]{0:T(128)S(1)} %get-tuple-element.85.place_ref, bf16[64,2048]{1,0:T(8,128)(2,1)S(1)} %collective-permute-done.5.refs_0_.refs_6_, bf16[64,2048]{1,0:T(8,128)(2,1)S(1)} %collective-permute-done.6.refs_1_.refs_7_, f32[1,8192]{1,0:T(1,128)S(1)} %bitcast.14, bf16[8192,1024]{1,0:T(8,128)(2,1)} %refs_3_.11, ...), custom_call_target="tpu_custom_call" | custom-call | tf_op jit(solution)/shard_map/project/pallas_call | solution.py:310
  65.1 1.5 %collective-permute-start.8 = (bf16[64,1536]{1,0:T(8,128)(2,1)S(1)}, bf16[64,1536]{1,0:T(8,128)(2,1)S(1)}, u32[]{:S(2)}, u32[]{:S(2)}) collective-permute-start(bf16[64,1536]{1,0:T(8,128)(2,1)S(1)} %project.8.refs_0_), channel_id=1, source_target_pairs={{0,8},{4,12},{8,0},{12,4},{1,9},{5,13},{9,1},{13,5},{2,10},{6,14},... | collective-permute-start | bytes 589832 | tf_op jit(solution)/shard_map/ppermute | solution.py:563
  66.6 2.8 %collective-permute-start.17 = (bf16[64,2048]{1,0:T(8,128)(2,1)S(1)}, bf16[64,2048]{1,0:T(8,128)(2,1)S(1)}, u32[]{:S(2)}, u32[]{:S(2)}) collective-permute-start(bf16[64,2048]{1,0:T(8,128)(2,1)S(1)} %get-tuple-element.70.refs_0_), channel_id=1, source_target_pairs={{0,2},{1,3},{2,0},{3,1},{4,6},{5,7},{6,4},{7,5},{8,10},{9,11},{10,... | collective-permute-start | bytes 786440 | tf_op jit(solution)/shard_map/ppermute | solution.py:635
  69.4 0.1 slice_bitcast_fusion.place_ref
  69.5 6.8 %project.10 = (f32[128,1536]{1,0:T(8,128)S(1)}, f32[128,128]{1,0:T(8,128)S(1)}) custom-call(s32[4]{0:T(128)S(1)} %slice_bitcast_fusion.place_ref, bf16[128,2048]{1,0:T(8,128)(2,1)S(1)} %collective-permute-done.11.refs_3_.refs_0_, bf16[128,2048]{1,0:T(8,128)(2,1)S(1)} %get-tuple-element.64.refs_1_, f32[1,8192]{1,0:T(1,128)S(1)} %bitcast.15, ...), custom_call_target="tpu_custom_call" | custom-call | tf_op jit(solution)/shard_map/project/pallas_call | solution.py:310
  76.2 0.0 collective-permute-done.12.refs_0_
  76.2 4.3 %project.11.refs_1_.refs_3_.refs_4_ = bf16[128,1536]{1,0:T(8,128)(2,1)S(1)} custom-call(s32[2]{0:T(128)S(1)} %get-tuple-element.85.place_ref, bf16[128,2048]{1,0:T(8,128)(2,1)S(1)} %collective-permute-done.12.refs_0_, bf16[128,2048]{1,0:T(8,128)(2,1)S(1)} %collective-permute-done.13.refs_1_, f32[1,8192]{1,0:T(1,128)S(1)} %bitcast.16, ...), custom_call_target="tpu_custom_call" | custom-call | tf_op jit(solution)/shard_map/project/pallas_call | solution.py:310
  80.6 0.1 collective-permute-start.16
  80.7 0.0 collective-permute-done.8.refs_0_.refs_4_
  80.7 0.0 collective-permute-done.18.refs_2_.refs_0_
  80.7 0.6 collective-permute-done.17.refs_1_
  81.3 1.9 %collective-permute-start.19 = (bf16[64,2048]{1,0:T(8,128)(2,1)S(1)}, bf16[64,2048]{1,0:T(8,128)(2,1)S(1)}, u32[]{:S(2)}, u32[]{:S(2)}) collective-permute-start(bf16[64,2048]{1,0:T(8,128)(2,1)S(1)} %get-tuple-element.71), channel_id=1, source_target_pairs={{1,2},{2,1},{5,6},{6,5},{9,10},{10,9},{13,14},{14,13},{17,18},{18,... | collective-permute-start | bytes 786440 | tf_op jit(solution)/shard_map/ppermute | solution.py:635
  83.2 1.3 %collective-permute-start.20 = (bf16[64,2048]{1,0:T(8,128)(2,1)S(1)}, bf16[64,2048]{1,0:T(8,128)(2,1)S(1)}, u32[]{:S(2)}, u32[]{:S(2)}) collective-permute-start(bf16[64,2048]{1,0:T(8,128)(2,1)S(1)} %get-tuple-element.72.refs_1_), channel_id=1, source_target_pairs={{2,3},{1,0},{6,7},{5,4},{10,11},{9,8},{14,15},{13,12},{18,19},{17,... | collective-permute-start | bytes 786440 | tf_op jit(solution)/shard_map/ppermute | solution.py:635
  84.5 7.2 %collective-permute-start.15 = (bf16[128,1536]{1,0:T(8,128)(2,1)S(1)}, bf16[128,1536]{1,0:T(8,128)(2,1)S(1)}, u32[]{:S(2)}, u32[]{:S(2)}) collective-permute-start(bf16[128,1536]{1,0:T(8,128)(2,1)S(1)} %project.11.refs_1_.refs_3_.refs_4_), channel_id=1, source_target_pairs={{0,4},{4,0},{8,12},{12,8},{1,5},{5,1},{9,13},{13,9},{2,6},{6,2},{1... | collective-permute-start | bytes 1179656 | tf_op jit(solution)/shard_map/ppermute | solution.py:567
  91.7 6.9 %project.12 = (f32[64,1536]{1,0:T(8,128)S(1)}, f32[64,128]{1,0:T(8,128)S(1)}) custom-call(s32[4]{0:T(128)S(1)} %slice_bitcast_fusion.place_ref, bf16[64,2048]{1,0:T(8,128)(2,1)S(1)} %collective-permute-done.18.refs_2_.refs_0_, bf16[64,2048]{1,0:T(8,128)(2,1)S(1)} %get-tuple-element.72.refs_1_, f32[1,8192]{1,0:T(1,128)S(1)} %bitcast.17, ...), custom_call_target="tpu_custom_call" | custom-call | tf_op jit(solution)/shard_map/project/pallas_call | solution.py:310
  98.6 0.0 collective-permute-done.20.refs_1_
  98.6 0.0 copy-start.4
  98.6 4.3 %project.13.refs_1_.refs_8_ = bf16[64,1536]{1,0:T(8,128)(2,1)S(1)} custom-call(s32[2]{0:T(128)S(1)} %get-tuple-element.85.place_ref, bf16[64,2048]{1,0:T(8,128)(2,1)S(1)} %collective-permute-done.19.refs_0_, bf16[64,2048]{1,0:T(8,128)(2,1)S(1)} %collective-permute-done.20.refs_1_, f32[1,8192]{1,0:T(1,128)S(1)} %bitcast.18, bf16[8192,1024]{1,0:T(8,128)(2,1)} %refs_3_.11, ...), custom_call_target="tpu_custom_call" | custom-call | tf_op jit(solution)/shard_map/project/pallas_call | solution.py:310
  102.9 0.0 collective-permute-done.16.refs_0_
  102.9 0.1 collective-permute-start.21
  103.0 0.5 collective-permute-start.7
  103.5 0.1 collective-permute-start.14
  103.6 1.4 %collective-permute-done.7.refs_1_ = bf16[64,1536]{1,0:T(8,128)(2,1)S(1)} collective-permute-done((bf16[64,1536]{1,0:T(8,128)(2,1)S(1)}, bf16[64,1536]{1,0:T(8,128)(2,1)S(1)}, u32[]{:S(2)}, u32[]{:S(2)}) %collective-permute-start.7) | collective-permute-done | bytes 196640 | tf_op jit(solution)/shard_map/ppermute | solution.py:567
  105.0 0.1 collective-permute-start.22
  105.1 0.1 collective-permute-done.14.refs_3_
  105.3 5.9 %attend.2 = (bf16[512,1024]{1,0:T(8,128)(2,1)}, bf16[2,512,256]{2,1,0:T(8,128)(2,1)}, f32[8,128]{1,0:T(8,128)S(1)}) custom-call(s32[4]{0:T(128)S(1)} %copy-done.3, s32[16]{0:T(128)S(1)} %copy-done.4, bf16[64,1536]{1,0:T(8,128)(2,1)S(1)} %project.8.refs_0_, bf16[64,1536]{1,0:T(8,128)(2,1)S(1)} %collective-permute-done.7.refs_1_, ...), custom_call_target="tpu_custom_call" | custom-call | tf_op jit(solution)/shard_map/attend/pallas_call | solution.py:534
  111.2 3.7 %collective-permute-start.24 = (bf16[64,1536]{1,0:T(8,128)(2,1)S(1)}, bf16[64,1536]{1,0:T(8,128)(2,1)S(1)}, u32[]{:S(2)}, u32[]{:S(2)}) collective-permute-start(bf16[64,1536]{1,0:T(8,128)(2,1)S(1)} %after.11.refs_10_), channel_id=1, source_target_pairs={{0,4},{4,0},{8,12},{12,8},{1,5},{5,1},{9,13},{13,9},{2,6},{6,2},{1... | collective-permute-start | bytes 589832 | tf_op jit(solution)/shard_map/ppermute | solution.py:567
  115.0 1.1 collective-permute-done.24.refs_11_
  116.0 4.2 %attend.3 = (bf16[512,1024]{1,0:T(8,128)(2,1)}, bf16[2,512,256]{2,1,0:T(8,128)(2,1)}, f32[8,128]{1,0:T(8,128)}) custom-call(s32[4]{0:T(128)S(1)} %copy-done.3, s32[16]{0:T(128)S(1)} %copy-done.4, bf16[64,1536]{1,0:T(8,128)(2,1)S(1)} %project.8.refs_0_, ...), custom_call_target="tpu_custom_call", output_to_operand_aliasing={{0}: (14, {}), {1}: (15, {})} | custom-call | tf_op jit(solution)/shard_map/attend/pallas_call | solution.py:534
  (27 shorter events, 0.1 us)
Async XLA Ops:
  0.6 4.7 %collective-permute-start = (bf16[512,2048]{1,0:T(8,128)(2,1)}, bf16[512,2048]{1,0:T(8,128)(2,1)S(1)}, u32[]{:S(2)}, u32[]{:S(2)}) collective-permute-start(bf16[512,2048]{1,0:T(8,128)(2,1)} %refs_0_.3), channel_id=1, source_target_pairs={{0,4},{4,0},{8,12},{12,8},{1,5},{5,1},{9,13},{13,9},{2,6},{6,2},{1... | collective-permute-start | bytes 6291464 | tf_op jit(solution)/shard_map/ppermute | solution.py:567
  1.4 1.6 %copy-start = (bf16[512,2048]{1,0:T(8,128)(2,1)S(1)}, bf16[512,2048]{1,0:T(8,128)(2,1)}, u32[]{:S(2)}) copy-start(bf16[512,2048]{1,0:T(8,128)(2,1)} %refs_0_.3) | copy-start | bytes 6291460
  3.0 0.7 copy-start.2
  3.6 3.8 %copy-start.1 = (bf16[512,2048]{1,0:T(8,128)(2,1)S(1)}, bf16[512,2048]{1,0:T(8,128)(2,1)}, u32[]{:S(2)}) copy-start(bf16[512,2048]{1,0:T(8,128)(2,1)} %refs_0_.3) | copy-start | bytes 6291460
  7.0 28.9 %copy-start.6 = (bf16[8192]{0:T(1024)(128)(2,1)S(1)}, bf16[8192]{0:T(1024)(128)(2,1)}, u32[]{:S(2)}) copy-start(bf16[8192]{0:T(1024)(128)(2,1)} %param.10) | copy-start | bytes 49156
  7.1 28.9 %copy-start.3 = (s32[4]{0:T(128)S(1)}, s32[4]{0:T(128)}, u32[]{:S(2)}) copy-start(s32[4]{0:T(128)} %lengths_ref.11) | copy-start | bytes 52
  7.1 28.9 %copy-start.5 = (f32[1,128]{1,0:T(1,128)S(1)}, f32[1,128]{1,0:T(1,128)}, u32[]{:S(2)}) copy-start(f32[1,128]{1,0:T(1,128)} %constant.14.clone.frequency_ref) | copy-start | bytes 1540
  7.1 7.6 %collective-permute-start.1 = (bf16[64,2048]{1,0:T(8,128)(2,1)S(1)}, bf16[64,2048]{1,0:T(8,128)(2,1)S(1)}, u32[]{:S(2)}, u32[]{:S(2)}) collective-permute-start(bf16[64,2048]{1,0:T(8,128)(2,1)S(1)} %bitcast.21), channel_id=1, source_target_pairs={{0,8},{4,12},{8,0},{12,4},{1,9},{5,13},{9,1},{13,5},{2,10},{6,14},... | collective-permute-start | bytes 786440 | tf_op jit(solution)/shard_map/ppermute | solution.py:563
  14.7 12.3 %collective-permute-start.3 = (bf16[128,2048]{1,0:T(8,128)(2,1)S(1)}, bf16[128,2048]{1,0:T(8,128)(2,1)S(1)}, u32[]{:S(2)}, u32[]{:S(2)}) collective-permute-start(bf16[128,2048]{1,0:T(8,128)(2,1)S(1)} %bitcast.19), channel_id=1, source_target_pairs={{0,8},{4,12},{8,0},{12,4},{1,9},{5,13},{9,1},{13,5},{2,10},{6,14},... | collective-permute-start | bytes 1572872 | tf_op jit(solution)/shard_map/ppermute | solution.py:563
  15.0 12.0 %collective-permute-start.4 = (bf16[64,2048]{1,0:T(8,128)(2,1)S(1)}, bf16[64,2048]{1,0:T(8,128)(2,1)S(1)}, u32[]{:S(2)}, u32[]{:S(2)}) collective-permute-start(bf16[64,2048]{1,0:T(8,128)(2,1)S(1)} %get-tuple-element.48.refs_0_), channel_id=1, source_target_pairs={{0,1},{1,0},{2,3},{3,2},{4,5},{5,4},{6,7},{7,6},{8,9},{9,8},{10,11... | collective-permute-start | bytes 786440 | tf_op jit(solution)/shard_map/ppermute | solution.py:635
  15.2 12.8 %collective-permute-start.2 = (bf16[64,2048]{1,0:T(8,128)(2,1)S(1)}, bf16[64,2048]{1,0:T(8,128)(2,1)S(1)}, u32[]{:S(2)}, u32[]{:S(2)}) collective-permute-start(bf16[64,2048]{1,0:T(8,128)(2,1)S(1)} %get-tuple-element.48.refs_0_), channel_id=1, source_target_pairs={{0,2},{1,3},{2,0},{3,1},{4,6},{5,7},{6,4},{7,5},{8,10},{9,11},{10,... | collective-permute-start | bytes 786440 | tf_op jit(solution)/shard_map/ppermute | solution.py:635
  28.0 28.5 %collective-permute-start.11 = (bf16[128,2048]{1,0:T(8,128)(2,1)S(1)}, bf16[128,2048]{1,0:T(8,128)(2,1)S(1)}, u32[]{:S(2)}, u32[]{:S(2)}) collective-permute-start(bf16[128,2048]{1,0:T(8,128)(2,1)S(1)} %get-tuple-element.57.anchor_ref.refs_0_), channel_id=1, source_target_pairs={{0,1},{1,0},{2,3},{3,2},{4,5},{5,4},{6,7},{7,6},{8,9},{9,8},{10,11... | collective-permute-start | bytes 1572872 | tf_op jit(solution)/shard_map/ppermute | solution.py:635
  28.0 28.5 %collective-permute-start.9 = (bf16[128,2048]{1,0:T(8,128)(2,1)S(1)}, bf16[128,2048]{1,0:T(8,128)(2,1)S(1)}, u32[]{:S(2)}, u32[]{:S(2)}) collective-permute-start(bf16[128,2048]{1,0:T(8,128)(2,1)S(1)} %get-tuple-element.57.anchor_ref.refs_0_), channel_id=1, source_target_pairs={{0,2},{1,3},{2,0},{3,1},{4,6},{5,7},{6,4},{7,5},{8,10},{9,11},{10,... | collective-permute-start | bytes 1572872 | tf_op jit(solution)/shard_map/ppermute | solution.py:635
  30.3 26.2 %collective-permute-start.5 = (bf16[64,2048]{1,0:T(8,128)(2,1)S(1)}, bf16[64,2048]{1,0:T(8,128)(2,1)S(1)}, u32[]{:S(2)}, u32[]{:S(2)}) collective-permute-start(bf16[64,2048]{1,0:T(8,128)(2,1)S(1)} %get-tuple-element.53.refs_0_), channel_id=1, source_target_pairs={{1,2},{2,1},{5,6},{6,5},{9,10},{10,9},{13,14},{14,13},{17,18},{18,... | collective-permute-start | bytes 786440 | tf_op jit(solution)/shard_map/ppermute | solution.py:635
  33.2 23.3 %collective-permute-start.6 = (bf16[64,2048]{1,0:T(8,128)(2,1)S(1)}, bf16[64,2048]{1,0:T(8,128)(2,1)S(1)}, u32[]{:S(2)}, u32[]{:S(2)}) collective-permute-start(bf16[64,2048]{1,0:T(8,128)(2,1)S(1)} %get-tuple-element.54.refs_2_), channel_id=1, source_target_pairs={{2,3},{1,0},{6,7},{5,4},{10,11},{9,8},{14,15},{13,12},{18,19},{17,... | collective-permute-start | bytes 786440 | tf_op jit(solution)/shard_map/ppermute | solution.py:635
  34.6 12.1 %collective-permute-start.10 = (bf16[64,2048]{1,0:T(8,128)(2,1)S(1)}, bf16[64,2048]{1,0:T(8,128)(2,1)S(1)}, u32[]{:S(2)}, u32[]{:S(2)}) collective-permute-start(bf16[64,2048]{1,0:T(8,128)(2,1)S(1)} %bitcast.20), channel_id=1, source_target_pairs={{0,8},{4,12},{8,0},{12,4},{1,9},{5,13},{9,1},{13,5},{2,10},{6,14},... | collective-permute-start | bytes 786440 | tf_op jit(solution)/shard_map/ppermute | solution.py:563
  56.5 19.7 %collective-permute-start.12 = (bf16[128,2048]{1,0:T(8,128)(2,1)S(1)}, bf16[128,2048]{1,0:T(8,128)(2,1)S(1)}, u32[]{:S(2)}, u32[]{:S(2)}) collective-permute-start(bf16[128,2048]{1,0:T(8,128)(2,1)S(1)} %get-tuple-element.63), channel_id=1, source_target_pairs={{1,2},{2,1},{5,6},{6,5},{9,10},{10,9},{13,14},{14,13},{17,18},{18,... | collective-permute-start | bytes 1572872 | tf_op jit(solution)/shard_map/ppermute | solution.py:635
  59.5 16.8 %collective-permute-start.13 = (bf16[128,2048]{1,0:T(8,128)(2,1)S(1)}, bf16[128,2048]{1,0:T(8,128)(2,1)S(1)}, u32[]{:S(2)}, u32[]{:S(2)}) collective-permute-start(bf16[128,2048]{1,0:T(8,128)(2,1)S(1)} %get-tuple-element.64.refs_1_), channel_id=1, source_target_pairs={{2,3},{1,0},{6,7},{5,4},{10,11},{9,8},{14,15},{13,12},{18,19},{17,... | collective-permute-start | bytes 1572872 | tf_op jit(solution)/shard_map/ppermute | solution.py:635
  65.1 15.6 %collective-permute-start.8 = (bf16[64,1536]{1,0:T(8,128)(2,1)S(1)}, bf16[64,1536]{1,0:T(8,128)(2,1)S(1)}, u32[]{:S(2)}, u32[]{:S(2)}) collective-permute-start(bf16[64,1536]{1,0:T(8,128)(2,1)S(1)} %project.8.refs_0_), channel_id=1, source_target_pairs={{0,8},{4,12},{8,0},{12,4},{1,9},{5,13},{9,1},{13,5},{2,10},{6,14},... | collective-permute-start | bytes 589832 | tf_op jit(solution)/shard_map/ppermute | solution.py:563
  66.6 14.1 %collective-permute-start.18 = (bf16[64,2048]{1,0:T(8,128)(2,1)S(1)}, bf16[64,2048]{1,0:T(8,128)(2,1)S(1)}, u32[]{:S(2)}, u32[]{:S(2)}) collective-permute-start(bf16[64,2048]{1,0:T(8,128)(2,1)S(1)} %get-tuple-element.70.refs_0_), channel_id=1, source_target_pairs={{0,1},{1,0},{2,3},{3,2},{4,5},{5,4},{6,7},{7,6},{8,9},{9,8},{10,11... | collective-permute-start | bytes 786440 | tf_op jit(solution)/shard_map/ppermute | solution.py:635
  66.6 14.7 %collective-permute-start.17 = (bf16[64,2048]{1,0:T(8,128)(2,1)S(1)}, bf16[64,2048]{1,0:T(8,128)(2,1)S(1)}, u32[]{:S(2)}, u32[]{:S(2)}) collective-permute-start(bf16[64,2048]{1,0:T(8,128)(2,1)S(1)} %get-tuple-element.70.refs_0_), channel_id=1, source_target_pairs={{0,2},{1,3},{2,0},{3,1},{4,6},{5,7},{6,4},{7,5},{8,10},{9,11},{10,... | collective-permute-start | bytes 786440 | tf_op jit(solution)/shard_map/ppermute | solution.py:635
  80.6 22.3 %collective-permute-start.16 = (bf16[128,1536]{1,0:T(8,128)(2,1)S(1)}, bf16[128,1536]{1,0:T(8,128)(2,1)S(1)}, u32[]{:S(2)}, u32[]{:S(2)}) collective-permute-start(bf16[128,1536]{1,0:T(8,128)(2,1)S(1)} %project.11.refs_1_.refs_3_.refs_4_), channel_id=1, source_target_pairs={{0,8},{4,12},{8,0},{12,4},{1,9},{5,13},{9,1},{13,5},{2,10},{6,14},... | collective-permute-start | bytes 1179656 | tf_op jit(solution)/shard_map/ppermute | solution.py:563
  81.3 17.3 %collective-permute-start.19 = (bf16[64,2048]{1,0:T(8,128)(2,1)S(1)}, bf16[64,2048]{1,0:T(8,128)(2,1)S(1)}, u32[]{:S(2)}, u32[]{:S(2)}) collective-permute-start(bf16[64,2048]{1,0:T(8,128)(2,1)S(1)} %get-tuple-element.71), channel_id=1, source_target_pairs={{1,2},{2,1},{5,6},{6,5},{9,10},{10,9},{13,14},{14,13},{17,18},{18,... | collective-permute-start | bytes 786440 | tf_op jit(solution)/shard_map/ppermute | solution.py:635
  83.2 15.4 %collective-permute-start.20 = (bf16[64,2048]{1,0:T(8,128)(2,1)S(1)}, bf16[64,2048]{1,0:T(8,128)(2,1)S(1)}, u32[]{:S(2)}, u32[]{:S(2)}) collective-permute-start(bf16[64,2048]{1,0:T(8,128)(2,1)S(1)} %get-tuple-element.72.refs_1_), channel_id=1, source_target_pairs={{2,3},{1,0},{6,7},{5,4},{10,11},{9,8},{14,15},{13,12},{18,19},{17,... | collective-permute-start | bytes 786440 | tf_op jit(solution)/shard_map/ppermute | solution.py:635
  84.5 20.7 %collective-permute-start.15 = (bf16[128,1536]{1,0:T(8,128)(2,1)S(1)}, bf16[128,1536]{1,0:T(8,128)(2,1)S(1)}, u32[]{:S(2)}, u32[]{:S(2)}) collective-permute-start(bf16[128,1536]{1,0:T(8,128)(2,1)S(1)} %project.11.refs_1_.refs_3_.refs_4_), channel_id=1, source_target_pairs={{0,4},{4,0},{8,12},{12,8},{1,5},{5,1},{9,13},{13,9},{2,6},{6,2},{1... | collective-permute-start | bytes 1179656 | tf_op jit(solution)/shard_map/ppermute | solution.py:567
  98.6 6.7 %copy-start.4 = (s32[16]{0:T(128)S(1)}, s32[16]{0:T(128)}, u32[]{:S(2)}) copy-start(s32[16]{0:T(128)} %plan_ref.3) | copy-start | bytes 196
  102.9 2.4 %collective-permute-start.21 = (bf16[128,1536]{1,0:T(8,128)(2,1)S(1)}, bf16[128,1536]{1,0:T(8,128)(2,1)S(1)}, u32[]{:S(2)}, u32[]{:S(2)}) collective-permute-start(bf16[128,1536]{1,0:T(8,128)(2,1)S(1)} %after.10.refs_6_), channel_id=1, source_target_pairs={{0,4},{4,0},{8,12},{12,8},{1,5},{5,1},{9,13},{13,9},{2,6},{6,2},{1... | collective-permute-start | bytes 1179656 | tf_op jit(solution)/shard_map/ppermute | solution.py:567
  103.0 2.0 %collective-permute-start.7 = (bf16[64,1536]{1,0:T(8,128)(2,1)S(1)}, bf16[64,1536]{1,0:T(8,128)(2,1)S(1)}, u32[]{:S(2)}, u32[]{:S(2)}) collective-permute-start(bf16[64,1536]{1,0:T(8,128)(2,1)S(1)} %project.8.refs_0_), channel_id=1, source_target_pairs={{0,4},{4,0},{8,12},{12,8},{1,5},{5,1},{9,13},{13,9},{2,6},{6,2},{1... | collective-permute-start | bytes 589832 | tf_op jit(solution)/shard_map/ppermute | solution.py:567
  103.5 1.8 %collective-permute-start.14 = (bf16[64,1536]{1,0:T(8,128)(2,1)S(1)}, bf16[64,1536]{1,0:T(8,128)(2,1)S(1)}, u32[]{:S(2)}, u32[]{:S(2)}) collective-permute-start(bf16[64,1536]{1,0:T(8,128)(2,1)S(1)} %after.8.refs_2_), channel_id=1, source_target_pairs={{0,4},{4,0},{8,12},{12,8},{1,5},{5,1},{9,13},{13,9},{2,6},{6,2},{1... | collective-permute-start | bytes 589832 | tf_op jit(solution)/shard_map/ppermute | solution.py:567
  103.6 7.7 %collective-permute-start.23 = (bf16[64,1536]{1,0:T(8,128)(2,1)S(1)}, bf16[64,1536]{1,0:T(8,128)(2,1)S(1)}, u32[]{:S(2)}, u32[]{:S(2)}) collective-permute-start(bf16[64,1536]{1,0:T(8,128)(2,1)S(1)} %project.13.refs_1_.refs_8_), channel_id=1, source_target_pairs={{0,8},{4,12},{8,0},{12,4},{1,9},{5,13},{9,1},{13,5},{2,10},{6,14},... | collective-permute-start | bytes 589832 | tf_op jit(solution)/shard_map/ppermute | solution.py:563
  105.0 10.0 %collective-permute-start.22 = (bf16[64,1536]{1,0:T(8,128)(2,1)S(1)}, bf16[64,1536]{1,0:T(8,128)(2,1)S(1)}, u32[]{:S(2)}, u32[]{:S(2)}) collective-permute-start(bf16[64,1536]{1,0:T(8,128)(2,1)S(1)} %project.13.refs_1_.refs_8_), channel_id=1, source_target_pairs={{0,4},{4,0},{8,12},{12,8},{1,5},{5,1},{9,13},{13,9},{2,6},{6,2},{1... | collective-permute-start | bytes 589832 | tf_op jit(solution)/shard_map/ppermute | solution.py:567
  111.2 4.8 %collective-permute-start.24 = (bf16[64,1536]{1,0:T(8,128)(2,1)S(1)}, bf16[64,1536]{1,0:T(8,128)(2,1)S(1)}, u32[]{:S(2)}, u32[]{:S(2)}) collective-permute-start(bf16[64,1536]{1,0:T(8,128)(2,1)S(1)} %after.11.refs_10_), channel_id=1, source_target_pairs={{0,4},{4,0},{8,12},{12,8},{1,5},{5,1},{9,13},{13,9},{2,6},{6,2},{1... | collective-permute-start | bytes 589832 | tf_op jit(solution)/shard_map/ppermute | solution.py:567
